TPU v7x, 256 devices: a whole 4x4x8 slice. The times are simulated.
256 devices in a mesh: inter: 4 (over x), intra: 64 (over z, y, core).
Axes of the slice: x: 4, y: 4, z: 8, core: 2. Of those that a mesh axis runs over, the one named last changes fastest.
Arguments:
- features: bfloat16 [2048, 4096], P(('inter', 'intra')), may hold values from -6 to 6
- preact: bfloat16 [2048, 16384], P('inter', 'intra'), may hold values from -6 to 6
- upstream: bfloat16 [2048, 16384], P('inter', 'intra'), may hold values from -16 to 16
- weight: bfloat16 [4096, 16384], P(None, 'intra'), may hold values from -0.046875 to 0.046875
- pairs: int32 [2048, 2], P('inter'), may hold values from 0 to 511
- station_weight: float32 [512], replicated, may hold values from 0.3 to 3
- counts: int32 [4], P('inter'), may hold values from 1 to 512, as said below
- error: bfloat16 [16384, 16384], P('inter', 'intra'), may hold values from -0.29882812 to 0.29882812
- basis: float32 [16384, 128], P('intra'), may hold values from -6 to 6
Outputs:
- grad_input: bfloat16 [2048, 4096], P(('inter', 'intra'))
- new_error: bfloat16 [16384, 16384], P('inter', 'intra')
- new_basis: float32 [16384, 128], P('intra')
Inputs may be any that keep to these rules, and one draw needn't show every extreme that they name: `pairs`: station indices. `counts`: group g holds at most ((g + 1) * 512) // 4 valid tokens and at least half as many; the last group is full.
All inputs are finite; a program needn't handle non-finite values.
Results may differ from a plain program's by a relative error of at most 0.0052.
Values may be sent and summed in bfloat16 or wider, within the bound.
No kernel may reach another device: no remote copies, remote signals or barrier semaphores. Data moves between devices by JAX's collectives and lax.ppermute only.
A program may use at most 128 MiB of HBM per device.

v0:
```python
import math

import jax
import jax.numpy as jnp
from jax import lax
from jax.sharding import PartitionSpec as P

HIGH = lax.Precision.HIGHEST


def gelu_slope(value):
    cdf = 0.5 * (1.0 + lax.erf(value / math.sqrt(2.0)))
    return cdf + value * jnp.exp(-0.5 * value * value) / math.sqrt(2.0 * math.pi)


def lookup(station_weight, column):
    table_size = station_weight.shape[0]
    onehot = (column[:, None] == jnp.arange(table_size, dtype=jnp.int32)[None, :]).astype(
        jnp.float32
    )
    return jnp.dot(onehot, station_weight, precision=HIGH)


def orthonormal(left):
    gram = jnp.dot(left.T, left, precision=HIGH)
    chol = jnp.linalg.cholesky(gram)
    return lax.linalg.triangular_solve(chol, left, left_side=False, lower=True, transpose_a=True)


def per_device(features, preact, upstream, weight, pairs, station_weight, counts, error, basis):
    n_inter = lax.axis_size("inter")
    group_rows = preact.shape[0]
    scale = lookup(station_weight, pairs[:, 0]) * lookup(station_weight, pairs[:, 1])
    live = (jnp.arange(group_rows, dtype=jnp.int32) < counts[0]).astype(jnp.float32)
    dpre = (
        upstream.astype(jnp.float32)
        * gelu_slope(preact.astype(jnp.float32))
        * (scale * live)[:, None]
    ).astype(jnp.bfloat16)
    rows = dpre
    grad_input = lax.psum_scatter(
        lax.dot_general(rows, weight, (((1,), (1,)), ((), ())), preferred_element_type=jnp.float32),
        "intra",
        scatter_dimension=0,
        tiled=True,
    ).astype(jnp.bfloat16)
    rows = dpre
    grad_raw = lax.dot_general(
        lax.all_gather(features, "intra", axis=0, tiled=True),
        rows,
        (((0,), (0,)), ((), ())),
        preferred_element_type=jnp.float32,
    )
    own_count = counts.astype(jnp.float32)[0]
    error_f = error.astype(jnp.float32)
    total = lax.psum(own_count, "inter")
    mean_count = total / n_inter
    merged = grad_raw / mean_count + error_f
    term = jnp.dot(merged, basis, precision=HIGH)
    left = lax.psum(term, ("inter", "intra"))
    ortho = orthonormal(left)
    right_term = lax.dot_general(merged, ortho, (((0,), (0,)), ((), ())), precision=HIGH)
    new_basis = lax.psum(right_term, "inter")
    decompressed = jnp.dot(ortho, new_basis.T, precision=HIGH) / n_inter
    new_error = (merged - decompressed).astype(jnp.bfloat16)
    return (grad_input, new_error, new_basis)


def solution(mesh):
    in_specs = (
        P(("inter", "intra"), None),
        P("inter", "intra"),
        P("inter", "intra"),
        P(None, "intra"),
        P("inter", None),
        P(),
        P("inter"),
        P("inter", "intra"),
        P("intra", None),
    )
    out_specs = (P(("inter", "intra"), None), P("inter", "intra"), P("intra", None))
    return jax.shard_map(
        per_device, mesh=mesh, in_specs=in_specs, out_specs=out_specs, check_vma=False
    )
```

profile of v0, /device:TPU:8, one launch (start us, length us, event | category | flops | bytes accessed | tf_op | source)
XLA Modules:
  0.0 507.9 jit_solution(13942084512107196208)
XLA Ops:
  7.2 0.0 copy-start
  7.2 0.0 all-gather.2.cloned.1.call-start
  7.2 0.7 all-gather.2.cloned.1.call-update
  7.9 0.0 all-reduce.5.cloned.1.call-start
  8.6 11.6 %psum.21 = f32[]{:T(128)} all-reduce(f32[]{:T(128)} %bitcast.7), channel_id=1, replica_groups=mesh['inter'=4,'intra'=64] {'inter'}, use_global_device_ids=true, to_apply=%region_1.0 | all-reduce | flops 1 | bytes 8 | tf_op jit(solution)/shard_map/psum | solution.py:56
  20.2 0.8 fusion.20
  21.0 1.3 fusion.4
  22.3 1.3 fusion.5
  23.6 0.0 copy-done
  23.6 5.6 %fusion.19 = f32[512,4096]{1,0:T(8,128)} fusion(bf16[4096,256]{1,0:T(8,128)(2,1)S(1)} %copy-done, bf16[512,256]{1,0:T(8,128)(2,1)} %param.10, bf16[512,256]{1,0:T(8,128)(2,1)} %param.11, f32[512]{0:T(512)S(1)} %multiply_select_fusion), kind=kOutput, calls=%fused_computation.37 | convolution fusion | flops 1075445760 | bytes 11012096 | tf_op jit(solution)/shard_map/dot_general | solution.py:42
  29.3 0.0 copy-start.5
  29.3 0.0 copy-start.6
  29.3 4.1 copy.16
  34.1 0.0 copy-start.7
  34.1 57.5 %all-gather.2.cloned.1.call-done = bf16[512,4096]{1,0:T(8,128)(2,1)} async-done(((bf16[8,4096]{1,0:T(8,128)(2,1)}), bf16[512,4096]{1,0:T(8,128)(2,1)}) %all-gather.2.cloned.1.call-update) | async-done | bytes 4194320 | tf_op jit(solution)/shard_map/all_gather | solution.py:49
  91.6 0.0 copy-done.5
  91.6 0.0 copy-done.6
  91.6 4.5 fusion.3
  96.1 0.0 copy-start.1
  96.1 1.9 copy-done.1
  98.1 0.0 copy-done.7
  98.1 8.3 %fusion.21 = f32[4096,128]{1,0:T(8,128)} fusion(f32[4096,256]{0,1:T(8,128)S(1)} %fusion.3, f32[256,128]{1,0:T(8,128)S(1)} %copy-done.7), kind=kOutput, calls=%fused_computation.39 | convolution fusion | flops 1610612736 | bytes 6422528 | tf_op jit(solution)/shard_map/dot_general | solution.py:59
  106.3 0.0 all-reduce.5.cloned.1.call-update
  106.3 0.0 copy-start.8
  106.4 0.0 all-reduce.7.cloned.1.call-start
  106.4 294.0 %all-reduce.8 = bf16[512,4096]{1,0:T(8,128)(2,1)} all-reduce(f32[512,4096]{1,0:T(8,128)} %fusion.19), channel_id=2, replica_groups=mesh['inter'=4,'intra'=64] {'intra'}, use_global_device_ids=true, to_apply=%region_0.0.clone | all-reduce | flops 2097152 | bytes 12582912
  400.4 0.0 copy-done.8
  400.4 0.6 dynamic-slice
  401.7 0.0 all-reduce.5.cloned.1.call-done
  401.7 5.7 %fusion.22 = f32[128,128]{1,0:T(8,128)S(1)} fusion(f32[4096,128]{1,0:T(8,128)} %all-reduce.5.cloned.1.call-done), kind=kOutput, calls=%fused_computation.40 | convolution fusion | flops 805306368 | bytes 2162688 | tf_op jit(solution)/shard_map/dot_general | solution.py:25
  407.4 0.1 copy.17
  407.5 11.7 %cholesky.16 = f32[128,128]{1,0:T(8,128)S(1)} custom-call(f32[128,128]{1,0:T(8,128)S(1)} %fusion.18), custom_call_target="Cholesky" | custom-call | tf_op jit(solution)/shard_map/jit(cholesky)/cholesky | solution.py:26
  419.3 0.6 compare_reduce_fusion
  419.9 0.7 fusion.15
  420.6 9.8 %custom-call.6 = f32[1,128,128]{1,2,0:T(8,128)S(1)} custom-call(f32[1,128,128]{2,1,0:T(8,128)S(1)} %fusion.15), custom_call_target="InvertDiagBlocksLowerTriangular" | custom-call | tf_op jit(solution)/shard_map/triangular_solve | solution.py:27
  430.4 0.0 copy-start.2
  430.4 3.6 fusion.16
  434.0 0.0 copy-start.3
  434.1 1.3 copy-done.3
  435.4 0.0 copy-done.2
  435.4 4.4 fusion.23
  439.7 0.0 all-reduce.7.cloned.1.call-update
  439.8 1.5 dynamic-slice_convert_fusion
  441.2 47.5 %all-reduce.7.cloned.1.call-done = f32[256,128]{1,0:T(8,128)} async-done(((f32[256,128]{1,0:T(8,128)}), f32[256,128]{1,0:T(8,128)}) %all-reduce.7.cloned.1.call-update) | async-done | bytes 131088 | tf_op jit(solution)/shard_map/psum | solution.py:63
  488.8 7.8 %fusion.1 = bf16[4096,256]{0,1:T(8,128)(2,1)} fusion(f32[4096,256]{0,1:T(8,128)} %copy-done.1, f32[4096,128]{1,0:T(8,128)} %copy-done.3, f32[256,128]{1,0:T(8,128)} %all-reduce.7.cloned.1.call-done), kind=kOutput, calls=%fused_computation.2 | convolution fusion | flops 1613758464 | bytes 8519680 | tf_op jit(solution)/shard_map/dot_general | solution.py:64
  496.6 0.0 copy-start.4
  496.6 4.1 copy.19
  500.7 0.0 copy-done.4
  500.7 0.7 copy.26
  (3 shorter events, 0.1 us)
Async XLA Ops:
  7.2 16.5 %copy-start = (bf16[4096,256]{1,0:T(8,128)(2,1)S(1)}, bf16[4096,256]{1,0:T(8,128)(2,1)}, u32[]{:S(2)}) copy-start(bf16[4096,256]{1,0:T(8,128)(2,1)} %param.12) | copy-start | bytes 6291460
  7.2 84.4 %all-gather.2.cloned.1.call-start = ((), (), s32[]{:S(2)}) async-start(), calls=%async_computation | async-start | bytes 4259840 | tf_op jit(solution)/shard_map/all_gather | solution.py:49
  7.9 393.8 %all-reduce.5.cloned.1.call-start = ((), (), s32[]{:S(2)}) async-start(), calls=%async_computation.1 | async-start | bytes 4194304 | tf_op jit(solution)/shard_map/psum | solution.py:60
  29.3 62.3 %copy-start.5 = (bf16[512,256]{1,0:T(8,128)(2,1)S(1)}, bf16[512,256]{1,0:T(8,128)(2,1)}, u32[]{:S(2)}) copy-start(bf16[512,256]{1,0:T(8,128)(2,1)} %param.10) | copy-start | bytes 786436
  29.3 62.3 %copy-start.6 = (bf16[512,256]{1,0:T(8,128)(2,1)S(1)}, bf16[512,256]{1,0:T(8,128)(2,1)}, u32[]{:S(2)}) copy-start(bf16[512,256]{1,0:T(8,128)(2,1)} %param.11) | copy-start | bytes 786436
  34.1 64.0 %copy-start.7 = (f32[256,128]{1,0:T(8,128)S(1)}, f32[256,128]{1,0:T(8,128)}, u32[]{:S(2)}) copy-start(f32[256,128]{1,0:T(8,128)} %param.17) | copy-start | bytes 393220
  96.1 2.0 copy-start.1
  106.3 294.1 %copy-start.8 = (u32[256]{0:T(256)S(1)}, u32[256]{0:T(256)}, u32[]{:S(2)}) copy-start(u32[256]{0:T(256)} %constant.62) | copy-start | bytes 3076
  106.4 382.4 %all-reduce.7.cloned.1.call-start = ((), (), s32[]{:S(2)}) async-start(), calls=%async_computation.2 | async-start | bytes 262144 | tf_op jit(solution)/shard_map/psum | solution.py:63
  430.4 5.0 copy-start.2
  434.0 1.3 copy-start.3
  496.6 4.1 copy-start.4
Sparse Core Ops, SparseCore 0:
  10.8 80.7 all-gather.1
  106.5 260.9 all-reduce.4
  439.9 48.8 all-reduce.6
where the time goes:
time: 508 us
  blocking collectives  306 us (60%)
  waiting for transfers between devices  106 us (21%)
  matrix products  42.6 us (8%)
  other arithmetic  22.9 us (5%)
  between operations  15.8 us (3%)
  local copies, waits for them, and re-layouts  15.1 us (3%)
    unnamed x1, blocking collectives  294 us
    all_gather x1, waiting for transfers between devices, per_device(): lax.all_gather(features, 'intra', axis=0, tiled=True)  57.5 us
    psum x1, waiting for transfers between devices, per_device(): new_basis = lax.psum(right_term, 'inter')  47.5 us
    unnamed x22, local copies, waits for them, and re-layouts  12.8 us
    another operation x3, other arithmetic, orthonormal(): chol = jnp.linalg.cholesky(gram)  12.4 us
    psum x1, blocking collectives, per_device(): total = lax.psum(own_count, 'inter')  11.6 us
    another operation x2, other arithmetic, orthonormal(): lax.linalg.triangular_solve(chol, left, left_side=False, lower=True, tran...  10.5 us
  transfers between devices with their start and end apart: 3, of which 2 were waited for; matrix products, arithmetic and copies ran while one was open for 3% of the time, Pallas kernels for 0%

commit v1 on v0

v1 whole, which is shorter than its diff:
```python
import math

import jax
import jax.numpy as jnp
from jax import lax
from jax.sharding import Mesh, PartitionSpec as P

F32 = jnp.float32
BF16 = jnp.bfloat16
PLANE = ("z", "y", "c")
ALL = ("x", "z", "y", "c")


def gelu_slope(value):
    cdf = 0.5 * (1.0 + lax.erf(value / math.sqrt(2.0)))
    return cdf + value * jnp.exp(-0.5 * value * value) / math.sqrt(2.0 * math.pi)


def split(value):
    head = lax.reduce_precision(value, 8, 7)
    return head.astype(BF16), (value - head).astype(BF16)


def mm(a, b, contract):
    return lax.dot_general(a, b, (contract, ((), ())), preferred_element_type=F32)


def mm_wide(a, wide, contract):
    head, rest = split(wide)
    out = mm(a, jnp.concatenate([head, rest], axis=1), contract)
    n = wide.shape[1]
    return out[:, :n] + out[:, n:]


def swap(value, axis, bit):
    n = lax.axis_size(axis)
    return lax.ppermute(value, axis, [(i, i ^ bit) for i in range(n)])


def lookup(station_weight, column):
    onehot = (
        column[:, None] == jnp.arange(station_weight.shape[0], dtype=jnp.int32)[None, :]
    ).astype(F32)
    return jnp.dot(onehot, station_weight, precision=lax.Precision.HIGHEST)


def halve(value, axis, bit):
    mine = (lax.axis_index(axis) // bit) % 2
    half = value.shape[0] // 2
    give = lax.dynamic_slice_in_dim(value, (1 - mine) * half, half, 0).astype(BF16)
    keep = lax.dynamic_slice_in_dim(value, mine * half, half, 0)
    return keep.astype(F32) + swap(give, axis, bit).astype(F32)


def per_device(features, preact, upstream, weight, pairs, station_weight, counts, error, basis):
    n_inter = lax.axis_size("x")
    group_rows, width = preact.shape[0], features.shape[1]
    rank = basis.shape[1]
    c = lax.axis_index("c")

    own = counts.astype(F32)
    own = own + swap(own, "x", 1)
    total = (own + swap(own, "x", 2))[0]
    inv_mean = n_inter / total

    all_features = lax.all_gather(features, PLANE, axis=0, tiled=True)
    other = swap(features, "c", 1)
    pair_features = jnp.where(
        c == 0, jnp.concatenate([features, other]), jnp.concatenate([other, features])
    )

    scale = lookup(station_weight, pairs[:, 0]) * lookup(station_weight, pairs[:, 1])
    live = (jnp.arange(group_rows, dtype=jnp.int32) < counts[0]).astype(F32)
    dpre = (
        upstream.astype(F32) * gelu_slope(preact.astype(F32)) * (scale * live)[:, None]
    ).astype(BF16)

    share = mm_wide(dpre, basis, ((1,), (0,)))
    share = share + swap(share, "c", 1)

    err_left = mm_wide(error, basis, ((1,), (0,)))
    half = width // 2
    err_give = lax.dynamic_slice_in_dim(err_left, (1 - c) * half, half, 0)
    err_keep = lax.dynamic_slice_in_dim(err_left, c * half, half, 0)
    err_half = err_keep + swap(err_give, "c", 1)

    rows = dpre.reshape(2, 2, 2, 2, 2, 2, 8, dpre.shape[1])
    rows = rows.transpose(5, 4, 2, 3, 1, 0, 6, 7).reshape(dpre.shape)
    grad = mm(rows, weight, ((1,), (1,))).astype(BF16)
    grad = halve(grad, "c", 1)
    grad = halve(grad, "y", 1)

    tokens = group_rows // 32
    share = lax.all_to_all(share, ("z", "y"), 0, 0, tiled=True)
    share = share.reshape(32, tokens, rank).sum(0) * inv_mean
    pair_half = lax.dynamic_slice_in_dim(pair_features, c * half, half, 1)
    part = err_half + mm_wide(pair_half, share, ((0,), (0,)))

    grad, part = lax.optimization_barrier((grad, part))
    grad = halve(grad, "z", 1)

    part = lax.all_to_all(part, ("x", "y"), 0, 0, tiled=True)
    part = part.reshape(16, half // 16, rank).sum(0)
    for bit in (1, 2, 4):
        part = part + swap(part, "z", bit)

    grad, part = lax.optimization_barrier((grad, part))
    grad = halve(grad, "y", 2)

    mine = lax.all_to_all(
        jnp.broadcast_to(part[None], (16,) + part.shape), ("x", "y"), 0, 0, tiled=True
    ).reshape(half, rank)
    gram = jnp.dot(mine.T, mine, precision=lax.Precision.HIGHEST)
    gram = gram + swap(gram, "c", 1)
    other = swap(mine, "c", 1)
    left = jnp.where(c == 0, jnp.concatenate([mine, other]), jnp.concatenate([other, mine]))

    grad, left = lax.optimization_barrier((grad, left))
    grad = halve(grad, "z", 2)

    raw = mm(all_features, dpre, ((0,), (0,)))
    merged = raw * inv_mean + error.astype(F32)
    right = lax.dot_general(
        merged, left, (((0,), (0,)), ((), ())), precision=lax.Precision.HIGH
    )
    right = right + swap(right, "x", 1)
    right = right + swap(right, "x", 2)

    grad = halve(grad, "z", 4).astype(BF16)

    chol = jnp.linalg.cholesky(gram)
    inverse = lax.linalg.triangular_solve(
        chol, jnp.eye(rank, dtype=F32), left_side=True, lower=True
    )
    new_basis = jnp.dot(right, inverse.T, precision=lax.Precision.HIGHEST)
    back = jnp.dot(new_basis, inverse, precision=lax.Precision.HIGHEST)
    new_error = (
        merged - jnp.dot(left, back.T, precision=lax.Precision.HIGH) / n_inter
    ).astype(BF16)
    return grad, new_error, new_basis


def solution(mesh):
    mesh = Mesh(mesh.devices.reshape(4, 8, 4, 2), ALL)
    in_specs = (
        P(ALL, None),
        P("x", PLANE),
        P("x", PLANE),
        P(None, PLANE),
        P("x", None),
        P(),
        P("x"),
        P("x", PLANE),
        P(PLANE, None),
    )
    out_specs = (P(ALL, None), P("x", PLANE), P(PLANE, None))
    return jax.shard_map(
        per_device, mesh=mesh, in_specs=in_specs, out_specs=out_specs, check_vma=False
    )
```

time: 508 us -> 210 us (0.41)
  blocking collectives: 306 us -> 0 us
  waiting for transfers between devices: 106 us -> 49.8 us
  starting transfers between devices: 0.12 us -> 52.1 us
  matrix products: 42.6 us -> 18.2 us
  other arithmetic: 22.9 us -> 46.6 us
  local copies, waits for them, and re-layouts: 15.1 us -> 24.1 us
    unnamed x1 -> x0, blocking collectives: 294 us -> none
    all_gather x1, waiting for transfers between devices: 57.5 us -> 0.01 us  [per_device(): all_features = lax.all_gather(features, PLANE, axis=0, tiled=True)]
    psum x2 -> x0, waiting for transfers between devices: 47.5 us -> none  [the longest x1 47.5 us: per_device(): new_basis = lax.psum(right_term, 'inter')]
    ppermute x0 -> x18, waiting for transfers between devices: none -> 33.7 us  [swap(): return lax.ppermute(value, axis, [(i, i ^ bit) for i in range(n)])]
    ppermute x0 -> x18, starting transfers between devices: none -> 26.5 us  [swap(): return lax.ppermute(value, axis, [(i, i ^ bit) for i in range(n)])]
    all_to_all x0 -> x3, starting transfers between devices: none -> 25.6 us  [the longest x1 11.7 us: per_device(): share = lax.all_to_all(share, ('z', 'y'), 0, 0, tiled=True)]
    dot_general x8 -> x12, matrix products: 39 us -> 18 us  [the longest x5 7.28 us: mm(): lax.dot_general(a, b, (contract, ((), ())), preferred_element_type=F32)]
    add x0 -> x14, other arithmetic: none -> 16 us  [the longest x5 11 us: halve(): return keep.astype(F32) + swap(give, axis, bit).astype(F32)]
  transfers between devices with their start and end apart: 3 -> 22, of which waited for: 2 -> 11; matrix products, arithmetic and copies ran while one was open for 3% -> 33% of each run, Pallas kernels for 0% -> 0%
where the time goes in v1:
time: 210 us; the launch traced here: 207 us
  starting transfers between devices  52.1 us (25%)
  waiting for transfers between devices  49.8 us (24%)
  other arithmetic  46.6 us (22%)
  local copies, waits for them, and re-layouts  24.1 us (11%)
  matrix products  18.2 us (9%)
  between operations  16.5 us (8%)
    ppermute x18, waiting for transfers between devices, swap(): return lax.ppermute(value, axis, [(i, i ^ bit) for i in range(n)])  33.7 us
    ppermute x18, starting transfers between devices, swap(): return lax.ppermute(value, axis, [(i, i ^ bit) for i in range(n)])  26.5 us
    another operation x3, other arithmetic, per_device(): chol = jnp.linalg.cholesky(gram)  13.2 us
    all_to_all x1, waiting for transfers between devices, per_device(): part = lax.all_to_all(part, ('x', 'y'), 0, 0, tiled=True)  12.3 us
    unnamed x28, local copies, waits for them, and re-layouts  12.1 us
    all_to_all x1, starting transfers between devices, per_device(): share = lax.all_to_all(share, ('z', 'y'), 0, 0, tiled=True)  11.7 us
    add x5, other arithmetic, halve(): return keep.astype(F32) + swap(give, axis, bit).astype(F32)  11 us
    another operation x2, other arithmetic, per_device(): lax.linalg.triangular_solve(chol, jnp.eye(rank, dtype=F32), left_side=Tru...  10.5 us
  transfers between devices with their start and end apart: 22, of which 11 were waited for; matrix products, arithmetic and copies ran while one was open for 33% of the time, Pallas kernels for 0%

profile of v1, /device:TPU:8, one launch (start us, length us, event | category | flops | bytes accessed | tf_op | source)
XLA Modules:
  0.0 207.4 jit_solution(6433713360783759295)
XLA Ops:
  7.2 0.9 fusion.39
  8.1 1.3 fusion.5
  9.4 1.3 fusion.6
  11.4 1.3 multiply_convert_fusion
  12.7 1.3 convolution_convert_fusion
  14.1 1.5 constant_dynamic-slice_fusion.1
  15.5 1.4 copy-done.1
  17.8 0.8 convolution_bitcast_fusion
  18.6 1.6 slice_add_fusion
  20.1 2.3 %constant_dynamic-slice_fusion = f32[2048,128]{0,1:T(8,128)} fusion(f32[4096,128]{0,1:T(8,128)} %slice_add_fusion, s32[]{:T(128)S(6)} %select_n.110), kind=kLoop, calls=%fused_computation.76 | loop fusion | bytes 2097156 | tf_op jit(solution)/shard_map/dynamic_slice | solution.py:83
  22.5 1.7 fusion.58
  24.2 11.7 %all-to-all-start = ((f32[32,16,128]{2,1,0:T(8,128)}), f32[32,16,128]{2,1,0:T(8,128)}, u32[]{:S(2)}, u32[]{:S(2)}) async-start(f32[32,16,128]{2,1,0:T(8,128)} %bitcast.11), calls=%async_computation | async-start | bytes 524288 | tf_op jit(solution)/shard_map/all_to_all | solution.py:94
  36.0 2.9 %convert_add_fusion = f32[256,4096]{1,0:T(8,128)S(1)} fusion(bf16[256,4096]{1,0:T(8,128)(2,1)} %collective-permute-done, bf16[512,4096]{1,0:T(8,128)(2,1)} %copy-done.1, s32[]{:T(128)S(6)} %select_n.104), kind=kLoop, calls=%fused_computation.6 | loop fusion | flops 3145728 | bytes 8388612 | tf_op jit(solution)/shard_map/add | solution.py:52
  39.0 2.0 copy-done.4
  41.8 2.9 %collective-permute-start.5 = (f32[1]{0:T(128)}, f32[1]{0:T(128)}, u32[]{:S(2)}, u32[]{:S(2)}) collective-permute-start(f32[1]{0:T(128)} %convert_element_type.88), channel_id=1, source_target_pairs={{0,64},{64,0},{128,192},{192,128},{1,65},{65,1},{129,193},{193,129... | collective-permute-start | bytes 20 | tf_op jit(solution)/shard_map/ppermute | solution.py:37
  44.7 0.7 collective-permute-done.5
  46.1 4.4 %collective-permute-start.6 = (f32[1]{0:T(128)}, f32[1]{0:T(128)}, u32[]{:S(2)}, u32[]{:S(2)}) collective-permute-start(f32[1]{0:T(128)} %add.168), channel_id=1, source_target_pairs={{0,128},{64,192},{128,0},{192,64},{1,129},{65,193},{129,1},{193,65... | collective-permute-start | bytes 20 | tf_op jit(solution)/shard_map/ppermute | solution.py:37
  50.5 0.7 collective-permute-done.6
  51.9 1.0 reduce_sum.18
  53.0 1.4 fusion.23
  54.6 1.7 fusion.4
  56.2 11.2 %collective-permute-done.1 = bf16[128,4096]{1,0:T(8,128)(2,1)} collective-permute-done((bf16[128,4096]{1,0:T(8,128)(2,1)S(1)}, bf16[128,4096]{1,0:T(8,128)(2,1)}, u32[]{:S(2)}, u32[]{:S(2)}) %collective-permute-start.1) | collective-permute-done | bytes 1048608 | tf_op jit(solution)/shard_map/ppermute | solution.py:37
  67.5 2.8 %convert_add_fusion.1 = f32[128,4096]{1,0:T(8,128)} fusion(bf16[128,4096]{1,0:T(8,128)(2,1)} %collective-permute-done.1, f32[256,4096]{1,0:T(8,128)S(1)} %copy-done.5, s32[]{:T(128)S(6)} %select_n.107), kind=kLoop, calls=%fused_computation.11 | loop fusion | flops 1048576 | bytes 5242884 | tf_op jit(solution)/shard_map/add | solution.py:52
  70.3 1.1 copy_bitcast_fusion
  71.4 7.5 %all-to-all-start.1 = ((f32[16,128,128]{1,2,0:T(8,128)}), f32[16,128,128]{1,2,0:T(8,128)S(1)}, u32[]{:S(2)}, u32[]{:S(2)}) async-start(f32[16,128,128]{1,2,0:T(8,128)} %copy_bitcast_fusion), calls=%async_computation.1 | async-start | bytes 2097152 | tf_op jit(solution)/shard_map/all_to_all | solution.py:102
  78.9 2.1 %dynamic-slice_convert_fusion.1 = bf16[64,4096]{1,0:T(8,128)(2,1)} fusion(f32[128,4096]{1,0:T(8,128)} %convert_add_fusion.1, s32[]{:T(128)S(6)} %select_n.115), kind=kLoop, calls=%fused_computation.18 | loop fusion | bytes 1048580 | tf_op jit(solution)/shard_map/convert_element_type | solution.py:50
  81.0 1.3 collective-permute-start.7
  82.3 12.3 %all-to-all-done.1 = f32[16,128,128]{1,2,0:T(8,128)S(1)} async-done(((f32[16,128,128]{1,2,0:T(8,128)}), f32[16,128,128]{1,2,0:T(8,128)S(1)}, u32[]{:S(2)}, u32[]{:S(2)}) %all-to-all-start.1) | async-done | bytes 1048608 | tf_op jit(solution)/shard_map/all_to_all | solution.py:102
  94.6 0.9 collective-permute-start.8
  95.5 4.0 %collective-permute-done.8 = f32[128,128]{0,1:T(8,128)S(1)} collective-permute-done((f32[128,128]{0,1:T(8,128)S(1)}, f32[128,128]{0,1:T(8,128)S(1)}, u32[]{:S(2)}, u32[]{:S(2)}) %collective-permute-start.8) | collective-permute-done | bytes 65568 | tf_op jit(solution)/shard_map/ppermute | solution.py:37
  99.5 1.7 collective-permute-start.9
  101.2 5.2 %collective-permute-done.9 = f32[128,128]{0,1:T(8,128)S(1)} collective-permute-done((f32[128,128]{0,1:T(8,128)S(1)}, f32[128,128]{0,1:T(8,128)S(1)}, u32[]{:S(2)}, u32[]{:S(2)}) %collective-permute-start.9) | collective-permute-done | bytes 65568 | tf_op jit(solution)/shard_map/ppermute | solution.py:37
  106.4 4.2 %collective-permute-start.10 = (f32[128,128]{0,1:T(8,128)S(1)}, f32[128,128]{0,1:T(8,128)S(1)}, u32[]{:S(2)}, u32[]{:S(2)}) collective-permute-start(f32[128,128]{0,1:T(8,128)S(1)} %add.177), channel_id=1, source_target_pairs={{0,32},{8,40},{16,48},{24,56},{32,0},{40,8},{48,16},{56,24},{1,33}... | collective-permute-start | bytes 196616 | tf_op jit(solution)/shard_map/ppermute | solution.py:37
  110.6 2.4 %convert_add_fusion.2 = f32[64,4096]{1,0:T(8,128)} fusion(bf16[64,4096]{1,0:T(8,128)(2,1)} %collective-permute-done.7, f32[128,4096]{1,0:T(8,128)} %convert_add_fusion.1, s32[]{:T(128)S(6)} %select_n.114), kind=kLoop, calls=%fused_computation.17 | loop fusion | flops 524288 | bytes 2621444 | tf_op jit(solution)/shard_map/add | solution.py:52
  113.0 2.2 %collective-permute-done.10 = f32[128,128]{0,1:T(8,128)S(1)} collective-permute-done((f32[128,128]{0,1:T(8,128)S(1)}, f32[128,128]{0,1:T(8,128)S(1)}, u32[]{:S(2)}, u32[]{:S(2)}) %collective-permute-start.10) | collective-permute-done | bytes 65568 | tf_op jit(solution)/shard_map/ppermute | solution.py:37
  115.3 1.1 broadcast_in_dim.3
  116.4 6.4 %all-to-all-start.2 = ((f32[16,128,128]{2,1,0:T(8,128)}), f32[16,128,128]{2,1,0:T(8,128)S(1)}, u32[]{:S(2)}, u32[]{:S(2)}) async-start(f32[16,128,128]{2,1,0:T(8,128)} %broadcast_in_dim.3), calls=%async_computation.2 | async-start | bytes 2097152 | tf_op jit(solution)/shard_map/all_to_all | solution.py:110
  122.8 1.8 dynamic-slice_convert_fusion.2
  124.6 2.1 %collective-permute-start.11 = (bf16[32,4096]{1,0:T(8,128)(2,1)}, bf16[32,4096]{1,0:T(8,128)(2,1)}, u32[]{:S(2)}, u32[]{:S(2)}) collective-permute-start(bf16[32,4096]{1,0:T(8,128)(2,1)} %dynamic-slice_convert_fusion.2), channel_id=1, source_target_pairs={{0,4},{2,6},{4,0},{6,2},{1,5},{3,7},{5,1},{7,3},{8,12},{10,14},{12... | collective-permute-start | bytes 786440 | tf_op jit(solution)/shard_map/ppermute | solution.py:37
  126.7 4.1 %copy.46 = bf16[4096,256]{0,1:T(8,128)(2,1)} copy(bf16[4096,256]{1,0:T(8,128)(2,1)} %param.16) | data formatting | bytes 4194304 | tf_op args[7]
  130.8 3.7 %all-to-all-done.2 = f32[16,128,128]{2,1,0:T(8,128)S(1)} async-done(((f32[16,128,128]{2,1,0:T(8,128)}), f32[16,128,128]{2,1,0:T(8,128)S(1)}, u32[]{:S(2)}, u32[]{:S(2)}) %all-to-all-start.2) | async-done | bytes 1048608 | tf_op jit(solution)/shard_map/all_to_all | solution.py:110
  134.6 1.8 convolution_bitcast_fusion.1
  136.4 0.6 collective-permute-start.17
  137.0 1.1 collective-permute-done.11
  138.1 1.8 convert_add_fusion.3
  140.0 0.6 fusion.29
  140.7 12.5 %cholesky.17 = f32[128,128]{1,0:T(8,128)S(1)} custom-call(f32[128,128]{1,0:T(8,128)} %fusion.29), custom_call_target="Cholesky" | custom-call | tf_op jit(solution)/shard_map/jit(cholesky)/cholesky | solution.py:131
  153.3 0.6 compare_reduce_fusion
  153.9 3.2 %maximum_select_fusion = f32[4096,128]{1,0:T(8,128)} fusion(f32[2048,128]{1,0:T(8,128)} %collective-permute-done.12, f32[2048,128]{1,0:T(8,128)S(1)} %bitcast.57, pred[]{:T(512)S(6)} %eq.50), kind=kLoop, calls=%fused_computation.9 | loop fusion | flops 1572864 | bytes 4194305 | tf_op jit(solution)/shard_map/jit(_where)/select_n | solution.py:116
  157.1 1.0 dynamic-slice_convert_fusion.3
  158.1 1.0 collective-permute-start.13
  159.1 0.7 fusion.20
  159.8 9.8 %custom-call.6 = f32[1,128,128]{1,2,0:T(8,128)S(1)} custom-call(f32[1,128,128]{2,1,0:T(8,128)S(1)} %fusion.20), custom_call_target="InvertDiagBlocksLowerTriangular" | custom-call | tf_op jit(solution)/shard_map/triangular_solve | solution.py:132
  169.6 1.0 convert_add_fusion.4
  170.6 4.0 %collective-permute-start.14 = (bf16[8,4096]{1,0:T(8,128)(2,1)S(1)}, bf16[8,4096]{1,0:T(8,128)(2,1)S(1)}, u32[]{:S(2)}, u32[]{:S(2)}) collective-permute-start(bf16[8,4096]{1,0:T(8,128)(2,1)S(1)} %dynamic-slice_convert_fusion.4), channel_id=1, source_target_pairs={{0,32},{8,40},{16,48},{24,56},{32,0},{40,8},{48,16},{56,24},{1,33}... | collective-permute-start | bytes 196616 | tf_op jit(solution)/shard_map/ppermute | solution.py:37
  174.7 3.6 %fusion.40 = f32[256,4096]{1,0:T(8,128)S(1)} fusion(bf16[512,256]{1,0:T(8,128)(2,1)S(1)} %multiply_convert_fusion, bf16[512,4096]{1,0:T(8,128)(2,1)} %all-gather.2.cloned.1.call-done), kind=kOutput, calls=%fused_computation.85 | convolution fusion | flops 1073741824 | bytes 8650752 | tf_op jit(solution)/shard_map/dot_general | solution.py:25
  178.3 2.0 fusion.2
  180.3 0.8 collective-permute-start.15
  181.4 4.3 %collective-permute-done.15 = f32[256,128]{1,0:T(8,128)S(1)} collective-permute-done((f32[256,128]{1,0:T(8,128)S(1)}, f32[256,128]{1,0:T(8,128)S(1)}, u32[]{:S(2)}, u32[]{:S(2)}) %collective-permute-start.15) | collective-permute-done | bytes 131104 | tf_op jit(solution)/shard_map/ppermute | solution.py:37
  185.6 1.6 collective-permute-start.16
  187.2 0.6 add_convert_fusion
  187.8 4.4 %collective-permute-done.16 = f32[256,128]{1,0:T(8,128)S(1)} collective-permute-done((f32[256,128]{1,0:T(8,128)S(1)}, f32[256,128]{1,0:T(8,128)S(1)}, u32[]{:S(2)}, u32[]{:S(2)}) %collective-permute-start.16) | collective-permute-done | bytes 131104 | tf_op jit(solution)/shard_map/ppermute | solution.py:37
  192.8 3.7 %fusion.1 = bf16[4096,256]{0,1:T(8,128)(2,1)} fusion(f32[4096,128]{1,0:T(8,128)S(1)} %copy-done.3, f32[256,128]{1,0:T(8,128)S(1)} %fusion.41, bf16[4096,256]{0,1:T(8,128)(2,1)S(1)} %copy-done.2, f32[256,4096]{1,0:T(8,128)S(1)} %fusion.40, f32[]{:T(128)} %bitcast.12), kind=kOutput, calls=%fused_computation.4 | convolution fusion | flops 811597824 | bytes 10616836 | tf_op jit(solution)/shard_map/dot_general | solution.py:138
  196.5 4.1 %copy.52 = bf16[4096,256]{1,0:T(8,128)(2,1)} copy(bf16[4096,256]{0,1:T(8,128)(2,1)} %fusion.1) | data formatting | bytes 4194304
  (63 shorter events, 3.2 us)
Async XLA Ops:
  7.2 5.5 %copy-start = (bf16[4096,256]{1,0:T(8,128)(2,1)S(1)}, bf16[4096,256]{1,0:T(8,128)(2,1)}, u32[]{:S(2)}) copy-start(bf16[4096,256]{1,0:T(8,128)(2,1)} %param.12) | copy-start | bytes 6291460
  14.0 2.9 %copy-start.1 = (bf16[512,4096]{1,0:T(8,128)(2,1)}, bf16[512,4096]{1,0:T(8,128)(2,1)S(1)}, u32[]{:S(2)}) copy-start(bf16[512,4096]{1,0:T(8,128)(2,1)S(1)} %convolution_convert_fusion) | copy-start | bytes 12582916
  14.0 2.9 %copy-start.12 = (f32[256,128]{1,0:T(8,128)S(1)}, f32[256,128]{1,0:T(8,128)}, u32[]{:S(2)}) copy-start(f32[256,128]{1,0:T(8,128)} %param.17) | copy-start | bytes 393220
  14.0 3.7 %copy-start.6 = (bf16[4096,256]{1,0:T(8,128)(2,1)S(1)}, bf16[4096,256]{1,0:T(8,128)(2,1)}, u32[]{:S(2)}) copy-start(bf16[4096,256]{1,0:T(8,128)(2,1)} %param.16) | copy-start | bytes 6291460
  16.9 19.1 %collective-permute-start = (bf16[256,4096]{1,0:T(8,128)(2,1)}, bf16[256,4096]{1,0:T(8,128)(2,1)}, u32[]{:S(2)}, u32[]{:S(2)}) collective-permute-start(bf16[256,4096]{1,0:T(8,128)(2,1)} %constant_dynamic-slice_fusion.1), channel_id=1, source_target_pairs={{0,1},{1,0},{2,3},{3,2},{4,5},{5,4},{6,7},{7,6},{8,9},{9,8},{10,11... | collective-permute-start | bytes 6291464 | tf_op jit(solution)/shard_map/ppermute | solution.py:37
  17.2 5.3 %collective-permute-start.4 = (f32[512,128]{1,0:T(8,128)S(1)}, f32[512,128]{1,0:T(8,128)}, u32[]{:S(2)}, u32[]{:S(2)}) collective-permute-start(f32[512,128]{1,0:T(8,128)S(1)} %slice_add_fusion.2), channel_id=1, source_target_pairs={{0,1},{1,0},{2,3},{3,2},{4,5},{5,4},{6,7},{7,6},{8,9},{9,8},{10,11... | collective-permute-start | bytes 786440 | tf_op jit(solution)/shard_map/ppermute | solution.py:37
  22.5 31.9 %collective-permute-start.2 = (f32[2048,128]{0,1:T(8,128)}, f32[2048,128]{0,1:T(8,128)}, u32[]{:S(2)}, u32[]{:S(2)}) collective-permute-start(f32[2048,128]{0,1:T(8,128)} %constant_dynamic-slice_fusion), channel_id=1, source_target_pairs={{0,1},{1,0},{2,3},{3,2},{4,5},{5,4},{6,7},{7,6},{8,9},{9,8},{10,11... | collective-permute-start | bytes 3145736 | tf_op jit(solution)/shard_map/ppermute | solution.py:37
  24.2 27.8 %all-to-all-start = ((f32[32,16,128]{2,1,0:T(8,128)}), f32[32,16,128]{2,1,0:T(8,128)}, u32[]{:S(2)}, u32[]{:S(2)}) async-start(f32[32,16,128]{2,1,0:T(8,128)} %bitcast.11), calls=%async_computation | async-start | bytes 524288 | tf_op jit(solution)/shard_map/all_to_all | solution.py:94
  35.9 138.7 %all-gather.2.cloned.1.call-start = ((), (), s32[]{:S(2)}) async-start(), calls=%async_computation.3 | async-start | bytes 4259840 | tf_op jit(solution)/shard_map/all_gather | solution.py:66
  38.9 2.0 copy-start.4
  41.0 0.8 copy-start.10
  41.0 12.0 %copy-start.11 = (bf16[8,4096]{1,0:T(8,128)(2,1)S(1)}, bf16[8,4096]{1,0:T(8,128)(2,1)}, u32[]{:S(2)}) copy-start(bf16[8,4096]{1,0:T(8,128)(2,1)} %param.9) | copy-start | bytes 196612
  41.1 26.4 %collective-permute-start.1 = (bf16[128,4096]{1,0:T(8,128)(2,1)S(1)}, bf16[128,4096]{1,0:T(8,128)(2,1)}, u32[]{:S(2)}, u32[]{:S(2)}) collective-permute-start(bf16[128,4096]{1,0:T(8,128)(2,1)S(1)} %dynamic-slice_convert_fusion), channel_id=1, source_target_pairs={{0,2},{2,0},{4,6},{6,4},{1,3},{3,1},{5,7},{7,5},{8,10},{10,8},{12,... | collective-permute-start | bytes 3145736 | tf_op jit(solution)/shard_map/ppermute | solution.py:37
  41.8 11.1 %collective-permute-start.3 = (bf16[8,4096]{1,0:T(8,128)(2,1)S(1)}, bf16[8,4096]{1,0:T(8,128)(2,1)}, u32[]{:S(2)}, u32[]{:S(2)}) collective-permute-start(bf16[8,4096]{1,0:T(8,128)(2,1)S(1)} %copy-done.10), channel_id=1, source_target_pairs={{0,1},{1,0},{2,3},{3,2},{4,5},{5,4},{6,7},{7,6},{8,9},{9,8},{10,11... | collective-permute-start | bytes 196616 | tf_op jit(solution)/shard_map/ppermute | solution.py:37
  41.8 3.6 %collective-permute-start.5 = (f32[1]{0:T(128)}, f32[1]{0:T(128)}, u32[]{:S(2)}, u32[]{:S(2)}) collective-permute-start(f32[1]{0:T(128)} %convert_element_type.88), channel_id=1, source_target_pairs={{0,64},{64,0},{128,192},{192,128},{1,65},{65,1},{129,193},{193,129... | collective-permute-start | bytes 20 | tf_op jit(solution)/shard_map/ppermute | solution.py:37
  46.1 5.1 %collective-permute-start.6 = (f32[1]{0:T(128)}, f32[1]{0:T(128)}, u32[]{:S(2)}, u32[]{:S(2)}) collective-permute-start(f32[1]{0:T(128)} %add.168), channel_id=1, source_target_pairs={{0,128},{64,192},{128,0},{192,64},{1,129},{65,193},{129,1},{193,65... | collective-permute-start | bytes 20 | tf_op jit(solution)/shard_map/ppermute | solution.py:37
  52.9 1.6 copy-start.7
  54.4 13.1 %copy-start.5 = (f32[256,4096]{1,0:T(8,128)S(1)}, f32[256,4096]{1,0:T(8,128)}, u32[]{:S(2)}) copy-start(f32[256,4096]{1,0:T(8,128)} %copy-done.4) | copy-start | bytes 12582916
  71.4 23.1 %all-to-all-start.1 = ((f32[16,128,128]{1,2,0:T(8,128)}), f32[16,128,128]{1,2,0:T(8,128)S(1)}, u32[]{:S(2)}, u32[]{:S(2)}) async-start(f32[16,128,128]{1,2,0:T(8,128)} %copy_bitcast_fusion), calls=%async_computation.1 | async-start | bytes 2097152 | tf_op jit(solution)/shard_map/all_to_all | solution.py:102
  81.0 29.6 %collective-permute-start.7 = (bf16[64,4096]{1,0:T(8,128)(2,1)}, bf16[64,4096]{1,0:T(8,128)(2,1)}, u32[]{:S(2)}, u32[]{:S(2)}) collective-permute-start(bf16[64,4096]{1,0:T(8,128)(2,1)} %dynamic-slice_convert_fusion.1), channel_id=1, source_target_pairs={{0,8},{8,0},{16,24},{24,16},{32,40},{40,32},{48,56},{56,48},{1,9},... | collective-permute-start | bytes 1572872 | tf_op jit(solution)/shard_map/ppermute | solution.py:37
  94.6 4.9 %collective-permute-start.8 = (f32[128,128]{0,1:T(8,128)S(1)}, f32[128,128]{0,1:T(8,128)S(1)}, u32[]{:S(2)}, u32[]{:S(2)}) collective-permute-start(f32[128,128]{0,1:T(8,128)S(1)} %reduce_sum.19), channel_id=1, source_target_pairs={{0,8},{8,0},{16,24},{24,16},{32,40},{40,32},{48,56},{56,48},{1,9},... | collective-permute-start | bytes 196616 | tf_op jit(solution)/shard_map/ppermute | solution.py:37
  99.5 6.9 %collective-permute-start.9 = (f32[128,128]{0,1:T(8,128)S(1)}, f32[128,128]{0,1:T(8,128)S(1)}, u32[]{:S(2)}, u32[]{:S(2)}) collective-permute-start(f32[128,128]{0,1:T(8,128)S(1)} %add.176), channel_id=1, source_target_pairs={{0,16},{8,24},{16,0},{24,8},{32,48},{40,56},{48,32},{56,40},{1,17}... | collective-permute-start | bytes 196616 | tf_op jit(solution)/shard_map/ppermute | solution.py:37
  106.4 8.8 %collective-permute-start.10 = (f32[128,128]{0,1:T(8,128)S(1)}, f32[128,128]{0,1:T(8,128)S(1)}, u32[]{:S(2)}, u32[]{:S(2)}) collective-permute-start(f32[128,128]{0,1:T(8,128)S(1)} %add.177), channel_id=1, source_target_pairs={{0,32},{8,40},{16,48},{24,56},{32,0},{40,8},{48,16},{56,24},{1,33}... | collective-permute-start | bytes 196616 | tf_op jit(solution)/shard_map/ppermute | solution.py:37
  116.4 18.1 %all-to-all-start.2 = ((f32[16,128,128]{2,1,0:T(8,128)}), f32[16,128,128]{2,1,0:T(8,128)S(1)}, u32[]{:S(2)}, u32[]{:S(2)}) async-start(f32[16,128,128]{2,1,0:T(8,128)} %broadcast_in_dim.3), calls=%async_computation.2 | async-start | bytes 2097152 | tf_op jit(solution)/shard_map/all_to_all | solution.py:110
  124.6 13.5 %collective-permute-start.11 = (bf16[32,4096]{1,0:T(8,128)(2,1)}, bf16[32,4096]{1,0:T(8,128)(2,1)}, u32[]{:S(2)}, u32[]{:S(2)}) collective-permute-start(bf16[32,4096]{1,0:T(8,128)(2,1)} %dynamic-slice_convert_fusion.2), channel_id=1, source_target_pairs={{0,4},{2,6},{4,0},{6,2},{1,5},{3,7},{5,1},{7,3},{8,12},{10,14},{12... | collective-permute-start | bytes 786440 | tf_op jit(solution)/shard_map/ppermute | solution.py:37
  134.6 3.6 %copy-start.8 = (f32[64,4096]{1,0:T(8,128)S(1)}, f32[64,4096]{1,0:T(8,128)}, u32[]{:S(2)}) copy-start(f32[64,4096]{1,0:T(8,128)} %convert_add_fusion.2) | copy-start | bytes 3145732
  134.6 19.4 %collective-permute-start.12 = (f32[2048,128]{1,0:T(8,128)S(1)}, f32[2048,128]{1,0:T(8,128)}, u32[]{:S(2)}, u32[]{:S(2)}) collective-permute-start(f32[2048,128]{1,0:T(8,128)S(1)} %bitcast.56), channel_id=1, source_target_pairs={{0,1},{1,0},{2,3},{3,2},{4,5},{5,4},{6,7},{7,6},{8,9},{9,8},{10,11... | collective-permute-start | bytes 3145736 | tf_op jit(solution)/shard_map/ppermute | solution.py:37
  136.4 3.6 %collective-permute-start.17 = (f32[128,128]{0,1:T(8,128)S(1)}, f32[128,128]{0,1:T(8,128)S(1)}, u32[]{:S(2)}, u32[]{:S(2)}) collective-permute-start(f32[128,128]{0,1:T(8,128)S(1)} %convolution_bitcast_fusion.1), channel_id=1, source_target_pairs={{0,1},{1,0},{2,3},{3,2},{4,5},{5,4},{6,7},{7,6},{8,9},{9,8},{10,11... | collective-permute-start | bytes 196616 | tf_op jit(solution)/shard_map/ppermute | solution.py:37
  158.1 11.5 %collective-permute-start.13 = (bf16[16,4096]{1,0:T(8,128)(2,1)S(1)}, bf16[16,4096]{1,0:T(8,128)(2,1)S(1)}, u32[]{:S(2)}, u32[]{:S(2)}) collective-permute-start(bf16[16,4096]{1,0:T(8,128)(2,1)S(1)} %dynamic-slice_convert_fusion.3), channel_id=1, source_target_pairs={{0,16},{8,24},{16,0},{24,8},{32,48},{40,56},{48,32},{56,40},{1,17}... | collective-permute-start | bytes 393224 | tf_op jit(solution)/shard_map/ppermute | solution.py:37
  170.6 16.6 %collective-permute-start.14 = (bf16[8,4096]{1,0:T(8,128)(2,1)S(1)}, bf16[8,4096]{1,0:T(8,128)(2,1)S(1)}, u32[]{:S(2)}, u32[]{:S(2)}) collective-permute-start(bf16[8,4096]{1,0:T(8,128)(2,1)S(1)} %dynamic-slice_convert_fusion.4), channel_id=1, source_target_pairs={{0,32},{8,40},{16,48},{24,56},{32,0},{40,8},{48,16},{56,24},{1,33}... | collective-permute-start | bytes 196616 | tf_op jit(solution)/shard_map/ppermute | solution.py:37
  174.7 3.6 %copy-start.2 = (bf16[4096,256]{0,1:T(8,128)(2,1)S(1)}, bf16[4096,256]{0,1:T(8,128)(2,1)}, u32[]{:S(2)}) copy-start(bf16[4096,256]{0,1:T(8,128)(2,1)} %copy.46) | copy-start | bytes 6291460
  174.7 3.6 %copy-start.3 = (f32[4096,128]{1,0:T(8,128)S(1)}, f32[4096,128]{1,0:T(8,128)}, u32[]{:S(2)}) copy-start(f32[4096,128]{1,0:T(8,128)} %maximum_select_fusion) | copy-start | bytes 6291460
  180.3 5.3 %collective-permute-start.15 = (f32[256,128]{1,0:T(8,128)S(1)}, f32[256,128]{1,0:T(8,128)S(1)}, u32[]{:S(2)}, u32[]{:S(2)}) collective-permute-start(f32[256,128]{1,0:T(8,128)S(1)} %fusion.2), channel_id=1, source_target_pairs={{0,64},{64,0},{128,192},{192,128},{1,65},{65,1},{129,193},{193,129... | collective-permute-start | bytes 393224 | tf_op jit(solution)/shard_map/ppermute | solution.py:37
  185.6 6.6 %collective-permute-start.16 = (f32[256,128]{1,0:T(8,128)S(1)}, f32[256,128]{1,0:T(8,128)S(1)}, u32[]{:S(2)}, u32[]{:S(2)}) collective-permute-start(f32[256,128]{1,0:T(8,128)S(1)} %add.192), channel_id=1, source_target_pairs={{0,128},{64,192},{128,0},{192,64},{1,129},{65,193},{129,1},{193,65... | collective-permute-start | bytes 393224 | tf_op jit(solution)/shard_map/ppermute | solution.py:37
  192.5 4.0 %copy-start.9 = (f32[256,128]{1,0:T(8,128)}, f32[256,128]{1,0:T(8,128)S(1)}, u32[]{:S(2)}) copy-start(f32[256,128]{1,0:T(8,128)S(1)} %fusion.17) | copy-start | bytes 393220
Sparse Core Ops, SparseCore 0:
  42.0 80.5 all-gather.1

commit v2 on v1

v2 whole, which is shorter than its diff:
```python
import functools, math
import jax
import jax.numpy as jnp
from jax import lax
from jax.experimental import pallas as pl
from jax.experimental.pallas import tpu as pltpu
from jax.sharding import Mesh, PartitionSpec as P

F32 = jnp.float32
BF16 = jnp.bfloat16
HIGHEST = lax.Precision.HIGHEST
VMEM = 48 * 1024 * 1024


def gelu_slope(value):
    cdf = 0.5 * (1.0 + lax.erf(value / math.sqrt(2.0)))
    return cdf + value * jnp.exp(-0.5 * value * value) / math.sqrt(2.0 * math.pi)


def split(value):
    head = value.astype(BF16)
    return head, (value - head.astype(F32)).astype(BF16)


def mm(a, b, contract):
    return lax.dot_general(a, b, (contract, ((), ())), preferred_element_type=F32)


def mm_wide(a, wide, contract):
    head, rest = split(wide)
    out = mm(a, jnp.concatenate([head, rest], axis=1), contract)
    n = wide.shape[1]
    return out[:, :n] + out[:, n:]


def mm_split(a, b, contract):
    return mm(a[0], b[0], contract) + (mm(a[0], b[1], contract) + mm(a[1], b[0], contract))


def params(**kw):
    return pltpu.CompilerParams(vmem_limit_bytes=VMEM, **kw)


def token_kernel(count_ref, pairs_ref, table_ref, up_ref, pre_ref, basis_ref, dpre_ref, share_ref):
    rows = up_ref.shape[0]
    stations = table_ref.shape[1]
    table = table_ref[...]
    head = table.astype(BF16)
    middle = (table - head.astype(F32)).astype(BF16)
    last = (table - head.astype(F32) - middle.astype(F32)).astype(BF16)
    which = lax.broadcasted_iota(jnp.int32, (stations, rows), 0)
    weight = None
    for end in range(2):
        onehot = (which == pairs_ref[end : end + 1, :]).astype(F32).astype(BF16)
        found = None
        for piece in (last, middle, head):
            term = mm(jnp.broadcast_to(piece, (16, stations)), onehot, ((1,), (0,)))[:1]
            found = term if found is None else found + term
        weight = found if weight is None else weight * found
    live = lax.broadcasted_iota(jnp.int32, (1, rows), 1) < count_ref[0]
    weight = jnp.where(live, weight, 0.0)
    column = jnp.transpose(jnp.broadcast_to(weight, (128, rows)))
    column = jnp.concatenate([column] * (up_ref.shape[1] // 128), axis=1)
    dpre = (up_ref[...].astype(F32) * gelu_slope(pre_ref[...].astype(F32)) * column).astype(BF16)
    dpre_ref[...] = dpre
    share_ref[...] = mm_wide(dpre, basis_ref[...], ((1,), (0,)))


def token_part(counts, pairs, table, upstream, preact, basis):
    vm = pl.BlockSpec(memory_space=pltpu.VMEM)
    return pl.pallas_call(
        token_kernel,
        out_shape=(
            jax.ShapeDtypeStruct(upstream.shape, BF16),
            jax.ShapeDtypeStruct((upstream.shape[0], basis.shape[1]), F32),
        ),
        in_specs=[pl.BlockSpec(memory_space=pltpu.SMEM)] + [vm] * 5,
        out_specs=(vm, vm),
        compiler_params=params(),
        cost_estimate=pl.CostEstimate(flops=10**8, bytes_accessed=10**6, transcendentals=10**5),
    )(counts, pairs.T, table[None], upstream, preact, basis)


def err_kernel(core_ref, error_ref, basis_ref, out_ref):
    out_ref[0] = mm_wide(error_ref[...], basis_ref[...], ((1,), (0,)))


def error_part(core, error, basis, step=2048):
    rows, cols = error.shape
    rank = basis.shape[1]
    half = rows // 2
    per = half // step
    return pl.pallas_call(
        err_kernel,
        out_shape=jax.ShapeDtypeStruct((2, half, rank), F32),
        grid_spec=pltpu.PrefetchScalarGridSpec(
            num_scalar_prefetch=1,
            grid=(2, per),
            in_specs=[
                pl.BlockSpec((step, cols), lambda h, i, core: ((core[0] + 1 - h) % 2 * per + i, 0)),
                pl.BlockSpec((cols, rank), lambda h, i, core: (0, 0)),
            ],
            out_specs=pl.BlockSpec((1, step, rank), lambda h, i, core: (1 - h, i, 0)),
        ),
        compiler_params=params(),
        cost_estimate=pl.CostEstimate(flops=10**9, bytes_accessed=4 * 10**6, transcendentals=0),
    )(core, error, basis)


def left_kernel(core_ref, inv_ref, share_ref, feat_ref, keep_ref, got_ref, out_ref):
    blocks = share_ref.shape[0]
    total = share_ref[0]
    for i in range(1, blocks):
        total = total + share_ref[i]
    total = total * inv_ref[0]
    out_ref[...] = keep_ref[0] + got_ref[...] + mm_wide(feat_ref[...], total, ((0,), (0,)))


def left_part(core, inv_mean, share, pair_features, err_halves, got):
    blocks, tokens, rank = share.shape
    half = got.shape[0]
    step = 1024
    per = half // step
    return pl.pallas_call(
        left_kernel,
        out_shape=jax.ShapeDtypeStruct((half, rank), F32),
        grid_spec=pltpu.PrefetchScalarGridSpec(
            num_scalar_prefetch=2,
            grid=(per,),
            in_specs=[
                pl.BlockSpec((blocks, tokens, rank), lambda i, core, inv: (0, 0, 0)),
                pl.BlockSpec((tokens, step), lambda i, core, inv: (0, core[0] * per + i)),
                pl.BlockSpec((1, step, rank), lambda i, core, inv: (0, i, 0)),
                pl.BlockSpec((step, rank), lambda i, core, inv: (i, 0)),
            ],
            out_specs=pl.BlockSpec((step, rank), lambda i, core, inv: (i, 0)),
        ),
        compiler_params=params(),
        cost_estimate=pl.CostEstimate(flops=10**8, bytes_accessed=4 * 10**6, transcendentals=0),
    )(core, inv_mean, share, pair_features, err_halves, got)


def merge_kernel(inv_ref, feat_ref, dpre_ref, error_ref, merged_ref, head_ref, rest_ref):
    raw = mm(feat_ref[...], dpre_ref[...], ((0,), (0,)))
    merged = raw * inv_ref[0] + error_ref[...].astype(F32)
    merged_ref[...] = merged
    head, rest = split(jnp.transpose(merged))
    head_ref[...] = head
    rest_ref[...] = rest


def merge_part(inv_mean, features, dpre, error):
    tokens, width = features.shape
    cols = dpre.shape[1]
    step = 512
    return pl.pallas_call(
        merge_kernel,
        out_shape=(
            jax.ShapeDtypeStruct((width, cols), F32),
            jax.ShapeDtypeStruct((cols, width), BF16),
            jax.ShapeDtypeStruct((cols, width), BF16),
        ),
        grid=(width // step,),
        in_specs=[
            pl.BlockSpec(memory_space=pltpu.SMEM),
            pl.BlockSpec((tokens, step), lambda i: (0, i)),
            pl.BlockSpec((tokens, cols), lambda i: (0, 0)),
            pl.BlockSpec((step, cols), lambda i: (i, 0)),
        ],
        out_specs=(
            pl.BlockSpec((step, cols), lambda i: (i, 0)),
            pl.BlockSpec((cols, step), lambda i: (0, i)),
            pl.BlockSpec((cols, step), lambda i: (0, i)),
        ),
        compiler_params=params(),
        cost_estimate=pl.CostEstimate(flops=2 * 10**9, bytes_accessed=16 * 10**6, transcendentals=0),
    )(inv_mean, features, dpre, error)


def right_kernel(head_ref, rest_ref, left_ref, right_ref):
    lh, ll = split(left_ref[...])
    rank = lh.shape[1]
    both = mm(head_ref[...], jnp.concatenate([lh, ll], axis=1), ((1,), (0,)))
    term = both[:, :rank] + both[:, rank:] + mm(rest_ref[...], lh, ((1,), (0,)))

    @pl.when(pl.program_id(0) == 0)
    def _():
        right_ref[...] = term

    @pl.when(pl.program_id(0) > 0)
    def _():
        right_ref[...] += term


def right_part(head, rest, left, step=2048):
    cols, width = head.shape
    rank = left.shape[1]
    return pl.pallas_call(
        right_kernel,
        out_shape=jax.ShapeDtypeStruct((cols, rank), F32),
        grid=(width // step,),
        in_specs=[
            pl.BlockSpec((cols, step), lambda i: (0, i)),
            pl.BlockSpec((cols, step), lambda i: (0, i)),
            pl.BlockSpec((step, rank), lambda i: (i, 0)),
        ],
        out_specs=pl.BlockSpec((cols, rank), lambda i: (0, 0)),
        compiler_params=params(),
        cost_estimate=pl.CostEstimate(flops=10**9, bytes_accessed=6 * 10**6, transcendentals=0),
    )(head, rest, left)


def inverse_kernel(gram_ref, out_ref):
    n = gram_ref.shape[0]
    a = gram_ref[...]
    b = (
        lax.broadcasted_iota(jnp.int32, (n, n), 0) == lax.broadcasted_iota(jnp.int32, (n, n), 1)
    ).astype(F32)
    for low in range(0, n, 8):
        left = n - low
        row_index = lax.broadcasted_iota(jnp.int32, (left, n), 0)
        columns = [
            jnp.broadcast_to(a[:, low + j : low + j + 1], (left, n)) for j in range(8)
        ]
        for j in range(8):
            column = columns[j]
            pivot = column[j : j + 1, :]
            scale = lax.rsqrt(pivot)
            scale = scale * (1.5 - 0.5 * pivot * scale * scale)
            row_a, row_b = a[j : j + 1, :], b[j : j + 1, :]
            out_ref[low + j : low + j + 1, :] = row_b * scale
            factor = jnp.where(row_index > j, column * (scale * scale), 0.0)
            for i in range(j + 1, 8):
                columns[i] = columns[i] - factor * column[i : i + 1, :]
            a = a - factor * row_a
            b = b - factor * row_b
        a, b = a[8:], b[8:]


def inverse_part(gram):
    vm = pl.BlockSpec(memory_space=pltpu.VMEM)
    return pl.pallas_call(
        inverse_kernel,
        out_shape=jax.ShapeDtypeStruct(gram.shape, F32),
        in_specs=[vm],
        out_specs=vm,
        compiler_params=params(),
        cost_estimate=pl.CostEstimate(flops=10**7, bytes_accessed=10**5, transcendentals=128),
    )(gram)


def last_kernel(merged_ref, left_ref, right_ref, inverse_ref, error_ref, basis_ref, back_ref):
    @pl.when(pl.program_id(0) == 0)
    def _():
        inverse = split(inverse_ref[...])
        basis = mm_split(split(right_ref[...]), inverse, ((1,), (1,)))
        basis_ref[...] = basis
        head, rest = split(mm_split(split(basis * 0.25), inverse, ((1,), (0,))))
        back_ref[0] = head
        back_ref[1] = rest

    out = mm_split(split(left_ref[...]), (back_ref[0], back_ref[1]), ((1,), (1,)))
    error_ref[...] = (merged_ref[...] - out).astype(BF16)


def last_part(merged, left, right, inverse, step=2048):
    width, cols = merged.shape
    rank = left.shape[1]
    whole = lambda i: (0, 0)
    return pl.pallas_call(
        last_kernel,
        out_shape=(
            jax.ShapeDtypeStruct((width, cols), BF16),
            jax.ShapeDtypeStruct((cols, rank), F32),
        ),
        grid=(width // step,),
        in_specs=[
            pl.BlockSpec((step, cols), lambda i: (i, 0)),
            pl.BlockSpec((step, rank), lambda i: (i, 0)),
            pl.BlockSpec((cols, rank), whole),
            pl.BlockSpec((rank, rank), whole),
        ],
        out_specs=(
            pl.BlockSpec((step, cols), lambda i: (i, 0)),
            pl.BlockSpec((cols, rank), whole),
        ),
        scratch_shapes=[pltpu.VMEM((2, cols, rank), BF16)],
        compiler_params=params(),
        cost_estimate=pl.CostEstimate(flops=10**9, bytes_accessed=8 * 10**6, transcendentals=0),
    )(merged, left, right, inverse)


PLANE = ("z", "y", "c")
ALL = ("x", "z", "y", "c")


def swap(value, axis, bit):
    n = lax.axis_size(axis)
    return lax.ppermute(value, axis, [(i, i ^ bit) for i in range(n)])


def per_device(features, preact, upstream, weight, pairs, station_weight, counts, error, basis):
    n_inter, n_z, n_y = lax.axis_size("x"), lax.axis_size("z"), lax.axis_size("y")
    group_rows, width = preact.shape[0], features.shape[1]
    rank, half = basis.shape[1], width // 2
    c = lax.axis_index("c")
    core = c.astype(jnp.int32)[None]

    all_features = lax.all_gather(features, PLANE, axis=0, tiled=True)
    own = counts.astype(F32)
    own = own + swap(own, "x", 1)
    other = swap(features, "c", 1)
    pair_features = jnp.where(
        c == 0, jnp.concatenate([features, other]), jnp.concatenate([other, features])
    )

    dpre, share = token_part(counts, pairs, station_weight, upstream, preact, basis)
    share = share + swap(share, "c", 1)

    own, error_late, share = lax.optimization_barrier((own, error, share))
    inv_mean = n_inter / (own + swap(own, "x", 2))
    halves = error_part(core, error_late, basis)
    halves_got = swap(halves[1], "c", 1)

    tokens = group_rows // (n_z * n_y)
    share = lax.all_to_all(share, ("z", "y"), 0, 0, tiled=True).reshape(-1, tokens, rank)
    part = left_part(core, inv_mean, share, pair_features, halves, halves_got)

    dpre_late, part = lax.optimization_barrier((dpre, part))
    rows = dpre_late.reshape(n_z, n_y, 2, 8, dpre.shape[1]).transpose(2, 1, 0, 3, 4)
    rows = rows.reshape(2, group_rows // 2, dpre.shape[1])
    give = lax.dynamic_index_in_dim(rows, 1 - c, 0, keepdims=False)
    keep = lax.dynamic_index_in_dim(rows, c, 0, keepdims=False)
    got = swap(mm(give, weight, ((1,), (1,))).astype(BF16), "c", 1)
    grad = (mm(keep, weight, ((1,), (1,))) + got.astype(F32)).astype(BF16)

    part = lax.all_to_all(part, ("x", "y"), 0, 0, tiled=True)
    part = part.reshape(n_inter * n_y, -1, rank).sum(0)

    grad, part = lax.optimization_barrier((grad, part))
    grad = lax.all_to_all(grad, "y", 0, 0, tiled=True)

    for bit in (1, 2, 4):
        part = part + swap(part, "z", bit)
    grad = grad.reshape(n_y, -1, width).astype(F32).sum(0).astype(BF16)

    grad, part = lax.optimization_barrier((grad, part))
    grad = lax.all_to_all(grad, "z", 0, 0, tiled=True)
    merged, head, rest = merge_part(inv_mean, all_features, dpre, error)
    mine = lax.all_to_all(
        jnp.broadcast_to(part[None], (n_inter * n_y,) + part.shape), ("x", "y"), 0, 0, tiled=True
    ).reshape(half, rank)
    merged, mine = lax.optimization_barrier((merged, mine))
    other = swap(mine, "c", 1)
    left = jnp.where(c == 0, jnp.concatenate([mine, other]), jnp.concatenate([other, mine]))

    right = right_part(head, rest, left)
    right_got = swap(right, "x", 1)
    mine, right = lax.optimization_barrier((mine, right))
    gram = jnp.dot(mine.T, mine, precision=HIGHEST)
    gram = gram + swap(gram, "c", 1)
    right = right + right_got
    gram, right = lax.optimization_barrier((gram, right))
    right = right + swap(right, "x", 2)
    inverse = inverse_part(gram)
    new_error, new_basis = last_part(merged, left, right, inverse)
    grad = grad.reshape(n_z, -1, width).astype(F32).sum(0).astype(BF16)
    return grad, new_error, new_basis


def solution(mesh):
    mesh = Mesh(mesh.devices.reshape(4, 8, 4, 2), ALL)
    in_specs = (
        P(ALL, None),
        P("x", PLANE),
        P("x", PLANE),
        P(None, PLANE),
        P("x", None),
        P(),
        P("x"),
        P("x", PLANE),
        P(PLANE, None),
    )
    out_specs = (P(ALL, None), P("x", PLANE), P(PLANE, None))
    return jax.shard_map(
        per_device, mesh=mesh, in_specs=in_specs, out_specs=out_specs, check_vma=False
    )
```

time: 210 us -> 181 us (0.86)
  other arithmetic: 46.6 us -> 9.65 us
  Pallas kernels: 0 us -> 24.2 us
  matrix products: 18.2 us -> 7.57 us
  waiting for transfers between devices: 49.8 us -> 57.6 us
  local copies, waits for them, and re-layouts: 24.1 us -> 16.8 us
  starting transfers between devices: 52.1 us -> 46.2 us
    pallas_call x0 -> x7, Pallas kernels: none -> 24.2 us  [the longest x1 8.1 us: merge_part(): pl.pallas_call(merge_kernel, out_shape=(jax.ShapeDtypeStruct((width, cols...]
    another operation x5 -> x0, other arithmetic: 23.7 us -> none  [the longest x3 13.2 us: per_device(): chol = jnp.linalg.cholesky(gram)]
    ppermute x18 -> x13, starting transfers between devices: 26.5 us -> 11.9 us  [swap(): return lax.ppermute(value, axis, [(i, i ^ bit) for i in range(n)])]
    add x9 -> x2, other arithmetic: 14.3 us -> 0.03 us  [the longest x1 0.02 us: per_device(): right = right + swap(right, 'x', 2)]
    all_to_all x2 -> x4, waiting for transfers between devices: 3.73 us -> 17.9 us  [the longest x1 5.25 us: per_device(): lax.all_to_all(share, ('z', 'y'), 0, 0, tiled=True)]
    ppermute x18 -> x13, waiting for transfers between devices: 33.7 us -> 21.8 us  [swap(): return lax.ppermute(value, axis, [(i, i ^ bit) for i in range(n)])]
    dot_general x7 -> x1, matrix products: 10.7 us -> 1.82 us  [per_device(): gram = jnp.dot(mine.T, mine, precision=HIGHEST)]
    all_to_all x2 -> x4, starting transfers between devices: 18.2 us -> 27 us  [the longest x1 11.7 us: per_device(): lax.all_to_all(share, ('z', 'y'), 0, 0, tiled=True)]
  transfers between devices with their start and end apart: 22 -> 19, of which waited for: 11 -> 12; matrix products, arithmetic and copies ran while one was open for 33% -> 11% of each run, Pallas kernels for 0% -> 11%
where the time goes in v2:
time: 181 us; the launch traced here: 178 us
  waiting for transfers between devices  57.6 us (32%)
  starting transfers between devices  46.2 us (26%)
  Pallas kernels  24.2 us (13%)
  local copies, waits for them, and re-layouts  16.8 us (9%)
  between operations  16.2 us (9%)
  other arithmetic  9.65 us (5%)
  matrix products  7.57 us (4%)
    ppermute x13, waiting for transfers between devices, swap(): return lax.ppermute(value, axis, [(i, i ^ bit) for i in range(n)])  21.8 us
    all_to_all x1, waiting for transfers between devices, per_device(): part = lax.all_to_all(part, ('x', 'y'), 0, 0, tiled=True)  17.2 us
    unnamed x38, local copies, waits for them, and re-layouts  14.6 us
    ppermute x13, starting transfers between devices, swap(): return lax.ppermute(value, axis, [(i, i ^ bit) for i in range(n)])  11.9 us
    all_to_all x1, starting transfers between devices, per_device(): lax.all_to_all(share, ('z', 'y'), 0, 0, tiled=True)  11.7 us
    pallas_call x1, Pallas kernels, merge_part(): pl.pallas_call(merge_kernel, out_shape=(jax.ShapeDtypeStruct((width, cols...  8.1 us
    all_to_all x1, starting transfers between devices, per_device(): part = lax.all_to_all(part, ('x', 'y'), 0, 0, tiled=True)  7.28 us
    all_to_all x1, starting transfers between devices, per_device(): grad = lax.all_to_all(grad, 'y', 0, 0, tiled=True)  5.87 us
  transfers between devices with their start and end apart: 19, of which 12 were waited for; matrix products, arithmetic and copies ran while one was open for 11% of the time, Pallas kernels for 11%

profile of v2, /device:TPU:8, one launch (start us, length us, event | category | flops | bytes accessed | tf_op | source)
XLA Modules:
  0.0 178.2 jit_solution(15626712193987988816)
XLA Ops:
  7.2 0.0 copy-start
  7.2 0.0 all-gather.2.cloned.1.call-start
  7.2 0.7 all-gather.2.cloned.1.call-update
  8.6 0.0 copy-start.9
  8.6 0.9 copy-done.9
  9.5 0.9 copy-done.11
  10.4 0.9 copy-done.12
  11.4 0.7 copy-done.16
  12.1 0.7 copy-done.17
  12.7 1.0 shard_map.112
  13.7 0.7 copy-done.13
  14.4 0.0 collective-permute-start.1
  14.4 2.8 %collective-permute-start = (f32[1]{0:T(128)}, f32[1]{0:T(128)}, u32[]{:S(2)}, u32[]{:S(2)}) collective-permute-start(f32[1]{0:T(128)} %convert_element_type.16), channel_id=1, source_target_pairs={{0,64},{64,0},{128,192},{192,128},{1,65},{65,1},{129,193},{193,129... | collective-permute-start | bytes 20 | tf_op jit(solution)/shard_map/ppermute | solution.py:299
  17.2 0.7 collective-permute-done
  18.6 0.7 add.39
  19.3 1.6 copy-done.8
  20.9 0.9 copy-done.10
  21.8 0.9 shard_map.113.keep_ref
  22.7 1.1 slice_bitcast_fusion
  23.8 1.3 copy-done.2
  25.1 0.5 collective-permute-start.3
  25.6 11.7 %all-to-all-start = ((f32[32,16,128]{2,1,0:T(8,128)}), f32[32,16,128]{2,1,0:T(8,128)S(1)}, u32[]{:S(2)}, u32[]{:S(2)}) async-start(f32[32,16,128]{2,1,0:T(8,128)} %bitcast.34), calls=%async_computation | async-start | bytes 524288 | tf_op jit(solution)/shard_map/all_to_all | solution.py:326
  37.4 1.0 maximum_select_fusion.1.feat_ref
  38.3 4.4 %collective-permute-start.2 = (f32[1]{0:T(128)}, f32[1]{0:T(128)}, u32[]{:S(2)}, u32[]{:S(2)}) collective-permute-start(f32[1]{0:T(128)} %add.38), channel_id=1, source_target_pairs={{0,128},{64,192},{128,0},{192,64},{1,129},{65,193},{129,1},{193,65... | collective-permute-start | bytes 20 | tf_op jit(solution)/shard_map/ppermute | solution.py:299
  42.7 0.8 collective-permute-done.2
  44.2 5.3 %all-to-all-done.share_ref = f32[32,16,128]{2,1,0:T(8,128)S(1)} async-done(((f32[32,16,128]{2,1,0:T(8,128)}), f32[32,16,128]{2,1,0:T(8,128)S(1)}, u32[]{:S(2)}, u32[]{:S(2)}) %all-to-all-start) | async-done | bytes 262176 | tf_op jit(solution)/shard_map/all_to_all | solution.py:326
  49.4 1.6 copy-done.3
  51.0 1.5 shard_map.114
  52.5 2.1 %convolution_convert_fusion = bf16[256,4096]{1,0:T(8,128)(2,1)} fusion(bf16[4096,256]{1,0:T(8,128)(2,1)S(1)} %copy-done, bf16[2,256,256]{2,1,0:T(8,128)(2,1)S(1)} %bitcast.35, s32[]{:T(128)S(6)} %select_n.26), kind=kOutput, calls=%fused_computation | convolution fusion | flops 537919488 | bytes 4325380 | tf_op jit(solution)/shard_map/dot_general | solution.py:26
  54.6 7.3 %all-to-all-start.1 = ((f32[16,128,128]{2,1,0:T(8,128)}), f32[16,128,128]{2,1,0:T(8,128)S(1)}, u32[]{:S(2)}, u32[]{:S(2)}) async-start(f32[16,128,128]{2,1,0:T(8,128)} %bitcast.11), calls=%async_computation.1 | async-start | bytes 2097152 | tf_op jit(solution)/shard_map/all_to_all | solution.py:337
  61.9 17.2 %all-to-all-done.1 = f32[16,128,128]{2,1,0:T(8,128)S(1)} async-done(((f32[16,128,128]{2,1,0:T(8,128)}), f32[16,128,128]{2,1,0:T(8,128)S(1)}, u32[]{:S(2)}, u32[]{:S(2)}) %all-to-all-start.1) | async-done | bytes 1048608 | tf_op jit(solution)/shard_map/all_to_all | solution.py:337
  79.0 0.1 reduce_sum.33
  79.1 3.7 %add_convert_fusion = bf16[256,4096]{1,0:T(8,128)(2,1)} fusion(bf16[256,4096]{1,0:T(8,128)(2,1)} %collective-permute-done.5, bf16[4096,256]{1,0:T(8,128)(2,1)S(1)} %copy-done, bf16[2,256,256]{2,1,0:T(8,128)(2,1)S(1)} %bitcast.36, s32[]{:T(128)S(6)} %select_n.25), kind=kOutput, calls=%fused_computation.1 | convolution fusion | flops 540016640 | bytes 6422532 | tf_op jit(solution)/shard_map/dot_general | solution.py:26
  82.8 5.9 %all-to-all-start.2 = ((bf16[4,64,4096]{2,1,0:T(8,128)(2,1)}), bf16[4,64,4096]{2,1,0:T(8,128)(2,1)}, u32[]{:S(2)}, u32[]{:S(2)}) async-start(bf16[4,64,4096]{2,1,0:T(8,128)(2,1)} %bitcast.32), calls=%async_computation.2 | async-start | bytes 4194304 | tf_op jit(solution)/shard_map/all_to_all | solution.py:341
  88.7 0.6 collective-permute-start.6
  89.3 4.0 %collective-permute-done.6 = f32[128,128]{1,0:T(8,128)S(1)} collective-permute-done((f32[128,128]{1,0:T(8,128)S(1)}, f32[128,128]{1,0:T(8,128)S(1)}, u32[]{:S(2)}, u32[]{:S(2)}) %collective-permute-start.6) | collective-permute-done | bytes 65568 | tf_op jit(solution)/shard_map/ppermute | solution.py:299
  93.3 1.0 collective-permute-start.7
  94.3 5.0 %collective-permute-done.7 = f32[128,128]{1,0:T(8,128)S(1)} collective-permute-done((f32[128,128]{1,0:T(8,128)S(1)}, f32[128,128]{1,0:T(8,128)S(1)}, u32[]{:S(2)}, u32[]{:S(2)}) %collective-permute-start.7) | collective-permute-done | bytes 65568 | tf_op jit(solution)/shard_map/ppermute | solution.py:299
  99.4 0.8 collective-permute-start.8
  100.2 7.7 %collective-permute-done.8 = f32[128,128]{1,0:T(8,128)S(1)} collective-permute-done((f32[128,128]{1,0:T(8,128)S(1)}, f32[128,128]{1,0:T(8,128)S(1)}, u32[]{:S(2)}, u32[]{:S(2)}) %collective-permute-start.8) | collective-permute-done | bytes 65568 | tf_op jit(solution)/shard_map/ppermute | solution.py:299
  107.9 4.9 %all-to-all-done.2 = bf16[4,64,4096]{2,1,0:T(8,128)(2,1)} async-done(((bf16[4,64,4096]{2,1,0:T(8,128)(2,1)}), bf16[4,64,4096]{2,1,0:T(8,128)(2,1)}, u32[]{:S(2)}, u32[]{:S(2)}) %all-to-all-start.2) | async-done | bytes 2097184 | tf_op jit(solution)/shard_map/all_to_all | solution.py:341
  112.8 2.8 %reduce_sum.34 = bf16[64,4096]{1,0:T(8,128)(2,1)} reduce(bf16[4,64,4096]{2,1,0:T(8,128)(2,1)} %all-to-all-done.2, bf16[]{:T(256)} %constant.23.clone.1), dimensions={0}, to_apply=%region_1.2 | reduce | flops 786432 | bytes 2621442 | tf_op jit(solution)/shard_map/reduce_sum | solution.py:345
  115.7 1.1 broadcast_in_dim.14
  116.7 5.1 %all-to-all-start.4 = ((f32[16,128,128]{2,1,0:T(8,128)}), f32[16,128,128]{2,1,0:T(8,128)S(1)}, u32[]{:S(2)}, u32[]{:S(2)}) async-start(f32[16,128,128]{2,1,0:T(8,128)} %broadcast_in_dim.14), calls=%async_computation.4 | async-start | bytes 2097152 | tf_op jit(solution)/shard_map/all_to_all | solution.py:350
  121.8 0.0 all-gather.2.cloned.1.call-done.feat_ref
  121.9 8.1 %shard_map.115 = (f32[4096,256]{1,0:T(8,128)}, bf16[256,4096]{1,0:T(8,128)(2,1)S(1)}, bf16[256,4096]{1,0:T(8,128)(2,1)S(1)}) custom-call(f32[1]{0:T(128)S(6)} %div.3.inv_ref, bf16[512,4096]{1,0:T(8,128)(2,1)} %all-gather.2.cloned.1.call-done.feat_ref, bf16[512,256]{1,0:T(8,128)(2,1)S(1)} %copy-done.15, bf16[4096,256]{1,0:T(8,128)(2,1)} %error_ref.2), custom_call_target="tpu_custom_call" | custom-call | flops 2000000000 | bytes 16000000 | tf_op jit(solution)/shard_map/pallas_call | solution.py:156
  130.0 1.4 copy-done.4
  131.3 1.3 copy-done.6
  132.7 3.9 %all-to-all-done.4 = f32[16,128,128]{2,1,0:T(8,128)S(1)} async-done(((f32[16,128,128]{2,1,0:T(8,128)}), f32[16,128,128]{2,1,0:T(8,128)S(1)}, u32[]{:S(2)}, u32[]{:S(2)}) %all-to-all-start.4) | async-done | bytes 1048608 | tf_op jit(solution)/shard_map/all_to_all | solution.py:350
  136.6 4.3 %all-to-all-start.3 = ((bf16[8,8,4096]{2,1,0:T(8,128)(2,1)}), bf16[8,8,4096]{2,1,0:T(8,128)(2,1)}, u32[]{:S(2)}, u32[]{:S(2)}) async-start(bf16[8,8,4096]{2,1,0:T(8,128)(2,1)} %bitcast.33), calls=%async_computation.3 | async-start | bytes 1048576 | tf_op jit(solution)/shard_map/all_to_all | solution.py:348
  141.0 3.2 %maximum_select_fusion.left_ref = f32[4096,128]{1,0:T(8,128)} fusion(f32[2048,128]{1,0:T(8,128)} %collective-permute-done.9, f32[2048,128]{1,0:T(8,128)S(1)} %bitcast.30, pred[]{:T(512)S(6)} %eq.4), kind=kLoop, calls=%fused_computation.2 | loop fusion | flops 1572864 | bytes 4194305 | tf_op jit(solution)/shard_map/jit(_where)/select_n | solution.py:355
  144.2 2.8 %shard_map.116 = f32[256,128]{1,0:T(8,128)S(1)} custom-call(bf16[256,4096]{1,0:T(8,128)(2,1)S(1)} %copy-done.5, bf16[256,4096]{1,0:T(8,128)(2,1)S(1)} %copy-done.7, f32[4096,128]{1,0:T(8,128)} %maximum_select_fusion.left_ref), custom_call_target="tpu_custom_call" | custom-call | flops 1000000000 | bytes 6000000 | tf_op jit(solution)/shard_map/pallas_call | solution.py:198
  147.0 0.2 collective-permute-start.11
  147.2 1.8 %fusion.9 = f32[128,128]{1,0:T(8,128)S(1)} fusion(f32[2048,128]{1,0:T(8,128)S(1)} %bitcast.31), kind=kOutput, calls=%fused_computation.12 | convolution fusion | flops 402653184 | bytes 1114112 | tf_op jit(solution)/shard_map/dot_general | solution.py:360
  149.0 0.5 collective-permute-start.10
  149.6 0.9 collective-permute-done.10
  150.5 2.6 %collective-permute-done.11 = f32[256,128]{1,0:T(8,128)S(1)} collective-permute-done((f32[256,128]{1,0:T(8,128)S(1)}, f32[256,128]{1,0:T(8,128)S(1)}, u32[]{:S(2)}, u32[]{:S(2)}) %collective-permute-start.11) | collective-permute-done | bytes 131104 | tf_op jit(solution)/shard_map/ppermute | solution.py:299
  153.0 1.1 collective-permute-start.12
  154.1 3.9 %all-to-all-done.3 = bf16[8,8,4096]{2,1,0:T(8,128)(2,1)} async-done(((bf16[8,8,4096]{2,1,0:T(8,128)(2,1)}), bf16[8,8,4096]{2,1,0:T(8,128)(2,1)}, u32[]{:S(2)}, u32[]{:S(2)}) %all-to-all-start.3) | async-done | bytes 524320 | tf_op jit(solution)/shard_map/all_to_all | solution.py:348
  158.0 1.8 reduce_sum.35
  159.7 5.0 %shard_map.117.inverse_ref = f32[128,128]{1,0:T(8,128)S(1)} custom-call(f32[128,128]{1,0:T(8,128)S(1)} %add.47.gram_ref), custom_call_target="tpu_custom_call" | custom-call | flops 10000000 | bytes 100000 | tf_op jit(solution)/shard_map/pallas_call | solution.py:242
  164.8 0.0 copy-start.1
  164.8 1.6 copy-done.1
  166.4 5.0 %shard_map.118 = (bf16[4096,256]{1,0:T(8,128)(2,1)}, f32[256,128]{1,0:T(8,128)}) custom-call(f32[4096,256]{1,0:T(8,128)} %get-tuple-element.37.merged_ref, f32[4096,128]{1,0:T(8,128)S(1)} %copy-done.1, f32[256,128]{1,0:T(8,128)S(1)} %add.49.right_ref, f32[128,128]{1,0:T(8,128)S(1)} %shard_map.117.inverse_ref), custom_call_target="tpu_custom_call" | custom-call | flops 1000000000 | bytes 8000000 | tf_op jit(solution)/shard_map/pallas_call | solution.py:270
  (38 shorter events, 0.2 us)
Async XLA Ops:
  7.2 45.4 %copy-start = (bf16[4096,256]{1,0:T(8,128)(2,1)S(1)}, bf16[4096,256]{1,0:T(8,128)(2,1)}, u32[]{:S(2)}) copy-start(bf16[4096,256]{1,0:T(8,128)(2,1)} %param.12) | copy-start | bytes 6291460
  7.2 114.7 %all-gather.2.cloned.1.call-start = ((), (), s32[]{:S(2)}) async-start(), calls=%async_computation.5 | async-start | bytes 4259840 | tf_op jit(solution)/shard_map/all_gather | solution.py:309
  8.6 0.9 copy-start.9
  9.5 0.9 copy-start.11
  10.4 0.9 copy-start.12
  11.4 0.7 copy-start.16
  12.1 0.7 copy-start.17
  13.7 0.7 copy-start.13
  14.4 4.2 %collective-permute-start.1 = (f32[512,128]{1,0:T(8,128)S(1)}, f32[512,128]{1,0:T(8,128)S(1)}, u32[]{:S(2)}, u32[]{:S(2)}) collective-permute-start(f32[512,128]{1,0:T(8,128)S(1)} %get-tuple-element.26), channel_id=1, source_target_pairs={{0,1},{1,0},{2,3},{3,2},{4,5},{5,4},{6,7},{7,6},{8,9},{9,8},{10,11... | collective-permute-start | bytes 786440 | tf_op jit(solution)/shard_map/ppermute | solution.py:299
  14.4 3.5 %collective-permute-start = (f32[1]{0:T(128)}, f32[1]{0:T(128)}, u32[]{:S(2)}, u32[]{:S(2)}) collective-permute-start(f32[1]{0:T(128)} %convert_element_type.16), channel_id=1, source_target_pairs={{0,64},{64,0},{128,192},{192,128},{1,65},{65,1},{129,193},{193,129... | collective-permute-start | bytes 20 | tf_op jit(solution)/shard_map/ppermute | solution.py:299
  19.3 1.6 copy-start.8
  20.9 0.9 copy-start.10
  21.8 3.3 %copy-start.18 = (bf16[8,4096]{1,0:T(8,128)(2,1)S(1)}, bf16[8,4096]{1,0:T(8,128)(2,1)}, u32[]{:S(2)}) copy-start(bf16[8,4096]{1,0:T(8,128)(2,1)} %param.9) | copy-start | bytes 196612
  23.8 1.3 copy-start.2
  25.1 24.3 %collective-permute-start.4 = (f32[2048,128]{1,0:T(8,128)}, f32[2048,128]{1,0:T(8,128)S(1)}, u32[]{:S(2)}, u32[]{:S(2)}) collective-permute-start(f32[2048,128]{1,0:T(8,128)} %slice_bitcast_fusion), channel_id=1, source_target_pairs={{0,1},{1,0},{2,3},{3,2},{4,5},{5,4},{6,7},{7,6},{8,9},{9,8},{10,11... | collective-permute-start | bytes 3145736 | tf_op jit(solution)/shard_map/ppermute | solution.py:299
  25.1 12.2 %collective-permute-start.3 = (bf16[8,4096]{1,0:T(8,128)(2,1)S(1)}, bf16[8,4096]{1,0:T(8,128)(2,1)}, u32[]{:S(2)}, u32[]{:S(2)}) collective-permute-start(bf16[8,4096]{1,0:T(8,128)(2,1)S(1)} %copy-done.18), channel_id=1, source_target_pairs={{0,1},{1,0},{2,3},{3,2},{4,5},{5,4},{6,7},{7,6},{8,9},{9,8},{10,11... | collective-permute-start | bytes 196616 | tf_op jit(solution)/shard_map/ppermute | solution.py:299
  25.6 23.8 %all-to-all-start = ((f32[32,16,128]{2,1,0:T(8,128)}), f32[32,16,128]{2,1,0:T(8,128)S(1)}, u32[]{:S(2)}, u32[]{:S(2)}) async-start(f32[32,16,128]{2,1,0:T(8,128)} %bitcast.34), calls=%async_computation | async-start | bytes 524288 | tf_op jit(solution)/shard_map/all_to_all | solution.py:326
  38.3 5.2 %collective-permute-start.2 = (f32[1]{0:T(128)}, f32[1]{0:T(128)}, u32[]{:S(2)}, u32[]{:S(2)}) collective-permute-start(f32[1]{0:T(128)} %add.38), channel_id=1, source_target_pairs={{0,128},{64,192},{128,0},{192,64},{1,129},{65,193},{129,1},{193,65... | collective-permute-start | bytes 20 | tf_op jit(solution)/shard_map/ppermute | solution.py:299
  49.4 1.6 copy-start.3
  51.0 1.5 copy-start.14
  54.6 24.5 %collective-permute-start.5 = (bf16[256,4096]{1,0:T(8,128)(2,1)}, bf16[256,4096]{1,0:T(8,128)(2,1)}, u32[]{:S(2)}, u32[]{:S(2)}) collective-permute-start(bf16[256,4096]{1,0:T(8,128)(2,1)} %convolution_convert_fusion), channel_id=1, source_target_pairs={{0,1},{1,0},{2,3},{3,2},{4,5},{5,4},{6,7},{7,6},{8,9},{9,8},{10,11... | collective-permute-start | bytes 6291464 | tf_op jit(solution)/shard_map/ppermute | solution.py:299
  54.6 24.4 %all-to-all-start.1 = ((f32[16,128,128]{2,1,0:T(8,128)}), f32[16,128,128]{2,1,0:T(8,128)S(1)}, u32[]{:S(2)}, u32[]{:S(2)}) async-start(f32[16,128,128]{2,1,0:T(8,128)} %bitcast.11), calls=%async_computation.1 | async-start | bytes 2097152 | tf_op jit(solution)/shard_map/all_to_all | solution.py:337
  82.8 30.0 %all-to-all-start.2 = ((bf16[4,64,4096]{2,1,0:T(8,128)(2,1)}), bf16[4,64,4096]{2,1,0:T(8,128)(2,1)}, u32[]{:S(2)}, u32[]{:S(2)}) async-start(bf16[4,64,4096]{2,1,0:T(8,128)(2,1)} %bitcast.32), calls=%async_computation.2 | async-start | bytes 4194304 | tf_op jit(solution)/shard_map/all_to_all | solution.py:341
  88.7 4.6 %collective-permute-start.6 = (f32[128,128]{1,0:T(8,128)S(1)}, f32[128,128]{1,0:T(8,128)S(1)}, u32[]{:S(2)}, u32[]{:S(2)}) collective-permute-start(f32[128,128]{1,0:T(8,128)S(1)} %reduce_sum.33), channel_id=1, source_target_pairs={{0,8},{8,0},{16,24},{24,16},{32,40},{40,32},{48,56},{56,48},{1,9},... | collective-permute-start | bytes 196616 | tf_op jit(solution)/shard_map/ppermute | solution.py:299
  93.3 6.1 %collective-permute-start.7 = (f32[128,128]{1,0:T(8,128)S(1)}, f32[128,128]{1,0:T(8,128)S(1)}, u32[]{:S(2)}, u32[]{:S(2)}) collective-permute-start(f32[128,128]{1,0:T(8,128)S(1)} %add.44), channel_id=1, source_target_pairs={{0,16},{8,24},{16,0},{24,8},{32,48},{40,56},{48,32},{56,40},{1,17}... | collective-permute-start | bytes 196616 | tf_op jit(solution)/shard_map/ppermute | solution.py:299
  99.4 8.5 %collective-permute-start.8 = (f32[128,128]{1,0:T(8,128)S(1)}, f32[128,128]{1,0:T(8,128)S(1)}, u32[]{:S(2)}, u32[]{:S(2)}) collective-permute-start(f32[128,128]{1,0:T(8,128)S(1)} %add.45), channel_id=1, source_target_pairs={{0,32},{8,40},{16,48},{24,56},{32,0},{40,8},{48,16},{56,24},{1,33}... | collective-permute-start | bytes 196616 | tf_op jit(solution)/shard_map/ppermute | solution.py:299
  115.7 6.2 %copy-start.15 = (bf16[512,256]{1,0:T(8,128)(2,1)S(1)}, bf16[512,256]{1,0:T(8,128)(2,1)}, u32[]{:S(2)}) copy-start(bf16[512,256]{1,0:T(8,128)(2,1)} %copy-done.13) | copy-start | bytes 786436
  116.7 19.9 %all-to-all-start.4 = ((f32[16,128,128]{2,1,0:T(8,128)}), f32[16,128,128]{2,1,0:T(8,128)S(1)}, u32[]{:S(2)}, u32[]{:S(2)}) async-start(f32[16,128,128]{2,1,0:T(8,128)} %broadcast_in_dim.14), calls=%async_computation.4 | async-start | bytes 2097152 | tf_op jit(solution)/shard_map/all_to_all | solution.py:350
  130.0 1.4 copy-start.4
  131.3 1.3 copy-start.6
  136.6 4.4 %collective-permute-start.9 = (f32[2048,128]{1,0:T(8,128)S(1)}, f32[2048,128]{1,0:T(8,128)}, u32[]{:S(2)}, u32[]{:S(2)}) collective-permute-start(f32[2048,128]{1,0:T(8,128)S(1)} %bitcast.29), channel_id=1, source_target_pairs={{0,1},{1,0},{2,3},{3,2},{4,5},{5,4},{6,7},{7,6},{8,9},{9,8},{10,11... | collective-permute-start | bytes 3145736 | tf_op jit(solution)/shard_map/ppermute | solution.py:299
  136.6 21.4 %all-to-all-start.3 = ((bf16[8,8,4096]{2,1,0:T(8,128)(2,1)}), bf16[8,8,4096]{2,1,0:T(8,128)(2,1)}, u32[]{:S(2)}, u32[]{:S(2)}) async-start(bf16[8,8,4096]{2,1,0:T(8,128)(2,1)} %bitcast.33), calls=%async_computation.3 | async-start | bytes 1048576 | tf_op jit(solution)/shard_map/all_to_all | solution.py:348
  140.9 3.3 %copy-start.5 = (bf16[256,4096]{1,0:T(8,128)(2,1)S(1)}, bf16[256,4096]{1,0:T(8,128)(2,1)}, u32[]{:S(2)}) copy-start(bf16[256,4096]{1,0:T(8,128)(2,1)} %copy-done.4) | copy-start | bytes 6291460
  140.9 3.3 %copy-start.7 = (bf16[256,4096]{1,0:T(8,128)(2,1)S(1)}, bf16[256,4096]{1,0:T(8,128)(2,1)}, u32[]{:S(2)}) copy-start(bf16[256,4096]{1,0:T(8,128)(2,1)} %copy-done.6) | copy-start | bytes 6291460
  147.0 6.0 %collective-permute-start.11 = (f32[256,128]{1,0:T(8,128)S(1)}, f32[256,128]{1,0:T(8,128)S(1)}, u32[]{:S(2)}, u32[]{:S(2)}) collective-permute-start(f32[256,128]{1,0:T(8,128)S(1)} %shard_map.116), channel_id=1, source_target_pairs={{0,64},{64,0},{128,192},{192,128},{1,65},{65,1},{129,193},{193,129... | collective-permute-start | bytes 393224 | tf_op jit(solution)/shard_map/ppermute | solution.py:299
  149.0 1.4 collective-permute-start.10
  153.0 11.7 %collective-permute-start.12 = (f32[256,128]{1,0:T(8,128)S(1)}, f32[256,128]{1,0:T(8,128)S(1)}, u32[]{:S(2)}, u32[]{:S(2)}) collective-permute-start(f32[256,128]{1,0:T(8,128)S(1)} %add.48), channel_id=1, source_target_pairs={{0,128},{64,192},{128,0},{192,64},{1,129},{65,193},{129,1},{193,65... | collective-permute-start | bytes 393224 | tf_op jit(solution)/shard_map/ppermute | solution.py:299
  164.8 1.6 copy-start.1
Sparse Core Ops, SparseCore 0:
  10.8 86.9 all-gather.1

commit v3 on v2

v3 whole, which is shorter than its diff:
```python
import functools, math
import jax
import jax.numpy as jnp
from jax import lax
from jax.experimental import pallas as pl
from jax.experimental.pallas import tpu as pltpu
from jax.sharding import Mesh, PartitionSpec as P

F32 = jnp.float32
BF16 = jnp.bfloat16
HIGHEST = lax.Precision.HIGHEST
VMEM = 56 * 1024 * 1024


def gelu_slope(value):
    cdf = 0.5 * (1.0 + lax.erf(value / math.sqrt(2.0)))
    return cdf + value * jnp.exp(-0.5 * value * value) / math.sqrt(2.0 * math.pi)


def split(value):
    head = value.astype(BF16)
    return head, (value - head.astype(F32)).astype(BF16)


def mm(a, b, contract):
    return lax.dot_general(a, b, (contract, ((), ())), preferred_element_type=F32)


def mm_wide(a, wide, contract):
    head, rest = split(wide)
    out = mm(a, jnp.concatenate([head, rest], axis=1), contract)
    n = wide.shape[1]
    return out[:, :n] + out[:, n:]


def mm_split(a, b, contract):
    return mm(a[0], b[0], contract) + (mm(a[0], b[1], contract) + mm(a[1], b[0], contract))


def params(limit=VMEM):
    return pltpu.CompilerParams(vmem_limit_bytes=limit)


def token_kernel(count_ref, pairs_ref, table_ref, up_ref, pre_ref, basis_ref, dpre_ref, share_ref):
    rows = up_ref.shape[0]
    stations = table_ref.shape[1]
    table = table_ref[...]
    head = table.astype(BF16)
    middle = (table - head.astype(F32)).astype(BF16)
    last = (table - head.astype(F32) - middle.astype(F32)).astype(BF16)
    which = lax.broadcasted_iota(jnp.int32, (stations, rows), 0)
    weight = None
    for end in range(2):
        onehot = (which == pairs_ref[end : end + 1, :]).astype(F32).astype(BF16)
        found = None
        for piece in (last, middle, head):
            term = mm(jnp.broadcast_to(piece, (16, stations)), onehot, ((1,), (0,)))[:1]
            found = term if found is None else found + term
        weight = found if weight is None else weight * found
    live = lax.broadcasted_iota(jnp.int32, (1, rows), 1) < count_ref[0]
    weight = jnp.where(live, weight, 0.0)
    column = jnp.transpose(jnp.broadcast_to(weight, (128, rows)))
    column = jnp.concatenate([column] * (up_ref.shape[1] // 128), axis=1)
    dpre = (up_ref[...].astype(F32) * gelu_slope(pre_ref[...].astype(F32)) * column).astype(BF16)
    dpre_ref[...] = dpre
    share_ref[...] = mm_wide(dpre, basis_ref[...], ((1,), (0,)))


def token_part(counts, pairs, table, upstream, preact, basis):
    vm = pl.BlockSpec(memory_space=pltpu.VMEM)
    return pl.pallas_call(
        token_kernel,
        out_shape=(
            jax.ShapeDtypeStruct(upstream.shape, BF16),
            jax.ShapeDtypeStruct((upstream.shape[0], basis.shape[1]), F32),
        ),
        in_specs=[pl.BlockSpec(memory_space=pltpu.SMEM)] + [vm] * 5,
        out_specs=(vm, vm),
        compiler_params=params(),
        cost_estimate=pl.CostEstimate(flops=10**5, bytes_accessed=10**4, transcendentals=0),
    )(counts, pairs.T, table[None], upstream, preact, basis)


def err_kernel(core_ref, error_ref, basis_ref, give_ref, keep_ref):
    product = mm_wide(error_ref[...], basis_ref[...], ((1,), (0,)))

    @pl.when(pl.program_id(0) == 0)
    def _():
        give_ref[...] = product

    @pl.when(pl.program_id(0) == 1)
    def _():
        keep_ref[...] = product


def error_part(core, error, basis):
    rows, cols = error.shape
    rank, half = basis.shape[1], rows // 2
    whole = lambda h, core: (0, 0)
    return pl.pallas_call(
        err_kernel,
        out_shape=(jax.ShapeDtypeStruct((half, rank), F32),) * 2,
        grid_spec=pltpu.PrefetchScalarGridSpec(
            num_scalar_prefetch=1,
            grid=(2,),
            in_specs=[
                pl.BlockSpec((half, cols), lambda h, core: ((core[0] + 1 + h) % 2, 0)),
                pl.BlockSpec((cols, rank), whole),
            ],
            out_specs=(pl.BlockSpec((half, rank), whole),) * 2,
        ),
        compiler_params=params(),
        cost_estimate=pl.CostEstimate(flops=10**5, bytes_accessed=10**4, transcendentals=0),
    )(core, error, basis)


def left_kernel(inv_ref, share_ref, feat_ref, keep_ref, got_ref, out_ref):
    share = share_ref[0]
    for i in range(1, share_ref.shape[0]):
        share = share + share_ref[i]
    out_ref[...] = (
        keep_ref[...]
        + got_ref[...]
        + mm_wide(feat_ref[...], share * inv_ref[0], ((0,), (0,)))
    )


def left_part(inv_mean, share, feats, keep, got):
    blocks, tokens, rank = share.shape
    half = got.shape[0]
    step = half // 2
    rows = pl.BlockSpec((step, rank), lambda i: (i, 0))
    return pl.pallas_call(
        left_kernel,
        out_shape=jax.ShapeDtypeStruct((half, rank), F32),
        grid=(half // step,),
        in_specs=[
            pl.BlockSpec(memory_space=pltpu.SMEM),
            pl.BlockSpec((blocks, tokens, rank), lambda i: (0, 0, 0)),
            pl.BlockSpec((tokens, step), lambda i: (0, i)),
            rows,
            rows,
        ],
        out_specs=rows,
        compiler_params=params(),
        cost_estimate=pl.CostEstimate(flops=10**8, bytes_accessed=4 * 10**6, transcendentals=0),
    )(inv_mean, share, feats, keep, got)


def merge_kernel(inv_ref, feat_ref, dpre_ref, error_ref, merged_ref, head_ref, rest_ref):
    raw = mm(feat_ref[...], dpre_ref[...], ((0,), (0,)))
    merged = raw * inv_ref[0] + error_ref[...].astype(F32)
    merged_ref[...] = merged
    head, rest = split(jnp.transpose(merged))
    head_ref[...] = head
    rest_ref[...] = rest


def merge_part(inv_mean, features, dpre, error):
    tokens, width = features.shape
    cols = dpre.shape[1]
    step = 512
    return pl.pallas_call(
        merge_kernel,
        out_shape=(
            jax.ShapeDtypeStruct((width, cols), F32),
            jax.ShapeDtypeStruct((cols, width), BF16),
            jax.ShapeDtypeStruct((cols, width), BF16),
        ),
        grid=(width // step,),
        in_specs=[
            pl.BlockSpec(memory_space=pltpu.SMEM),
            pl.BlockSpec((tokens, step), lambda i: (0, i)),
            pl.BlockSpec((tokens, cols), lambda i: (0, 0)),
            pl.BlockSpec((step, cols), lambda i: (i, 0)),
        ],
        out_specs=(
            pl.BlockSpec((step, cols), lambda i: (i, 0)),
            pl.BlockSpec((cols, step), lambda i: (0, i)),
            pl.BlockSpec((cols, step), lambda i: (0, i)),
        ),
        compiler_params=params(),
        cost_estimate=pl.CostEstimate(flops=2 * 10**9, bytes_accessed=16 * 10**6, transcendentals=0),
    )(inv_mean, features, dpre, error)


def right_kernel(core_ref, head_ref, rest_ref, own_ref, other_ref, right_ref):
    def term(left):
        lh, ll = split(left)
        rank = lh.shape[1]
        both = mm(head_ref[...], jnp.concatenate([lh, ll], axis=1), ((1,), (0,)))
        return both[:, :rank] + both[:, rank:] + mm(rest_ref[...], lh, ((1,), (0,)))

    @pl.when(pl.program_id(0) == 0)
    def _():
        right_ref[...] = term(own_ref[...])

    @pl.when(pl.program_id(0) == 1)
    def _():
        right_ref[...] += term(other_ref[...])


def right_part(core, head, rest, own, other):
    cols, width = head.shape
    half, rank = own.shape
    whole = lambda h, core: (0, 0)
    column = pl.BlockSpec((cols, half), lambda h, core: (0, (core[0] + h) % 2))
    return pl.pallas_call(
        right_kernel,
        out_shape=jax.ShapeDtypeStruct((cols, rank), F32),
        grid_spec=pltpu.PrefetchScalarGridSpec(
            num_scalar_prefetch=1,
            grid=(2,),
            in_specs=[column, column] + [pl.BlockSpec((half, rank), whole)] * 2,
            out_specs=pl.BlockSpec((cols, rank), whole),
        ),
        compiler_params=params(),
        cost_estimate=pl.CostEstimate(flops=10**9, bytes_accessed=6 * 10**6, transcendentals=0),
    )(core, head, rest, own, other)


def inverse_kernel(gram_ref, out_ref):
    n = gram_ref.shape[0]
    a = gram_ref[...]
    b = (
        lax.broadcasted_iota(jnp.int32, (n, n), 0) == lax.broadcasted_iota(jnp.int32, (n, n), 1)
    ).astype(F32)
    for low in range(0, n, 8):
        left = n - low
        row_index = lax.broadcasted_iota(jnp.int32, (left, n), 0)
        columns = [
            jnp.broadcast_to(a[:, low + j : low + j + 1], (left, n)) for j in range(8)
        ]
        for j in range(8):
            column = columns[j]
            pivot = column[j : j + 1, :]
            scale = lax.rsqrt(pivot)
            scale = scale * (1.5 - 0.5 * pivot * scale * scale)
            row_a, row_b = a[j : j + 1, :], b[j : j + 1, :]
            out_ref[low + j : low + j + 1, :] = row_b * scale
            factor = jnp.where(row_index > j, column * (scale * scale), 0.0)
            for i in range(j + 1, 8):
                columns[i] = columns[i] - factor * column[i : i + 1, :]
            a = a - factor * row_a
            b = b - factor * row_b
        a, b = a[8:], b[8:]


def inverse_part(gram):
    vm = pl.BlockSpec(memory_space=pltpu.VMEM)
    return pl.pallas_call(
        inverse_kernel,
        out_shape=jax.ShapeDtypeStruct(gram.shape, F32),
        in_specs=[vm],
        out_specs=vm,
        compiler_params=params(VMEM // 8),
        cost_estimate=pl.CostEstimate(flops=10**7, bytes_accessed=10**5, transcendentals=128),
    )(gram)


def last_kernel(core_ref, merged_ref, own_ref, other_ref, right_ref, inverse_ref, error_ref, basis_ref, back_ref):
    def fill(left):
        out = mm_split(split(left), (back_ref[0], back_ref[1]), ((1,), (1,)))
        error_ref[...] = (merged_ref[...] - out).astype(BF16)

    @pl.when(pl.program_id(0) == 0)
    def _():
        inverse = split(inverse_ref[...])
        basis = mm_split(split(right_ref[...]), inverse, ((1,), (1,)))
        basis_ref[...] = basis
        head, rest = split(mm_split(split(basis * 0.25), inverse, ((1,), (0,))))
        back_ref[0] = head
        back_ref[1] = rest
        fill(own_ref[...])

    pl.when(pl.program_id(0) == 1)(lambda: fill(other_ref[...]))


def last_part(core, merged, own, other, right, inverse):
    width, cols = merged.shape
    half, rank = own.shape
    whole = lambda h, core: (0, 0)
    row = pl.BlockSpec((half, cols), lambda h, core: ((core[0] + h) % 2, 0))
    return pl.pallas_call(
        last_kernel,
        out_shape=(
            jax.ShapeDtypeStruct((width, cols), BF16),
            jax.ShapeDtypeStruct((cols, rank), F32),
        ),
        grid_spec=pltpu.PrefetchScalarGridSpec(
            num_scalar_prefetch=1,
            grid=(2,),
            in_specs=[
                row,
                pl.BlockSpec((half, rank), whole),
                pl.BlockSpec((half, rank), whole),
                pl.BlockSpec((cols, rank), whole),
                pl.BlockSpec((rank, rank), whole),
            ],
            out_specs=(row, pl.BlockSpec((cols, rank), whole)),
            scratch_shapes=[pltpu.VMEM((2, cols, rank), BF16)],
        ),
        compiler_params=params(),
        cost_estimate=pl.CostEstimate(flops=10**9, bytes_accessed=8 * 10**6, transcendentals=0),
    )(core, merged, own, other, right, inverse)


PLANE = ("z", "y", "c")
ALL = ("x", "z", "y", "c")


def swap(value, axis, bit):
    n = lax.axis_size(axis)
    return lax.ppermute(value, axis, [(i, i ^ bit) for i in range(n)])


def shift(value, axis, by):
    n = lax.axis_size(axis)
    return lax.ppermute(value, axis, [(i, (i + by) % n) for i in range(n)])


def pick(value, index):
    return lax.dynamic_index_in_dim(value, index, 0, keepdims=False)


def per_device(features, preact, upstream, weight, pairs, station_weight, counts, error, basis):
    tie = lax.optimization_barrier
    n_inter, n_z, n_y = lax.axis_size("x"), lax.axis_size("z"), lax.axis_size("y")
    group_rows, width = preact.shape[0], features.shape[1]
    rank, half = basis.shape[1], width // 2
    cols = preact.shape[1]
    c, y = lax.axis_index("c"), lax.axis_index("y")
    core = c.astype(jnp.int32)[None]

    all_features = lax.all_gather(features, PLANE, axis=0, tiled=True)
    give = lax.dynamic_slice_in_dim(features, (1 - c) * half, half, 1)
    keep = lax.dynamic_slice_in_dim(features, c * half, half, 1)
    got = swap(give, "c", 1)
    pair = jnp.where(c == 0, jnp.concatenate([keep, got]), jnp.concatenate([got, keep]))
    count = counts.astype(F32)
    count = count + swap(count, "x", 1)

    dpre, share = token_part(counts, pairs, station_weight, upstream, preact, basis)
    share = share + swap(share, "c", 1)
    count, share, error_late, late = tie((count, share, error, dpre))
    inv_mean = n_inter / (count + swap(count, "x", 2))
    err_give, err_keep = error_part(core, error_late, basis)
    err_got = swap(err_give, "c", 1)

    rows = late.reshape(n_z, n_y, 2, 8, cols).transpose(2, 1, 0, 3, 4).reshape(2, -1, cols)
    got = swap(mm(pick(rows, 1 - c), weight, ((1,), (1,))).astype(BF16), "c", 1)
    share = lax.all_to_all(share, ("z", "y"), 0, 0, tiled=True).reshape(n_z * n_y, -1, rank)
    grad = (mm(pick(rows, c), weight, ((1,), (1,))) + got.astype(F32)).astype(BF16)
    grad = grad.reshape(n_y, -1, width)
    piece = grad.shape[1] // 2
    far = pick(grad, (y + 2) % n_y)
    far_up, far_down = far[:piece], far[piece:]
    inv_mean, share, err_got, pair, grad, far_up, far_down = tie(
        (inv_mean, share, err_got, pair, grad, far_up, far_down)
    )
    part = left_part(inv_mean, share, pair, err_keep, err_got)

    up, down = shift(far_up, "y", 1), shift(far_down, "y", -1)
    after, before = pick(grad, (y + 1) % n_y), pick(grad, (y + 3) % n_y)
    after = jnp.concatenate([after[:piece] + up, after[piece:]])
    before = jnp.concatenate([before[:piece], before[piece:] + down])
    part = lax.all_to_all(part, ("x", "y"), 0, 0, tiled=True)
    after, before, part = tie((after, before, part))

    up, down = shift(after, "y", 1), shift(before, "y", -1)
    part = part.reshape(n_inter * n_y, -1, rank).sum(0)
    for bit in (1, 2, 4):
        part = part + swap(part, "z", bit)
    up, down, part = tie((up, down, part))

    mine = lax.all_to_all(
        jnp.broadcast_to(part[None], (n_inter * n_y,) + part.shape), ("x", "y"), 0, 0, tiled=True
    ).reshape(half, rank)
    merged, head, rest = merge_part(inv_mean, all_features, dpre, error)
    grad = pick(grad, y).astype(F32) + up.astype(F32) + down.astype(F32)
    grad = grad.astype(BF16)
    grad, merged, mine = tie((grad, merged, mine))

    other = swap(mine, "c", 1)
    gram = jnp.dot(mine.T, mine, precision=HIGHEST)
    gram, other = tie((gram, other))
    gram = gram + swap(gram, "c", 1)
    right = right_part(core, head, rest, mine, other)
    gram, grad, right = tie((gram, grad, right))
    right = right + swap(right, "x", 1)
    grad = lax.all_to_all(grad, "z", 0, 0, tiled=True)
    gram, right = tie((gram, right))
    inverse = inverse_part(gram)
    right = right + swap(right, "x", 2)
    new_error, new_basis = last_part(core, merged, mine, other, right, inverse)
    grad, new_basis = tie((grad, new_basis))
    grad = grad.reshape(n_z, -1, width).astype(F32).sum(0).astype(BF16)
    return grad, new_error, new_basis


def solution(mesh):
    mesh = Mesh(mesh.devices.reshape(4, 8, 4, 2), ALL)
    in_specs = (
        P(ALL, None),
        P("x", PLANE),
        P("x", PLANE),
        P(None, PLANE),
        P("x", None),
        P(),
        P("x"),
        P("x", PLANE),
        P(PLANE, None),
    )
    out_specs = (P(ALL, None), P("x", PLANE), P(PLANE, None))
    return jax.shard_map(
        per_device, mesh=mesh, in_specs=in_specs, out_specs=out_specs, check_vma=False
    )
```

time: 181 us -> 164 us (0.906)
  waiting for transfers between devices: 57.6 us -> 43.3 us
  local copies, waits for them, and re-layouts: 16.8 us -> 6.65 us
  Pallas kernels: 24.2 us -> 33.9 us
    unnamed x38 -> x14, local copies, waits for them, and re-layouts: 14.6 us -> 2.81 us
    all_to_all x1, waiting for transfers between devices: 17.2 us -> 10.4 us  [per_device(): part = lax.all_to_all(part, ('x', 'y'), 0, 0, tiled=True)]
    all_to_all x1 -> x0, starting transfers between devices: 5.87 us -> none  [per_device(): grad = lax.all_to_all(grad, 'y', 0, 0, tiled=True)]
    all_to_all x1 -> x0, waiting for transfers between devices: 4.9 us -> none  [per_device(): grad = lax.all_to_all(grad, 'y', 0, 0, tiled=True)]
    ppermute x0 -> x4, starting transfers between devices: none -> 4.51 us  [shift(): return lax.ppermute(value, axis, [(i, (i + by) % n) for i in range(n)])]
    ppermute x13, waiting for transfers between devices: 21.8 us -> 25.8 us  [swap(): return lax.ppermute(value, axis, [(i, i ^ bit) for i in range(n)])]
    all_to_all x1, waiting for transfers between devices: 3.93 us -> 0.01 us  [per_device(): lax.all_to_all(jnp.broadcast_to(part[None], (n_inter * n_y,) + part.shape...]
    all_to_all x1, waiting for transfers between devices: 3.86 us -> 0.01 us  [per_device(): grad = lax.all_to_all(grad, 'z', 0, 0, tiled=True)]
  transfers between devices with their start and end apart: 19 -> 22, of which waited for: 12 -> 8; matrix products, arithmetic and copies ran while one was open for 11% -> 12% of each run, Pallas kernels for 11% -> 21%
where the time goes in v3:
time: 164 us; the launch traced here: 163 us
  starting transfers between devices  47 us (29%)
  waiting for transfers between devices  43.3 us (26%)
  Pallas kernels  33.9 us (21%)
  between operations  16.2 us (10%)
  other arithmetic  9.45 us (6%)
  local copies, waits for them, and re-layouts  6.65 us (4%)
  matrix products  6.24 us (4%)
    ppermute x13, waiting for transfers between devices, swap(): return lax.ppermute(value, axis, [(i, i ^ bit) for i in range(n)])  25.8 us
    ppermute x13, starting transfers between devices, swap(): return lax.ppermute(value, axis, [(i, i ^ bit) for i in range(n)])  15 us
    all_to_all x1, starting transfers between devices, per_device(): lax.all_to_all(share, ('z', 'y'), 0, 0, tiled=True)  11.7 us
    all_to_all x1, waiting for transfers between devices, per_device(): part = lax.all_to_all(part, ('x', 'y'), 0, 0, tiled=True)  10.4 us
    pallas_call x1, Pallas kernels, merge_part(): pl.pallas_call(merge_kernel, out_shape=(jax.ShapeDtypeStruct((width, cols...  9.66 us
    all_to_all x1, waiting for transfers between devices, per_device(): lax.all_to_all(share, ('z', 'y'), 0, 0, tiled=True)  6.48 us
    all_to_all x1, starting transfers between devices, per_device(): part = lax.all_to_all(part, ('x', 'y'), 0, 0, tiled=True)  6.13 us
    all_to_all x1, starting transfers between devices, per_device(): lax.all_to_all(jnp.broadcast_to(part[None], (n_inter * n_y,) + part.shape...  6.07 us
  transfers between devices with their start and end apart: 22, of which 8 were waited for; matrix products, arithmetic and copies ran while one was open for 12% of the time, Pallas kernels for 21%

profile of v3, /device:TPU:8, one launch (start us, length us, event | category | flops | bytes accessed | tf_op | source)
XLA Modules:
  0.0 162.8 jit_solution(2129174182010940002)
XLA Ops:
  7.2 0.0 copy-start
  7.2 0.0 all-gather.2.cloned.1.call-start
  7.2 0.7 all-gather.2.cloned.1.call-update
  8.6 2.8 %shard_map.112 = (bf16[512,256]{1,0:T(8,128)(2,1)}, f32[512,128]{1,0:T(8,128)}) custom-call(s32[1]{0:T(128)S(6)} %copy.13.count_ref, s32[2,512]{1,0:T(2,128)} %bitcast.62, f32[1,512]{1,0:T(1,128)} %bitcast.63, bf16[512,256]{1,0:T(8,128)(2,1)} %up_ref.1, bf16[512,256]{1,0:T(8,128)(2,1)} %pre_ref.1, f32[256,128]{1,0:T(8,128)} %basis_ref.3), custom_call_target="tpu_custom_call" | custom-call | flops 100000 | bytes 10000 | tf_op jit(solution)/shard_map/pallas_call | solution.py:71
  11.3 0.0 collective-permute-start.1
  11.3 2.8 %collective-permute-start = (f32[1]{0:T(128)}, f32[1]{0:T(128)}, u32[]{:S(2)}, u32[]{:S(2)}) collective-permute-start(f32[1]{0:T(128)} %convert_element_type.29), channel_id=1, source_target_pairs={{0,64},{64,0},{128,192},{192,128},{1,65},{65,1},{129,193},{193,129... | collective-permute-start | bytes 20 | tf_op jit(solution)/shard_map/ppermute | solution.py:314
  14.1 0.7 collective-permute-done
  15.5 1.7 %add.89 = f32[512,128]{1,0:T(8,128)} add(f32[512,128]{1,0:T(8,128)} %get-tuple-element.41, f32[512,128]{1,0:T(8,128)S(1)} %collective-permute-done.1) | non-fusion elementwise | flops 65536 | bytes 786432 | tf_op jit(solution)/shard_map/add | solution.py:344
  17.2 1.0 copy.12
  18.1 0.0 copy-start.6
  18.1 2.1 %convolution_convert_fusion = bf16[256,4096]{1,0:T(8,128)(2,1)} fusion(bf16[4096,256]{1,0:T(8,128)(2,1)S(1)} %copy-done, bf16[2,256,256]{2,1,0:T(8,128)(2,1)S(1)} %bitcast.59, s32[]{:T(128)S(6)} %select_n.54), kind=kOutput, calls=%fused_computation | convolution fusion | flops 537919488 | bytes 4325380 | tf_op jit(solution)/shard_map/dot_general | solution.py:26
  20.2 0.0 collective-permute-start.5
  20.2 0.6 collective-permute-start.4
  20.8 3.5 %shard_map.113 = (f32[2048,128]{1,0:T(8,128)}, f32[2048,128]{1,0:T(8,128)}) custom-call(s32[1]{0:T(128)} %bitcast.3.core_ref, bf16[4096,256]{1,0:T(8,128)(2,1)} %error_ref.2, f32[256,128]{1,0:T(8,128)} %basis_ref.3), custom_call_target="tpu_custom_call" | custom-call | flops 100000 | bytes 10000 | tf_op jit(solution)/shard_map/pallas_call | solution.py:100
  24.4 0.1 collective-permute-start.3
  24.5 0.0 collective-permute-done.4
  24.5 0.6 maximum_select_fusion.feat_ref
  25.1 4.3 %collective-permute-start.2 = (f32[1]{0:T(128)}, f32[1]{0:T(128)}, u32[]{:S(2)}, u32[]{:S(2)}) collective-permute-start(f32[1]{0:T(128)} %add.88), channel_id=1, source_target_pairs={{0,128},{64,192},{128,0},{192,64},{1,129},{65,193},{129,1},{193,65... | collective-permute-start | bytes 20 | tf_op jit(solution)/shard_map/ppermute | solution.py:314
  29.4 11.7 %all-to-all-start = ((f32[32,16,128]{2,1,0:T(8,128)}), f32[32,16,128]{2,1,0:T(8,128)S(1)}, u32[]{:S(2)}, u32[]{:S(2)}) async-start(f32[32,16,128]{2,1,0:T(8,128)} %bitcast.2), calls=%async_computation | async-start | bytes 524288 | tf_op jit(solution)/shard_map/all_to_all | solution.py:352
  41.8 0.0 collective-permute-done.5
  41.8 2.3 %add_convert_fusion = bf16[256,4096]{1,0:T(8,128)(2,1)S(1)} fusion(bf16[256,4096]{1,0:T(8,128)(2,1)} %collective-permute-done.5, bf16[4096,256]{1,0:T(8,128)(2,1)S(1)} %copy-done, bf16[2,256,256]{2,1,0:T(8,128)(2,1)S(1)} %bitcast.60, s32[]{:T(128)S(6)} %select_n.53), kind=kOutput, calls=%fused_computation.1 | convolution fusion | flops 540016640 | bytes 6422532 | tf_op jit(solution)/shard_map/dot_general | solution.py:26
  44.2 0.0 copy-start.3
  44.2 1.3 copy-done.3
  45.5 0.7 dynamic-slice_bitcast_fusion.4
  46.3 6.5 %all-to-all-done.share_ref = f32[32,16,128]{2,1,0:T(8,128)S(1)} async-done(((f32[32,16,128]{2,1,0:T(8,128)}), f32[32,16,128]{2,1,0:T(8,128)S(1)}, u32[]{:S(2)}, u32[]{:S(2)}) %all-to-all-start) | async-done | bytes 262176 | tf_op jit(solution)/shard_map/all_to_all | solution.py:352
  52.7 1.7 %collective-permute-start.7 = (bf16[32,4096]{1,0:T(8,128)(2,1)}, bf16[32,4096]{1,0:T(8,128)(2,1)}, u32[]{:S(2)}, u32[]{:S(2)}) collective-permute-start(bf16[32,4096]{1,0:T(8,128)(2,1)} %get-tuple-element.50), channel_id=1, source_target_pairs={{0,6},{2,0},{4,2},{6,4},{1,7},{3,1},{5,3},{7,5},{8,14},{10,8},{12,... | collective-permute-start | bytes 786440 | tf_op jit(solution)/shard_map/ppermute | solution.py:319
  54.4 0.3 collective-permute-start.6
  54.8 2.9 %shard_map.114 = f32[2048,128]{1,0:T(8,128)} custom-call(f32[1]{0:T(128)S(6)} %div.3.inv_ref, f32[32,16,128]{2,1,0:T(8,128)} %copy-done.5, bf16[16,2048]{1,0:T(8,128)(2,1)} %maximum_select_fusion.feat_ref, f32[2048,128]{1,0:T(8,128)} %get-tuple-element.54.keep_ref, f32[2048,128]{1,0:T(8,128)} %collective-permute-done.3.got_ref), custom_call_target="tpu_custom_call" | custom-call | flops 100000000 | bytes 4000000 | tf_op jit(solution)/shard_map/pallas_call | solution.py:133
  57.7 6.1 %all-to-all-start.1 = ((f32[16,128,128]{2,1,0:T(8,128)}), f32[16,128,128]{2,1,0:T(8,128)S(1)}, u32[]{:S(2)}, u32[]{:S(2)}) async-start(f32[16,128,128]{2,1,0:T(8,128)} %bitcast.56), calls=%async_computation.1 | async-start | bytes 2097152 | tf_op jit(solution)/shard_map/all_to_all | solution.py:367
  63.9 1.1 dynamic-slice_bitcast_fusion.1
  64.9 0.0 collective-permute-done.7
  64.9 1.3 fusion.2
  66.3 1.1 pad_maximum_fusion
  67.3 10.4 %all-to-all-done.1 = f32[16,128,128]{2,1,0:T(8,128)S(1)} async-done(((f32[16,128,128]{2,1,0:T(8,128)}), f32[16,128,128]{2,1,0:T(8,128)S(1)}, u32[]{:S(2)}, u32[]{:S(2)}) %all-to-all-start.1) | async-done | bytes 1048608 | tf_op jit(solution)/shard_map/all_to_all | solution.py:367
  77.7 2.5 %collective-permute-start.8 = (bf16[64,4096]{1,0:T(8,128)(2,1)}, bf16[64,4096]{1,0:T(8,128)(2,1)}, u32[]{:S(2)}, u32[]{:S(2)}) collective-permute-start(bf16[64,4096]{1,0:T(8,128)(2,1)} %get-tuple-element.56), channel_id=1, source_target_pairs={{0,2},{2,4},{4,6},{6,0},{1,3},{3,5},{5,7},{7,1},{8,10},{10,12},{12... | collective-permute-start | bytes 1572872 | tf_op jit(solution)/shard_map/ppermute | solution.py:319
  80.2 0.1 reduce_sum.21
  80.2 0.9 collective-permute-start.10
  81.1 4.3 %collective-permute-done.10 = f32[128,128]{1,0:T(8,128)S(1)} collective-permute-done((f32[128,128]{1,0:T(8,128)S(1)}, f32[128,128]{1,0:T(8,128)S(1)}, u32[]{:S(2)}, u32[]{:S(2)}) %collective-permute-start.10) | collective-permute-done | bytes 65568 | tf_op jit(solution)/shard_map/ppermute | solution.py:314
  85.4 1.0 collective-permute-start.11
  86.4 7.2 %collective-permute-done.11 = f32[128,128]{1,0:T(8,128)S(1)} collective-permute-done((f32[128,128]{1,0:T(8,128)S(1)}, f32[128,128]{1,0:T(8,128)S(1)}, u32[]{:S(2)}, u32[]{:S(2)}) %collective-permute-start.11) | collective-permute-done | bytes 65568 | tf_op jit(solution)/shard_map/ppermute | solution.py:314
  93.7 0.3 collective-permute-start.12
  94.0 8.4 %collective-permute-done.12 = f32[128,128]{1,0:T(8,128)S(1)} collective-permute-done((f32[128,128]{1,0:T(8,128)S(1)}, f32[128,128]{1,0:T(8,128)S(1)}, u32[]{:S(2)}, u32[]{:S(2)}) %collective-permute-start.12) | collective-permute-done | bytes 65568 | tf_op jit(solution)/shard_map/ppermute | solution.py:314
  102.4 0.0 collective-permute-done.8
  102.5 1.1 broadcast_in_dim.14
  103.5 6.1 %all-to-all-start.2 = ((f32[16,128,128]{2,1,0:T(8,128)}), f32[16,128,128]{2,1,0:T(8,128)S(1)}, u32[]{:S(2)}, u32[]{:S(2)}) async-start(f32[16,128,128]{2,1,0:T(8,128)} %broadcast_in_dim.14), calls=%async_computation.2 | async-start | bytes 2097152 | tf_op jit(solution)/shard_map/all_to_all | solution.py:376
  109.6 2.4 %fusion.1 = bf16[64,4096]{1,0:T(8,128)(2,1)} fusion(bf16[64,4096]{1,0:T(8,128)(2,1)} %collective-permute-done.9, bf16[64,4096]{1,0:T(8,128)(2,1)} %collective-permute-done.8, bf16[4,64,4096]{2,1,0:T(8,128)(2,1)} %bitcast.55, s32[]{:T(128)S(6)} %select_n.57), kind=kLoop, calls=%fused_computation.4 | loop fusion | flops 1572864 | bytes 2097156 | tf_op jit(solution)/shard_map/convert_element_type | solution.py:381
  112.0 9.7 %shard_map.115 = (f32[4096,256]{1,0:T(8,128)}, bf16[256,4096]{1,0:T(8,128)(2,1)}, bf16[256,4096]{1,0:T(8,128)(2,1)}) custom-call(f32[1]{0:T(128)S(6)} %div.3.inv_ref, bf16[512,4096]{1,0:T(8,128)(2,1)} %all-gather.2.cloned.1.call-done.feat_ref, bf16[512,256]{1,0:T(8,128)(2,1)} %get-tuple-element.47.dpre_ref, bf16[4096,256]{1,0:T(8,128)(2,1)} %error_ref.2), custom_call_target="tpu_custom_call" | custom-call | flops 2000000000 | bytes 16000000 | tf_op jit(solution)/shard_map/pallas_call | solution.py:163
  121.6 0.1 collective-permute-start.13
  121.7 1.8 %fusion.13 = f32[128,128]{1,0:T(8,128)S(1)} fusion(f32[2048,128]{1,0:T(8,128)S(1)} %bitcast.49), kind=kOutput, calls=%fused_computation.26 | convolution fusion | flops 402653184 | bytes 1114112 | tf_op jit(solution)/shard_map/dot_general | solution.py:385
  123.6 0.8 collective-permute-done.13.other_ref
  124.4 0.1 collective-permute-start.14
  124.5 0.8 copy-done.4
  125.4 4.3 %shard_map.116 = f32[256,128]{1,0:T(8,128)} custom-call(s32[1]{0:T(128)} %bitcast.3.core_ref, bf16[256,4096]{1,0:T(8,128)(2,1)} %get-tuple-element.66.head_ref, bf16[256,4096]{1,0:T(8,128)(2,1)} %get-tuple-element.67.rest_ref, f32[2048,128]{1,0:T(8,128)} %bitcast.50, f32[2048,128]{1,0:T(8,128)} %copy-done.4), custom_call_target="tpu_custom_call" | custom-call | flops 1000000000 | bytes 6000000 | tf_op jit(solution)/shard_map/pallas_call | solution.py:208
  129.7 3.5 %all-to-all-start.3 = ((bf16[8,8,4096]{2,1,0:T(8,128)(2,1)}), bf16[8,8,4096]{2,1,0:T(8,128)(2,1)S(1)}, u32[]{:S(2)}, u32[]{:S(2)}) async-start(bf16[8,8,4096]{2,1,0:T(8,128)(2,1)} %bitcast.57), calls=%async_computation.3 | async-start | bytes 1048576 | tf_op jit(solution)/shard_map/all_to_all | solution.py:391
  133.2 1.6 collective-permute-start.15
  134.7 4.3 %collective-permute-done.15 = f32[256,128]{1,0:T(8,128)S(1)} collective-permute-done((f32[256,128]{1,0:T(8,128)}, f32[256,128]{1,0:T(8,128)S(1)}, u32[]{:S(2)}, u32[]{:S(2)}) %collective-permute-start.15) | collective-permute-done | bytes 131104 | tf_op jit(solution)/shard_map/ppermute | solution.py:314
  139.0 0.9 add.114
  139.9 3.3 %collective-permute-start.16 = (f32[256,128]{1,0:T(8,128)S(1)}, f32[256,128]{1,0:T(8,128)S(1)}, u32[]{:S(2)}, u32[]{:S(2)}) collective-permute-start(f32[256,128]{1,0:T(8,128)S(1)} %add.114), channel_id=1, source_target_pairs={{0,128},{64,192},{128,0},{192,64},{1,129},{65,193},{129,1},{193,65... | collective-permute-start | bytes 393224 | tf_op jit(solution)/shard_map/ppermute | solution.py:314
  143.2 5.0 %shard_map.117.inverse_ref = f32[128,128]{1,0:T(8,128)S(1)} custom-call(f32[128,128]{1,0:T(8,128)S(1)} %add.113.gram_ref), custom_call_target="tpu_custom_call" | custom-call | flops 10000000 | bytes 100000 | tf_op jit(solution)/shard_map/pallas_call | solution.py:251
  148.2 0.0 copy-start.1
  148.2 0.6 copy-done.1
  148.9 0.7 add.115.right_ref
  149.5 5.7 %shard_map.118 = (bf16[4096,256]{1,0:T(8,128)(2,1)}, f32[256,128]{1,0:T(8,128)}) custom-call(s32[1]{0:T(128)} %bitcast.3.core_ref, f32[4096,256]{1,0:T(8,128)} %get-tuple-element.70.merged_ref, f32[2048,128]{1,0:T(8,128)} %bitcast.51, f32[2048,128]{1,0:T(8,128)} %copy-done.4, f32[256,128]{1,0:T(8,128)} %add.115.right_ref, f32[128,128]{1,0:T(8,128)} %copy-done.1), custom_call_target="tpu_custom_call" | custom-call | flops 1000000000 | bytes 8000000 | tf_op jit(solution)/shard_map/pallas_call | solution.py:284
  155.2 0.7 bitcast_reduce_fusion
  (23 shorter events, 0.1 us)
Async XLA Ops:
  7.2 11.0 %copy-start = (bf16[4096,256]{1,0:T(8,128)(2,1)S(1)}, bf16[4096,256]{1,0:T(8,128)(2,1)}, u32[]{:S(2)}) copy-start(bf16[4096,256]{1,0:T(8,128)(2,1)} %param.12) | copy-start | bytes 6291460
  7.2 104.8 %all-gather.2.cloned.1.call-start = ((), (), s32[]{:S(2)}) async-start(), calls=%async_computation.4 | async-start | bytes 4259840 | tf_op jit(solution)/shard_map/all_gather | solution.py:335
  11.3 4.1 %collective-permute-start.1 = (f32[512,128]{1,0:T(8,128)}, f32[512,128]{1,0:T(8,128)S(1)}, u32[]{:S(2)}, u32[]{:S(2)}) collective-permute-start(f32[512,128]{1,0:T(8,128)} %get-tuple-element.41), channel_id=1, source_target_pairs={{0,1},{1,0},{2,3},{3,2},{4,5},{5,4},{6,7},{7,6},{8,9},{9,8},{10,11... | collective-permute-start | bytes 786440 | tf_op jit(solution)/shard_map/ppermute | solution.py:314
  11.3 3.5 %collective-permute-start = (f32[1]{0:T(128)}, f32[1]{0:T(128)}, u32[]{:S(2)}, u32[]{:S(2)}) collective-permute-start(f32[1]{0:T(128)} %convert_element_type.29), channel_id=1, source_target_pairs={{0,64},{64,0},{128,192},{192,128},{1,65},{65,1},{129,193},{193,129... | collective-permute-start | bytes 20 | tf_op jit(solution)/shard_map/ppermute | solution.py:314
  18.1 2.1 %copy-start.6 = (bf16[8,4096]{1,0:T(8,128)(2,1)S(1)}, bf16[8,4096]{1,0:T(8,128)(2,1)}, u32[]{:S(2)}) copy-start(bf16[8,4096]{1,0:T(8,128)(2,1)} %param.9) | copy-start | bytes 196612
  20.2 21.6 %collective-permute-start.5 = (bf16[256,4096]{1,0:T(8,128)(2,1)}, bf16[256,4096]{1,0:T(8,128)(2,1)}, u32[]{:S(2)}, u32[]{:S(2)}) collective-permute-start(bf16[256,4096]{1,0:T(8,128)(2,1)} %convolution_convert_fusion), channel_id=1, source_target_pairs={{0,1},{1,0},{2,3},{3,2},{4,5},{5,4},{6,7},{7,6},{8,9},{9,8},{10,11... | collective-permute-start | bytes 6291464 | tf_op jit(solution)/shard_map/ppermute | solution.py:314
  20.2 4.2 %collective-permute-start.4 = (bf16[8,2048]{1,0:T(8,128)(2,1)S(1)}, bf16[8,2048]{1,0:T(8,128)(2,1)S(1)}, u32[]{:S(2)}, u32[]{:S(2)}) collective-permute-start(bf16[8,2048]{1,0:T(8,128)(2,1)S(1)} %get-tuple-element.86), channel_id=1, source_target_pairs={{0,1},{1,0},{2,3},{3,2},{4,5},{5,4},{6,7},{7,6},{8,9},{9,8},{10,11... | collective-permute-start | bytes 98312 | tf_op jit(solution)/shard_map/ppermute | solution.py:314
  24.4 28.4 %collective-permute-start.3 = (f32[2048,128]{1,0:T(8,128)}, f32[2048,128]{1,0:T(8,128)}, u32[]{:S(2)}, u32[]{:S(2)}) collective-permute-start(f32[2048,128]{1,0:T(8,128)} %get-tuple-element.46), channel_id=1, source_target_pairs={{0,1},{1,0},{2,3},{3,2},{4,5},{5,4},{6,7},{7,6},{8,9},{9,8},{10,11... | collective-permute-start | bytes 3145736 | tf_op jit(solution)/shard_map/ppermute | solution.py:314
  25.1 16.1 %collective-permute-start.2 = (f32[1]{0:T(128)}, f32[1]{0:T(128)}, u32[]{:S(2)}, u32[]{:S(2)}) collective-permute-start(f32[1]{0:T(128)} %add.88), channel_id=1, source_target_pairs={{0,128},{64,192},{128,0},{192,64},{1,129},{65,193},{129,1},{193,65... | collective-permute-start | bytes 20 | tf_op jit(solution)/shard_map/ppermute | solution.py:314
  29.4 23.3 %all-to-all-start = ((f32[32,16,128]{2,1,0:T(8,128)}), f32[32,16,128]{2,1,0:T(8,128)S(1)}, u32[]{:S(2)}, u32[]{:S(2)}) async-start(f32[32,16,128]{2,1,0:T(8,128)} %bitcast.2), calls=%async_computation | async-start | bytes 524288 | tf_op jit(solution)/shard_map/all_to_all | solution.py:352
  44.2 1.3 copy-start.3
  52.7 2.0 %copy-start.5 = (f32[32,16,128]{2,1,0:T(8,128)}, f32[32,16,128]{2,1,0:T(8,128)S(1)}, u32[]{:S(2)}) copy-start(f32[32,16,128]{2,1,0:T(8,128)S(1)} %all-to-all-done.share_ref) | copy-start | bytes 786436
  52.7 12.2 %collective-permute-start.7 = (bf16[32,4096]{1,0:T(8,128)(2,1)}, bf16[32,4096]{1,0:T(8,128)(2,1)}, u32[]{:S(2)}, u32[]{:S(2)}) collective-permute-start(bf16[32,4096]{1,0:T(8,128)(2,1)} %get-tuple-element.50), channel_id=1, source_target_pairs={{0,6},{2,0},{4,2},{6,4},{1,7},{3,1},{5,3},{7,5},{8,14},{10,8},{12,... | collective-permute-start | bytes 786440 | tf_op jit(solution)/shard_map/ppermute | solution.py:319
  54.4 10.5 %collective-permute-start.6 = (bf16[32,4096]{1,0:T(8,128)(2,1)S(1)}, bf16[32,4096]{1,0:T(8,128)(2,1)}, u32[]{:S(2)}, u32[]{:S(2)}) collective-permute-start(bf16[32,4096]{1,0:T(8,128)(2,1)S(1)} %get-tuple-element.49), channel_id=1, source_target_pairs={{0,2},{2,4},{4,6},{6,0},{1,3},{3,5},{5,7},{7,1},{8,10},{10,12},{12... | collective-permute-start | bytes 786440 | tf_op jit(solution)/shard_map/ppermute | solution.py:319
  57.7 20.0 %all-to-all-start.1 = ((f32[16,128,128]{2,1,0:T(8,128)}), f32[16,128,128]{2,1,0:T(8,128)S(1)}, u32[]{:S(2)}, u32[]{:S(2)}) async-start(f32[16,128,128]{2,1,0:T(8,128)} %bitcast.56), calls=%async_computation.1 | async-start | bytes 2097152 | tf_op jit(solution)/shard_map/all_to_all | solution.py:367
  77.7 24.8 %collective-permute-start.8 = (bf16[64,4096]{1,0:T(8,128)(2,1)}, bf16[64,4096]{1,0:T(8,128)(2,1)}, u32[]{:S(2)}, u32[]{:S(2)}) collective-permute-start(bf16[64,4096]{1,0:T(8,128)(2,1)} %get-tuple-element.56), channel_id=1, source_target_pairs={{0,2},{2,4},{4,6},{6,0},{1,3},{3,5},{5,7},{7,1},{8,10},{10,12},{12... | collective-permute-start | bytes 1572872 | tf_op jit(solution)/shard_map/ppermute | solution.py:319
  80.2 22.3 %collective-permute-start.9 = (bf16[64,4096]{1,0:T(8,128)(2,1)}, bf16[64,4096]{1,0:T(8,128)(2,1)}, u32[]{:S(2)}, u32[]{:S(2)}) collective-permute-start(bf16[64,4096]{1,0:T(8,128)(2,1)} %get-tuple-element.57), channel_id=1, source_target_pairs={{0,6},{2,0},{4,2},{6,4},{1,7},{3,1},{5,3},{7,5},{8,14},{10,8},{12,... | collective-permute-start | bytes 1572872 | tf_op jit(solution)/shard_map/ppermute | solution.py:319
  80.2 5.2 %collective-permute-start.10 = (f32[128,128]{1,0:T(8,128)S(1)}, f32[128,128]{1,0:T(8,128)S(1)}, u32[]{:S(2)}, u32[]{:S(2)}) collective-permute-start(f32[128,128]{1,0:T(8,128)S(1)} %reduce_sum.21), channel_id=1, source_target_pairs={{0,8},{8,0},{16,24},{24,16},{32,40},{40,32},{48,56},{56,48},{1,9},... | collective-permute-start | bytes 196616 | tf_op jit(solution)/shard_map/ppermute | solution.py:314
  85.4 8.2 %collective-permute-start.11 = (f32[128,128]{1,0:T(8,128)S(1)}, f32[128,128]{1,0:T(8,128)S(1)}, u32[]{:S(2)}, u32[]{:S(2)}) collective-permute-start(f32[128,128]{1,0:T(8,128)S(1)} %add.108), channel_id=1, source_target_pairs={{0,16},{8,24},{16,0},{24,8},{32,48},{40,56},{48,32},{56,40},{1,17}... | collective-permute-start | bytes 196616 | tf_op jit(solution)/shard_map/ppermute | solution.py:314
  93.7 8.7 %collective-permute-start.12 = (f32[128,128]{1,0:T(8,128)S(1)}, f32[128,128]{1,0:T(8,128)S(1)}, u32[]{:S(2)}, u32[]{:S(2)}) collective-permute-start(f32[128,128]{1,0:T(8,128)S(1)} %add.109), channel_id=1, source_target_pairs={{0,32},{8,40},{16,48},{24,56},{32,0},{40,8},{48,16},{56,24},{1,33}... | collective-permute-start | bytes 196616 | tf_op jit(solution)/shard_map/ppermute | solution.py:314
  103.5 18.1 %all-to-all-start.2 = ((f32[16,128,128]{2,1,0:T(8,128)}), f32[16,128,128]{2,1,0:T(8,128)S(1)}, u32[]{:S(2)}, u32[]{:S(2)}) async-start(f32[16,128,128]{2,1,0:T(8,128)} %broadcast_in_dim.14), calls=%async_computation.2 | async-start | bytes 2097152 | tf_op jit(solution)/shard_map/all_to_all | solution.py:376
  121.6 2.9 %copy-start.2 = (f32[16,128,128]{2,1,0:T(8,128)}, f32[16,128,128]{2,1,0:T(8,128)S(1)}, u32[]{:S(2)}) copy-start(f32[16,128,128]{2,1,0:T(8,128)S(1)} %all-to-all-done.2) | copy-start | bytes 3145732
  121.6 2.7 %collective-permute-start.13 = (f32[2048,128]{1,0:T(8,128)S(1)}, f32[2048,128]{1,0:T(8,128)S(1)}, u32[]{:S(2)}, u32[]{:S(2)}) collective-permute-start(f32[2048,128]{1,0:T(8,128)S(1)} %bitcast.48), channel_id=1, source_target_pairs={{0,1},{1,0},{2,3},{3,2},{4,5},{5,4},{6,7},{7,6},{8,9},{9,8},{10,11... | collective-permute-start | bytes 3145736 | tf_op jit(solution)/shard_map/ppermute | solution.py:314
  124.4 1.0 copy-start.4
  124.4 5.3 %collective-permute-start.14 = (f32[128,128]{1,0:T(8,128)S(1)}, f32[128,128]{1,0:T(8,128)S(1)}, u32[]{:S(2)}, u32[]{:S(2)}) collective-permute-start(f32[128,128]{1,0:T(8,128)S(1)} %fusion.13), channel_id=1, source_target_pairs={{0,1},{1,0},{2,3},{3,2},{4,5},{5,4},{6,7},{7,6},{8,9},{9,8},{10,11... | collective-permute-start | bytes 196616 | tf_op jit(solution)/shard_map/ppermute | solution.py:314
  129.7 25.6 %all-to-all-start.3 = ((bf16[8,8,4096]{2,1,0:T(8,128)(2,1)}), bf16[8,8,4096]{2,1,0:T(8,128)(2,1)S(1)}, u32[]{:S(2)}, u32[]{:S(2)}) async-start(bf16[8,8,4096]{2,1,0:T(8,128)(2,1)} %bitcast.57), calls=%async_computation.3 | async-start | bytes 1048576 | tf_op jit(solution)/shard_map/all_to_all | solution.py:391
  133.2 5.8 %collective-permute-start.15 = (f32[256,128]{1,0:T(8,128)}, f32[256,128]{1,0:T(8,128)S(1)}, u32[]{:S(2)}, u32[]{:S(2)}) collective-permute-start(f32[256,128]{1,0:T(8,128)} %shard_map.116), channel_id=1, source_target_pairs={{0,64},{64,0},{128,192},{192,128},{1,65},{65,1},{129,193},{193,129... | collective-permute-start | bytes 393224 | tf_op jit(solution)/shard_map/ppermute | solution.py:314
  139.9 8.9 %collective-permute-start.16 = (f32[256,128]{1,0:T(8,128)S(1)}, f32[256,128]{1,0:T(8,128)S(1)}, u32[]{:S(2)}, u32[]{:S(2)}) collective-permute-start(f32[256,128]{1,0:T(8,128)S(1)} %add.114), channel_id=1, source_target_pairs={{0,128},{64,192},{128,0},{192,64},{1,129},{65,193},{129,1},{193,65... | collective-permute-start | bytes 393224 | tf_op jit(solution)/shard_map/ppermute | solution.py:314
  148.2 0.6 copy-start.1
Sparse Core Ops, SparseCore 0:
  10.8 91.2 all-gather.1

commit v4 on v3

--- a/solution.py
+++ b/solution.py
@@ -41,7 +41,7 @@
     return pltpu.CompilerParams(vmem_limit_bytes=limit)
 
 
-def token_kernel(count_ref, pairs_ref, table_ref, up_ref, pre_ref, basis_ref, dpre_ref, share_ref):
+def token_kernel(count_ref, pairs_ref, table_ref, up_ref, pre_ref, basis_ref, dpre_ref, rows_ref, share_ref):
     rows = up_ref.shape[0]
     stations = table_ref.shape[1]
     table = table_ref[...]
@@ -61,8 +61,13 @@
     weight = jnp.where(live, weight, 0.0)
     column = jnp.transpose(jnp.broadcast_to(weight, (128, rows)))
     column = jnp.concatenate([column] * (up_ref.shape[1] // 128), axis=1)
-    dpre = (up_ref[...].astype(F32) * gelu_slope(pre_ref[...].astype(F32)) * column).astype(BF16)
+    wide = up_ref[...].astype(F32) * gelu_slope(pre_ref[...].astype(F32)) * column
+    dpre = wide.astype(BF16)
     dpre_ref[...] = dpre
+    starts = [
+        ((z * 4 + y) * 2 + core) * 8 for core in range(2) for y in range(4) for z in range(rows // 64)
+    ]
+    rows_ref[...] = jnp.concatenate([wide[s : s + 8] for s in starts], axis=0).astype(BF16)
     share_ref[...] = mm_wide(dpre, basis_ref[...], ((1,), (0,)))
 
 
@@ -72,10 +77,11 @@
         token_kernel,
         out_shape=(
             jax.ShapeDtypeStruct(upstream.shape, BF16),
+            jax.ShapeDtypeStruct(upstream.shape, BF16),
             jax.ShapeDtypeStruct((upstream.shape[0], basis.shape[1]), F32),
         ),
         in_specs=[pl.BlockSpec(memory_space=pltpu.SMEM)] + [vm] * 5,
-        out_specs=(vm, vm),
+        out_specs=(vm, vm, vm),
         compiler_params=params(),
         cost_estimate=pl.CostEstimate(flops=10**5, bytes_accessed=10**4, transcendentals=0),
     )(counts, pairs.T, table[None], upstream, preact, basis)
@@ -114,10 +120,8 @@
     )(core, error, basis)
 
 
-def left_kernel(inv_ref, share_ref, feat_ref, keep_ref, got_ref, out_ref):
-    share = share_ref[0]
-    for i in range(1, share_ref.shape[0]):
-        share = share + share_ref[i]
+def left_kernel(inv_ref, share_ref, other_ref, feat_ref, keep_ref, got_ref, out_ref):
+    share = share_ref[...] + other_ref[...]
     out_ref[...] = (
         keep_ref[...]
         + got_ref[...]
@@ -125,8 +129,8 @@
     )
 
 
-def left_part(inv_mean, share, feats, keep, got):
-    blocks, tokens, rank = share.shape
+def left_part(inv_mean, share, share_got, feats, keep, got):
+    tokens, rank = share.shape
     half = got.shape[0]
     step = half // 2
     rows = pl.BlockSpec((step, rank), lambda i: (i, 0))
@@ -136,7 +140,8 @@
         grid=(half // step,),
         in_specs=[
             pl.BlockSpec(memory_space=pltpu.SMEM),
-            pl.BlockSpec((blocks, tokens, rank), lambda i: (0, 0, 0)),
+            pl.BlockSpec((tokens, rank), lambda i: (0, 0)),
+            pl.BlockSpec((tokens, rank), lambda i: (0, 0)),
             pl.BlockSpec((tokens, step), lambda i: (0, i)),
             rows,
             rows,
@@ -144,7 +149,7 @@
         out_specs=rows,
         compiler_params=params(),
         cost_estimate=pl.CostEstimate(flops=10**8, bytes_accessed=4 * 10**6, transcendentals=0),
-    )(inv_mean, share, feats, keep, got)
+    )(inv_mean, share, share_got, feats, keep, got)
 
 
 def merge_kernel(inv_ref, feat_ref, dpre_ref, error_ref, merged_ref, head_ref, rest_ref):
@@ -258,7 +263,7 @@
     )(gram)
 
 
-def last_kernel(core_ref, merged_ref, own_ref, other_ref, right_ref, inverse_ref, error_ref, basis_ref, back_ref):
+def last_kernel(core_ref, merged_ref, own_ref, other_ref, right_ref, got_ref, inverse_ref, error_ref, basis_ref, back_ref):
     def fill(left):
         out = mm_split(split(left), (back_ref[0], back_ref[1]), ((1,), (1,)))
         error_ref[...] = (merged_ref[...] - out).astype(BF16)
@@ -266,7 +271,7 @@
     @pl.when(pl.program_id(0) == 0)
     def _():
         inverse = split(inverse_ref[...])
-        basis = mm_split(split(right_ref[...]), inverse, ((1,), (1,)))
+        basis = mm_split(split(right_ref[...] + got_ref[...]), inverse, ((1,), (1,)))
         basis_ref[...] = basis
         head, rest = split(mm_split(split(basis * 0.25), inverse, ((1,), (0,))))
         back_ref[0] = head
@@ -276,7 +281,7 @@
     pl.when(pl.program_id(0) == 1)(lambda: fill(other_ref[...]))
 
 
-def last_part(core, merged, own, other, right, inverse):
+def last_part(core, merged, own, other, right, got, inverse):
     width, cols = merged.shape
     half, rank = own.shape
     whole = lambda h, core: (0, 0)
@@ -295,6 +300,7 @@
                 pl.BlockSpec((half, rank), whole),
                 pl.BlockSpec((half, rank), whole),
                 pl.BlockSpec((cols, rank), whole),
+                pl.BlockSpec((cols, rank), whole),
                 pl.BlockSpec((rank, rank), whole),
             ],
             out_specs=(row, pl.BlockSpec((cols, rank), whole)),
@@ -302,7 +308,7 @@
         ),
         compiler_params=params(),
         cost_estimate=pl.CostEstimate(flops=10**9, bytes_accessed=8 * 10**6, transcendentals=0),
-    )(core, merged, own, other, right, inverse)
+    )(core, merged, own, other, right, got, inverse)
 
 
 PLANE = ("z", "y", "c")
@@ -340,14 +346,13 @@
     count = counts.astype(F32)
     count = count + swap(count, "x", 1)
 
-    dpre, share = token_part(counts, pairs, station_weight, upstream, preact, basis)
-    share = share + swap(share, "c", 1)
-    count, share, error_late, late = tie((count, share, error, dpre))
-    inv_mean = n_inter / (count + swap(count, "x", 2))
+    dpre, rows, share = token_part(counts, pairs, station_weight, upstream, preact, basis)
+    count, share, error_late, rows = tie((count, share, error, rows))
     err_give, err_keep = error_part(core, error_late, basis)
     err_got = swap(err_give, "c", 1)
-
-    rows = late.reshape(n_z, n_y, 2, 8, cols).transpose(2, 1, 0, 3, 4).reshape(2, -1, cols)
+    inv_mean = n_inter / (count + swap(count, "x", 2))
+
+    rows = rows.reshape(2, -1, cols)
     got = swap(mm(pick(rows, 1 - c), weight, ((1,), (1,))).astype(BF16), "c", 1)
     share = lax.all_to_all(share, ("z", "y"), 0, 0, tiled=True).reshape(n_z * n_y, -1, rank)
     grad = (mm(pick(rows, c), weight, ((1,), (1,))) + got.astype(F32)).astype(BF16)
@@ -358,9 +363,11 @@
     inv_mean, share, err_got, pair, grad, far_up, far_down = tie(
         (inv_mean, share, err_got, pair, grad, far_up, far_down)
     )
-    part = left_part(inv_mean, share, pair, err_keep, err_got)
+    share = share.sum(0)
+    part = left_part(inv_mean, share, swap(share, "c", 1), pair, err_keep, err_got)
 
     up, down = shift(far_up, "y", 1), shift(far_down, "y", -1)
+    grad, part = tie((grad, part))
     after, before = pick(grad, (y + 1) % n_y), pick(grad, (y + 3) % n_y)
     after = jnp.concatenate([after[:piece] + up, after[piece:]])
     before = jnp.concatenate([before[:piece], before[piece:] + down])
@@ -382,19 +389,18 @@
     grad, merged, mine = tie((grad, merged, mine))
 
     other = swap(mine, "c", 1)
+    grad = lax.all_to_all(grad, "z", 0, 0, tiled=True)
     gram = jnp.dot(mine.T, mine, precision=HIGHEST)
+    gram = gram + swap(gram, "c", 1)
     gram, other = tie((gram, other))
-    gram = gram + swap(gram, "c", 1)
     right = right_part(core, head, rest, mine, other)
-    gram, grad, right = tie((gram, grad, right))
+    inverse = inverse_part(gram)
     right = right + swap(right, "x", 1)
-    grad = lax.all_to_all(grad, "z", 0, 0, tiled=True)
-    gram, right = tie((gram, right))
-    inverse = inverse_part(gram)
-    right = right + swap(right, "x", 2)
-    new_error, new_basis = last_part(core, merged, mine, other, right, inverse)
-    grad, new_basis = tie((grad, new_basis))
+    inverse, right = tie((inverse, right))
+    right_got = swap(right, "x", 2)
     grad = grad.reshape(n_z, -1, width).astype(F32).sum(0).astype(BF16)
+    grad, right_got = tie((grad, right_got))
+    new_error, new_basis = last_part(core, merged, mine, other, right, right_got, inverse)
     return grad, new_error, new_basis
 
 

time: 164 us -> 158 us (0.963)
  waiting for transfers between devices: 43.3 us -> 32.1 us
  starting transfers between devices: 47 us -> 53.4 us
    ppermute x13, waiting for transfers between devices: 25.8 us -> 16.7 us  [swap(): return lax.ppermute(value, axis, [(i, i ^ bit) for i in range(n)])]
    ppermute x13, starting transfers between devices: 15 us -> 20.6 us  [swap(): return lax.ppermute(value, axis, [(i, i ^ bit) for i in range(n)])]
    all_to_all x1, waiting for transfers between devices: 6.48 us -> 1.7 us  [per_device(): lax.all_to_all(share, ('z', 'y'), 0, 0, tiled=True)]
    all_to_all x1, waiting for transfers between devices: 10.4 us -> 13 us  [per_device(): part = lax.all_to_all(part, ('x', 'y'), 0, 0, tiled=True)]
    add x2 -> x0, other arithmetic: 2.35 us -> none  [the longest x1 1.67 us: per_device(): share = share + swap(share, 'c', 1)]
    all_to_all x1, starting transfers between devices: 3.5 us -> 5.35 us  [per_device(): grad = lax.all_to_all(grad, 'z', 0, 0, tiled=True)]
  transfers between devices with their start and end apart: 22 -> 22, of which waited for: 8 -> 7; matrix products, arithmetic and copies ran while one was open for 12% -> 12% of each run, Pallas kernels for 21% -> 18%
where the time goes in v4:
time: 158 us; the launch traced here: 157 us
  starting transfers between devices  53.4 us (34%)
  Pallas kernels  34 us (22%)
  waiting for transfers between devices  32.1 us (20%)
  between operations  16.4 us (10%)
  other arithmetic  8.11 us (5%)
  matrix products  7.25 us (5%)
  local copies, waits for them, and re-layouts  6.18 us (4%)
    ppermute x13, starting transfers between devices, swap(): return lax.ppermute(value, axis, [(i, i ^ bit) for i in range(n)])  20.6 us
    ppermute x13, waiting for transfers between devices, swap(): return lax.ppermute(value, axis, [(i, i ^ bit) for i in range(n)])  16.7 us
    all_to_all x1, waiting for transfers between devices, per_device(): part = lax.all_to_all(part, ('x', 'y'), 0, 0, tiled=True)  13 us
    all_to_all x1, starting transfers between devices, per_device(): lax.all_to_all(share, ('z', 'y'), 0, 0, tiled=True)  11.7 us
    pallas_call x1, Pallas kernels, merge_part(): pl.pallas_call(merge_kernel, out_shape=(jax.ShapeDtypeStruct((width, cols...  9.66 us
    all_to_all x1, starting transfers between devices, per_device(): part = lax.all_to_all(part, ('x', 'y'), 0, 0, tiled=True)  5.91 us
    pallas_call x1, Pallas kernels, last_part(): pl.pallas_call(last_kernel, out_shape=(jax.ShapeDtypeStruct((width, cols)...  5.78 us
    all_to_all x1, starting transfers between devices, per_device(): lax.all_to_all(jnp.broadcast_to(part[None], (n_inter * n_y,) + part.shape...  5.61 us
  transfers between devices with their start and end apart: 22, of which 7 were waited for; matrix products, arithmetic and copies ran while one was open for 12% of the time, Pallas kernels for 18%

profile of v4, /device:TPU:8, one launch (start us, length us, event | category | flops | bytes accessed | tf_op | source)
XLA Modules:
  0.0 157.4 jit_solution(15714522650300910102)
XLA Ops:
  7.2 0.0 copy-start
  7.2 0.0 all-gather.2.cloned.1.call-start
  7.2 0.7 all-gather.2.cloned.1.call-update
  8.6 2.9 %collective-permute-start = (f32[1]{0:T(128)}, f32[1]{0:T(128)}, u32[]{:S(2)}, u32[]{:S(2)}) collective-permute-start(f32[1]{0:T(128)} %convert_element_type.29), channel_id=1, source_target_pairs={{0,64},{64,0},{128,192},{192,128},{1,65},{65,1},{129,193},{193,129... | collective-permute-start | bytes 20 | tf_op jit(solution)/shard_map/ppermute | solution.py:320
  11.4 2.9 %shard_map.112 = (bf16[512,256]{1,0:T(8,128)(2,1)}, bf16[512,256]{1,0:T(8,128)(2,1)}, f32[512,128]{1,0:T(8,128)}) custom-call(s32[1]{0:T(128)S(6)} %copy.12.count_ref, s32[2,512]{1,0:T(2,128)} %bitcast.54, f32[1,512]{1,0:T(1,128)} %bitcast.55, bf16[512,256]{1,0:T(8,128)(2,1)} %up_ref.1, bf16[512,256]{1,0:T(8,128)(2,1)} %pre_ref.1, f32[256,128]{1,0:T(8,128)} %basis_ref.3), custom_call_target="tpu_custom_call" | custom-call | flops 100000 | bytes 10000 | tf_op jit(solution)/shard_map/pallas_call | solution.py:76
  15.0 0.0 copy-start.6
  15.0 3.0 %convolution_convert_fusion = bf16[256,4096]{1,0:T(8,128)(2,1)} fusion(bf16[4096,256]{1,0:T(8,128)(2,1)S(1)} %copy-done, bf16[2,256,256]{2,1,0:T(8,128)(2,1)} %bitcast.52, s32[]{:T(128)S(6)} %select_n.54), kind=kOutput, calls=%fused_computation | convolution fusion | flops 537919488 | bytes 4325380 | tf_op jit(solution)/shard_map/dot_general | solution.py:26
  18.0 0.0 collective-permute-start.4
  18.1 0.6 collective-permute-start.3
  18.6 4.0 %collective-permute-start.1 = (f32[1]{0:T(128)}, f32[1]{0:T(128)}, u32[]{:S(2)}, u32[]{:S(2)}) collective-permute-start(f32[1]{0:T(128)} %add.82), channel_id=1, source_target_pairs={{0,128},{64,192},{128,0},{192,64},{1,129},{65,193},{129,1},{193,65... | collective-permute-start | bytes 20 | tf_op jit(solution)/shard_map/ppermute | solution.py:320
  22.7 11.7 %all-to-all-start = ((f32[32,16,128]{2,1,0:T(8,128)}), f32[32,16,128]{2,1,0:T(8,128)S(1)}, u32[]{:S(2)}, u32[]{:S(2)}) async-start(f32[32,16,128]{2,1,0:T(8,128)} %bitcast.2), calls=%async_computation | async-start | bytes 524288 | tf_op jit(solution)/shard_map/all_to_all | solution.py:357
  34.4 3.6 %shard_map.113 = (f32[2048,128]{1,0:T(8,128)}, f32[2048,128]{1,0:T(8,128)}) custom-call(s32[1]{0:T(128)} %bitcast.3.core_ref, bf16[4096,256]{1,0:T(8,128)(2,1)} %error_ref.2, f32[256,128]{1,0:T(8,128)} %basis_ref.3), custom_call_target="tpu_custom_call" | custom-call | flops 100000 | bytes 10000 | tf_op jit(solution)/shard_map/pallas_call | solution.py:106
  38.0 0.0 collective-permute-start.2
  38.7 0.0 collective-permute-done.3
  38.7 0.6 maximum_select_fusion.feat_ref
  39.4 0.0 collective-permute-done.4
  39.4 2.4 %add_convert_fusion = bf16[256,4096]{1,0:T(8,128)(2,1)S(1)} fusion(bf16[256,4096]{1,0:T(8,128)(2,1)} %collective-permute-done.4, bf16[4096,256]{1,0:T(8,128)(2,1)S(1)} %copy-done, bf16[2,256,256]{2,1,0:T(8,128)(2,1)} %bitcast.53, s32[]{:T(128)S(6)} %select_n.53), kind=kOutput, calls=%fused_computation.1 | convolution fusion | flops 540016640 | bytes 6422532 | tf_op jit(solution)/shard_map/dot_general | solution.py:26
  41.8 0.0 copy-start.3
  41.8 1.3 copy-done.3
  43.1 0.8 dynamic-slice_bitcast_fusion.4
  44.0 1.7 %all-to-all-done = f32[32,16,128]{2,1,0:T(8,128)S(1)} async-done(((f32[32,16,128]{2,1,0:T(8,128)}), f32[32,16,128]{2,1,0:T(8,128)S(1)}, u32[]{:S(2)}, u32[]{:S(2)}) %all-to-all-start) | async-done | bytes 262176 | tf_op jit(solution)/shard_map/all_to_all | solution.py:357
  45.6 0.0 collective-permute-done.2.got_ref
  45.7 0.0 copy-start.8
  45.7 0.1 collective-permute-start.5
  45.8 2.1 %collective-permute-start.7 = (bf16[32,4096]{1,0:T(8,128)(2,1)}, bf16[32,4096]{1,0:T(8,128)(2,1)S(1)}, u32[]{:S(2)}, u32[]{:S(2)}) collective-permute-start(bf16[32,4096]{1,0:T(8,128)(2,1)} %get-tuple-element.56), channel_id=1, source_target_pairs={{0,6},{2,0},{4,2},{6,4},{1,7},{3,1},{5,3},{7,5},{8,14},{10,8},{12,... | collective-permute-start | bytes 786440 | tf_op jit(solution)/shard_map/ppermute | solution.py:325
  48.0 0.6 copy-done.9
  48.6 2.7 %shard_map.114 = f32[2048,128]{1,0:T(8,128)} custom-call(f32[1]{0:T(128)S(6)} %div.3.inv_ref, f32[16,128]{1,0:T(8,128)} %copy-done.8, f32[16,128]{1,0:T(8,128)} %copy-done.9, bf16[16,2048]{1,0:T(8,128)(2,1)} %maximum_select_fusion.feat_ref, f32[2048,128]{1,0:T(8,128)} %get-tuple-element.52.keep_ref, f32[2048,128]{1,0:T(8,128)} %copy-done.4), custom_call_target="tpu_custom_call" | custom-call | flops 100000000 | bytes 4000000 | tf_op jit(solution)/shard_map/pallas_call | solution.py:137
  51.3 5.9 %all-to-all-start.1 = ((f32[16,128,128]{2,1,0:T(8,128)}), f32[16,128,128]{2,1,0:T(8,128)S(1)}, u32[]{:S(2)}, u32[]{:S(2)}) async-start(f32[16,128,128]{2,1,0:T(8,128)} %bitcast.50), calls=%async_computation.1 | async-start | bytes 2097152 | tf_op jit(solution)/shard_map/all_to_all | solution.py:374
  57.2 1.1 dynamic-slice_bitcast_fusion.1
  58.3 0.0 collective-permute-done.7
  58.3 1.2 fusion.2
  59.6 1.1 pad_maximum_fusion
  60.6 13.0 %all-to-all-done.1 = f32[16,128,128]{2,1,0:T(8,128)S(1)} async-done(((f32[16,128,128]{2,1,0:T(8,128)}), f32[16,128,128]{2,1,0:T(8,128)S(1)}, u32[]{:S(2)}, u32[]{:S(2)}) %all-to-all-start.1) | async-done | bytes 1048608 | tf_op jit(solution)/shard_map/all_to_all | solution.py:374
  73.6 0.1 collective-permute-start.8
  73.7 2.0 %collective-permute-start.9 = (bf16[64,4096]{1,0:T(8,128)(2,1)}, bf16[64,4096]{1,0:T(8,128)(2,1)}, u32[]{:S(2)}, u32[]{:S(2)}) collective-permute-start(bf16[64,4096]{1,0:T(8,128)(2,1)} %get-tuple-element.59), channel_id=1, source_target_pairs={{0,6},{2,0},{4,2},{6,4},{1,7},{3,1},{5,3},{7,5},{8,14},{10,8},{12,... | collective-permute-start | bytes 1572872 | tf_op jit(solution)/shard_map/ppermute | solution.py:325
  75.7 0.1 reduce_sum.31
  75.7 0.9 collective-permute-start.10
  76.6 4.3 %collective-permute-done.10 = f32[128,128]{1,0:T(8,128)S(1)} collective-permute-done((f32[128,128]{1,0:T(8,128)S(1)}, f32[128,128]{1,0:T(8,128)S(1)}, u32[]{:S(2)}, u32[]{:S(2)}) %collective-permute-start.10) | collective-permute-done | bytes 65568 | tf_op jit(solution)/shard_map/ppermute | solution.py:320
  80.9 2.2 %collective-permute-start.11 = (f32[128,128]{1,0:T(8,128)S(1)}, f32[128,128]{1,0:T(8,128)S(1)}, u32[]{:S(2)}, u32[]{:S(2)}) collective-permute-start(f32[128,128]{1,0:T(8,128)S(1)} %add.101), channel_id=1, source_target_pairs={{0,16},{8,24},{16,0},{24,8},{32,48},{40,56},{48,32},{56,40},{1,17}... | collective-permute-start | bytes 196616 | tf_op jit(solution)/shard_map/ppermute | solution.py:320
  83.1 5.9 %collective-permute-done.11 = f32[128,128]{1,0:T(8,128)S(1)} collective-permute-done((f32[128,128]{1,0:T(8,128)S(1)}, f32[128,128]{1,0:T(8,128)S(1)}, u32[]{:S(2)}, u32[]{:S(2)}) %collective-permute-start.11) | collective-permute-done | bytes 65568 | tf_op jit(solution)/shard_map/ppermute | solution.py:320
  89.0 5.3 %collective-permute-start.12 = (f32[128,128]{1,0:T(8,128)S(1)}, f32[128,128]{1,0:T(8,128)S(1)}, u32[]{:S(2)}, u32[]{:S(2)}) collective-permute-start(f32[128,128]{1,0:T(8,128)S(1)} %add.102), channel_id=1, source_target_pairs={{0,32},{8,40},{16,48},{24,56},{32,0},{40,8},{48,16},{56,24},{1,33}... | collective-permute-start | bytes 196616 | tf_op jit(solution)/shard_map/ppermute | solution.py:320
  94.2 3.1 %collective-permute-done.12 = f32[128,128]{1,0:T(8,128)S(1)} collective-permute-done((f32[128,128]{1,0:T(8,128)S(1)}, f32[128,128]{1,0:T(8,128)S(1)}, u32[]{:S(2)}, u32[]{:S(2)}) %collective-permute-start.12) | collective-permute-done | bytes 65568 | tf_op jit(solution)/shard_map/ppermute | solution.py:320
  97.4 0.0 collective-permute-done.8
  97.4 1.1 broadcast_in_dim.14
  98.5 5.6 %all-to-all-start.2 = ((f32[16,128,128]{2,1,0:T(8,128)}), f32[16,128,128]{2,1,0:T(8,128)S(1)}, u32[]{:S(2)}, u32[]{:S(2)}) async-start(f32[16,128,128]{2,1,0:T(8,128)} %broadcast_in_dim.14), calls=%async_computation.2 | async-start | bytes 2097152 | tf_op jit(solution)/shard_map/all_to_all | solution.py:383
  104.1 2.4 %fusion.1 = bf16[64,4096]{1,0:T(8,128)(2,1)} fusion(bf16[64,4096]{1,0:T(8,128)(2,1)} %collective-permute-done.9, bf16[64,4096]{1,0:T(8,128)(2,1)} %collective-permute-done.8, bf16[4,64,4096]{2,1,0:T(8,128)(2,1)} %bitcast.49, s32[]{:T(128)S(6)} %select_n.57), kind=kLoop, calls=%fused_computation.4 | loop fusion | flops 1572864 | bytes 2097156 | tf_op jit(solution)/shard_map/convert_element_type | solution.py:388
  106.5 9.7 %shard_map.115 = (f32[4096,256]{1,0:T(8,128)}, bf16[256,4096]{1,0:T(8,128)(2,1)}, bf16[256,4096]{1,0:T(8,128)(2,1)}) custom-call(f32[1]{0:T(128)S(6)} %div.3.inv_ref, bf16[512,4096]{1,0:T(8,128)(2,1)} %all-gather.2.cloned.1.call-done.feat_ref, bf16[512,256]{1,0:T(8,128)(2,1)} %get-tuple-element.63.dpre_ref, bf16[4096,256]{1,0:T(8,128)(2,1)} %error_ref.2), custom_call_target="tpu_custom_call" | custom-call | flops 2000000000 | bytes 16000000 | tf_op jit(solution)/shard_map/pallas_call | solution.py:168
  116.1 0.1 collective-permute-start.14
  116.2 5.4 %all-to-all-start.3 = ((bf16[8,8,4096]{2,1,0:T(8,128)(2,1)}), bf16[8,8,4096]{2,1,0:T(8,128)(2,1)}, u32[]{:S(2)}, u32[]{:S(2)}) async-start(bf16[8,8,4096]{2,1,0:T(8,128)(2,1)} %bitcast.51), calls=%async_computation.3 | async-start | bytes 1048576 | tf_op jit(solution)/shard_map/all_to_all | solution.py:392
  121.6 1.8 %fusion.13 = f32[128,128]{1,0:T(8,128)S(1)} fusion(f32[2048,128]{1,0:T(8,128)S(1)} %bitcast.43), kind=kOutput, calls=%fused_computation.25 | convolution fusion | flops 402653184 | bytes 1114112 | tf_op jit(solution)/shard_map/dot_general | solution.py:393
  123.4 0.3 collective-permute-start.13
  123.7 1.1 collective-permute-done.13
  124.8 4.3 %shard_map.117 = f32[256,128]{1,0:T(8,128)} custom-call(s32[1]{0:T(128)} %bitcast.3.core_ref, bf16[256,4096]{1,0:T(8,128)(2,1)} %get-tuple-element.69.head_ref, bf16[256,4096]{1,0:T(8,128)(2,1)} %get-tuple-element.70.rest_ref, f32[2048,128]{1,0:T(8,128)} %bitcast.44, f32[2048,128]{1,0:T(8,128)} %collective-permute-done.14.other_ref), custom_call_target="tpu_custom_call" | custom-call | flops 1000000000 | bytes 6000000 | tf_op jit(solution)/shard_map/pallas_call | solution.py:213
  129.1 1.5 collective-permute-start.15
  130.6 5.0 %shard_map.116.inverse_ref = f32[128,128]{1,0:T(8,128)S(1)} custom-call(f32[128,128]{1,0:T(8,128)S(1)} %add.106.gram_ref), custom_call_target="tpu_custom_call" | custom-call | flops 10000000 | bytes 100000 | tf_op jit(solution)/shard_map/pallas_call | solution.py:256
  135.6 0.6 copy-done.1
  136.2 0.0 collective-permute-done.15
  136.2 0.9 add.107.right_ref
  137.2 2.8 %collective-permute-start.16 = (f32[256,128]{1,0:T(8,128)S(1)}, f32[256,128]{1,0:T(8,128)S(1)}, u32[]{:S(2)}, u32[]{:S(2)}) collective-permute-start(f32[256,128]{1,0:T(8,128)S(1)} %add.107.right_ref), channel_id=1, source_target_pairs={{0,128},{64,192},{128,0},{192,64},{1,129},{65,193},{129,1},{193,65... | collective-permute-start | bytes 393224 | tf_op jit(solution)/shard_map/ppermute | solution.py:320
  139.9 0.0 all-to-all-done.3
  139.9 1.8 %reduce_sum.32 = bf16[8,4096]{1,0:T(8,128)(2,1)} reduce(bf16[8,8,4096]{2,1,0:T(8,128)(2,1)} %all-to-all-done.3, bf16[]{:T(256)} %constant.61.clone.1), dimensions={0}, to_apply=%region_2.3 | reduce | flops 229376 | bytes 589826 | tf_op jit(solution)/shard_map/reduce_sum | solution.py:401
  141.7 2.4 %collective-permute-done.16.got_ref = f32[256,128]{1,0:T(8,128)S(1)} collective-permute-done((f32[256,128]{1,0:T(8,128)S(1)}, f32[256,128]{1,0:T(8,128)S(1)}, u32[]{:S(2)}, u32[]{:S(2)}) %collective-permute-start.16) | collective-permute-done | bytes 131104 | tf_op jit(solution)/shard_map/ppermute | solution.py:320
  144.1 0.7 copy-done.7
  144.7 5.8 %shard_map.118 = (bf16[4096,256]{1,0:T(8,128)(2,1)}, f32[256,128]{1,0:T(8,128)}) custom-call(s32[1]{0:T(128)} %bitcast.3.core_ref, f32[4096,256]{1,0:T(8,128)} %get-tuple-element.74.merged_ref, f32[2048,128]{1,0:T(8,128)} %bitcast.45, f32[2048,128]{1,0:T(8,128)} %collective-permute-done.14.other_ref, f32[256,128]{1,0:T(8,128)} %copy-done.5, ...), custom_call_target="tpu_custom_call" | custom-call | flops 1000000000 | bytes 8000000 | tf_op jit(solution)/shard_map/pallas_call | solution.py:289
  (27 shorter events, 0.1 us)
Async XLA Ops:
  7.2 7.9 %copy-start = (bf16[4096,256]{1,0:T(8,128)(2,1)S(1)}, bf16[4096,256]{1,0:T(8,128)(2,1)}, u32[]{:S(2)}) copy-start(bf16[4096,256]{1,0:T(8,128)(2,1)} %param.12) | copy-start | bytes 6291460
  7.2 99.3 %all-gather.2.cloned.1.call-start = ((), (), s32[]{:S(2)}) async-start(), calls=%async_computation.4 | async-start | bytes 4259840 | tf_op jit(solution)/shard_map/all_gather | solution.py:341
  8.6 5.8 %collective-permute-start = (f32[1]{0:T(128)}, f32[1]{0:T(128)}, u32[]{:S(2)}, u32[]{:S(2)}) collective-permute-start(f32[1]{0:T(128)} %convert_element_type.29), channel_id=1, source_target_pairs={{0,64},{64,0},{128,192},{192,128},{1,65},{65,1},{129,193},{193,129... | collective-permute-start | bytes 20 | tf_op jit(solution)/shard_map/ppermute | solution.py:320
  15.0 3.0 %copy-start.6 = (bf16[8,4096]{1,0:T(8,128)(2,1)S(1)}, bf16[8,4096]{1,0:T(8,128)(2,1)}, u32[]{:S(2)}) copy-start(bf16[8,4096]{1,0:T(8,128)(2,1)} %param.9) | copy-start | bytes 196612
  18.0 21.3 %collective-permute-start.4 = (bf16[256,4096]{1,0:T(8,128)(2,1)}, bf16[256,4096]{1,0:T(8,128)(2,1)}, u32[]{:S(2)}, u32[]{:S(2)}) collective-permute-start(bf16[256,4096]{1,0:T(8,128)(2,1)} %convolution_convert_fusion), channel_id=1, source_target_pairs={{0,1},{1,0},{2,3},{3,2},{4,5},{5,4},{6,7},{7,6},{8,9},{9,8},{10,11... | collective-permute-start | bytes 6291464 | tf_op jit(solution)/shard_map/ppermute | solution.py:320
  18.1 20.7 %collective-permute-start.3 = (bf16[8,2048]{1,0:T(8,128)(2,1)S(1)}, bf16[8,2048]{1,0:T(8,128)(2,1)S(1)}, u32[]{:S(2)}, u32[]{:S(2)}) collective-permute-start(bf16[8,2048]{1,0:T(8,128)(2,1)S(1)} %get-tuple-element.86), channel_id=1, source_target_pairs={{0,1},{1,0},{2,3},{3,2},{4,5},{5,4},{6,7},{7,6},{8,9},{9,8},{10,11... | collective-permute-start | bytes 98312 | tf_op jit(solution)/shard_map/ppermute | solution.py:320
  18.6 19.3 %collective-permute-start.1 = (f32[1]{0:T(128)}, f32[1]{0:T(128)}, u32[]{:S(2)}, u32[]{:S(2)}) collective-permute-start(f32[1]{0:T(128)} %add.82), channel_id=1, source_target_pairs={{0,128},{64,192},{128,0},{192,64},{1,129},{65,193},{129,1},{193,65... | collective-permute-start | bytes 20 | tf_op jit(solution)/shard_map/ppermute | solution.py:320
  22.7 23.0 %all-to-all-start = ((f32[32,16,128]{2,1,0:T(8,128)}), f32[32,16,128]{2,1,0:T(8,128)S(1)}, u32[]{:S(2)}, u32[]{:S(2)}) async-start(f32[32,16,128]{2,1,0:T(8,128)} %bitcast.2), calls=%async_computation | async-start | bytes 524288 | tf_op jit(solution)/shard_map/all_to_all | solution.py:357
  38.0 7.7 %collective-permute-start.2 = (f32[2048,128]{1,0:T(8,128)}, f32[2048,128]{1,0:T(8,128)S(1)}, u32[]{:S(2)}, u32[]{:S(2)}) collective-permute-start(f32[2048,128]{1,0:T(8,128)} %get-tuple-element.46), channel_id=1, source_target_pairs={{0,1},{1,0},{2,3},{3,2},{4,5},{5,4},{6,7},{7,6},{8,9},{9,8},{10,11... | collective-permute-start | bytes 3145736 | tf_op jit(solution)/shard_map/ppermute | solution.py:320
  41.8 1.3 copy-start.3
  45.7 2.3 %copy-start.4 = (f32[2048,128]{1,0:T(8,128)}, f32[2048,128]{1,0:T(8,128)S(1)}, u32[]{:S(2)}) copy-start(f32[2048,128]{1,0:T(8,128)S(1)} %collective-permute-done.2.got_ref) | copy-start | bytes 3145732
  45.7 2.3 %copy-start.8 = (f32[16,128]{1,0:T(8,128)}, f32[16,128]{1,0:T(8,128)S(1)}, u32[]{:S(2)}) copy-start(f32[16,128]{1,0:T(8,128)S(1)} %reduce_sum.30.share_ref) | copy-start | bytes 24580
  45.7 2.3 %collective-permute-start.5 = (f32[16,128]{1,0:T(8,128)S(1)}, f32[16,128]{1,0:T(8,128)S(1)}, u32[]{:S(2)}, u32[]{:S(2)}) collective-permute-start(f32[16,128]{1,0:T(8,128)S(1)} %reduce_sum.30.share_ref), channel_id=1, source_target_pairs={{0,1},{1,0},{2,3},{3,2},{4,5},{5,4},{6,7},{7,6},{8,9},{9,8},{10,11... | collective-permute-start | bytes 24584 | tf_op jit(solution)/shard_map/ppermute | solution.py:320
  45.8 12.5 %collective-permute-start.7 = (bf16[32,4096]{1,0:T(8,128)(2,1)}, bf16[32,4096]{1,0:T(8,128)(2,1)S(1)}, u32[]{:S(2)}, u32[]{:S(2)}) collective-permute-start(bf16[32,4096]{1,0:T(8,128)(2,1)} %get-tuple-element.56), channel_id=1, source_target_pairs={{0,6},{2,0},{4,2},{6,4},{1,7},{3,1},{5,3},{7,5},{8,14},{10,8},{12,... | collective-permute-start | bytes 786440 | tf_op jit(solution)/shard_map/ppermute | solution.py:325
  48.0 10.3 %collective-permute-start.6 = (bf16[32,4096]{1,0:T(8,128)(2,1)}, bf16[32,4096]{1,0:T(8,128)(2,1)}, u32[]{:S(2)}, u32[]{:S(2)}) collective-permute-start(bf16[32,4096]{1,0:T(8,128)(2,1)} %get-tuple-element.55), channel_id=1, source_target_pairs={{0,2},{2,4},{4,6},{6,0},{1,3},{3,5},{5,7},{7,1},{8,10},{10,12},{12... | collective-permute-start | bytes 786440 | tf_op jit(solution)/shard_map/ppermute | solution.py:325
  48.0 0.6 copy-start.9
  51.3 22.3 %all-to-all-start.1 = ((f32[16,128,128]{2,1,0:T(8,128)}), f32[16,128,128]{2,1,0:T(8,128)S(1)}, u32[]{:S(2)}, u32[]{:S(2)}) async-start(f32[16,128,128]{2,1,0:T(8,128)} %bitcast.50), calls=%async_computation.1 | async-start | bytes 2097152 | tf_op jit(solution)/shard_map/all_to_all | solution.py:374
  73.6 23.8 %collective-permute-start.8 = (bf16[64,4096]{1,0:T(8,128)(2,1)}, bf16[64,4096]{1,0:T(8,128)(2,1)}, u32[]{:S(2)}, u32[]{:S(2)}) collective-permute-start(bf16[64,4096]{1,0:T(8,128)(2,1)} %get-tuple-element.58), channel_id=1, source_target_pairs={{0,2},{2,4},{4,6},{6,0},{1,3},{3,5},{5,7},{7,1},{8,10},{10,12},{12... | collective-permute-start | bytes 1572872 | tf_op jit(solution)/shard_map/ppermute | solution.py:325
  73.7 23.7 %collective-permute-start.9 = (bf16[64,4096]{1,0:T(8,128)(2,1)}, bf16[64,4096]{1,0:T(8,128)(2,1)}, u32[]{:S(2)}, u32[]{:S(2)}) collective-permute-start(bf16[64,4096]{1,0:T(8,128)(2,1)} %get-tuple-element.59), channel_id=1, source_target_pairs={{0,6},{2,0},{4,2},{6,4},{1,7},{3,1},{5,3},{7,5},{8,14},{10,8},{12,... | collective-permute-start | bytes 1572872 | tf_op jit(solution)/shard_map/ppermute | solution.py:325
  75.7 5.2 %collective-permute-start.10 = (f32[128,128]{1,0:T(8,128)S(1)}, f32[128,128]{1,0:T(8,128)S(1)}, u32[]{:S(2)}, u32[]{:S(2)}) collective-permute-start(f32[128,128]{1,0:T(8,128)S(1)} %reduce_sum.31), channel_id=1, source_target_pairs={{0,8},{8,0},{16,24},{24,16},{32,40},{40,32},{48,56},{56,48},{1,9},... | collective-permute-start | bytes 196616 | tf_op jit(solution)/shard_map/ppermute | solution.py:320
  80.9 8.0 %collective-permute-start.11 = (f32[128,128]{1,0:T(8,128)S(1)}, f32[128,128]{1,0:T(8,128)S(1)}, u32[]{:S(2)}, u32[]{:S(2)}) collective-permute-start(f32[128,128]{1,0:T(8,128)S(1)} %add.101), channel_id=1, source_target_pairs={{0,16},{8,24},{16,0},{24,8},{32,48},{40,56},{48,32},{56,40},{1,17}... | collective-permute-start | bytes 196616 | tf_op jit(solution)/shard_map/ppermute | solution.py:320
  89.0 8.4 %collective-permute-start.12 = (f32[128,128]{1,0:T(8,128)S(1)}, f32[128,128]{1,0:T(8,128)S(1)}, u32[]{:S(2)}, u32[]{:S(2)}) collective-permute-start(f32[128,128]{1,0:T(8,128)S(1)} %add.102), channel_id=1, source_target_pairs={{0,32},{8,40},{16,48},{24,56},{32,0},{40,8},{48,16},{56,24},{1,33}... | collective-permute-start | bytes 196616 | tf_op jit(solution)/shard_map/ppermute | solution.py:320
  98.5 17.6 %all-to-all-start.2 = ((f32[16,128,128]{2,1,0:T(8,128)}), f32[16,128,128]{2,1,0:T(8,128)S(1)}, u32[]{:S(2)}, u32[]{:S(2)}) async-start(f32[16,128,128]{2,1,0:T(8,128)} %broadcast_in_dim.14), calls=%async_computation.2 | async-start | bytes 2097152 | tf_op jit(solution)/shard_map/all_to_all | solution.py:383
  116.1 8.7 %copy-start.2 = (f32[16,128,128]{2,1,0:T(8,128)}, f32[16,128,128]{2,1,0:T(8,128)S(1)}, u32[]{:S(2)}) copy-start(f32[16,128,128]{2,1,0:T(8,128)S(1)} %all-to-all-done.2) | copy-start | bytes 3145732
  116.1 8.6 %collective-permute-start.14 = (f32[2048,128]{1,0:T(8,128)S(1)}, f32[2048,128]{1,0:T(8,128)}, u32[]{:S(2)}, u32[]{:S(2)}) collective-permute-start(f32[2048,128]{1,0:T(8,128)S(1)} %bitcast.42), channel_id=1, source_target_pairs={{0,1},{1,0},{2,3},{3,2},{4,5},{5,4},{6,7},{7,6},{8,9},{9,8},{10,11... | collective-permute-start | bytes 3145736 | tf_op jit(solution)/shard_map/ppermute | solution.py:320
  116.2 23.7 %all-to-all-start.3 = ((bf16[8,8,4096]{2,1,0:T(8,128)(2,1)}), bf16[8,8,4096]{2,1,0:T(8,128)(2,1)}, u32[]{:S(2)}, u32[]{:S(2)}) async-start(bf16[8,8,4096]{2,1,0:T(8,128)(2,1)} %bitcast.51), calls=%async_computation.3 | async-start | bytes 1048576 | tf_op jit(solution)/shard_map/all_to_all | solution.py:392
  123.4 1.3 collective-permute-start.13
  129.1 7.1 %collective-permute-start.15 = (f32[256,128]{1,0:T(8,128)}, f32[256,128]{1,0:T(8,128)S(1)}, u32[]{:S(2)}, u32[]{:S(2)}) collective-permute-start(f32[256,128]{1,0:T(8,128)} %shard_map.117), channel_id=1, source_target_pairs={{0,64},{64,0},{128,192},{192,128},{1,65},{65,1},{129,193},{193,129... | collective-permute-start | bytes 393224 | tf_op jit(solution)/shard_map/ppermute | solution.py:320
  135.6 0.6 copy-start.1
  137.1 6.9 %copy-start.5 = (f32[256,128]{1,0:T(8,128)}, f32[256,128]{1,0:T(8,128)S(1)}, u32[]{:S(2)}) copy-start(f32[256,128]{1,0:T(8,128)S(1)} %add.107.right_ref) | copy-start | bytes 393220
  137.2 6.9 %collective-permute-start.16 = (f32[256,128]{1,0:T(8,128)S(1)}, f32[256,128]{1,0:T(8,128)S(1)}, u32[]{:S(2)}, u32[]{:S(2)}) collective-permute-start(f32[256,128]{1,0:T(8,128)S(1)} %add.107.right_ref), channel_id=1, source_target_pairs={{0,128},{64,192},{128,0},{192,64},{1,129},{65,193},{129,1},{193,65... | collective-permute-start | bytes 393224 | tf_op jit(solution)/shard_map/ppermute | solution.py:320
  144.1 0.7 copy-start.7
Sparse Core Ops, SparseCore 0:
  10.8 85.7 all-gather.1

commit v5 on v4

--- a/solution.py
+++ b/solution.py
@@ -164,7 +164,7 @@
 def merge_part(inv_mean, features, dpre, error):
     tokens, width = features.shape
     cols = dpre.shape[1]
-    step = 512
+    step = 2048
     return pl.pallas_call(
         merge_kernel,
         out_shape=(
@@ -350,7 +350,7 @@
     count, share, error_late, rows = tie((count, share, error, rows))
     err_give, err_keep = error_part(core, error_late, basis)
     err_got = swap(err_give, "c", 1)
-    inv_mean = n_inter / (count + swap(count, "x", 2))
+    inv_mean = n_inter / (count + swap(count, "x", 3))
 
     rows = rows.reshape(2, -1, cols)
     got = swap(mm(pick(rows, 1 - c), weight, ((1,), (1,))).astype(BF16), "c", 1)
@@ -376,7 +376,7 @@
 
     up, down = shift(after, "y", 1), shift(before, "y", -1)
     part = part.reshape(n_inter * n_y, -1, rank).sum(0)
-    for bit in (1, 2, 4):
+    for bit in (1, 2, 7):
         part = part + swap(part, "z", bit)
     up, down, part = tie((up, down, part))
 
@@ -390,17 +390,17 @@
 
     other = swap(mine, "c", 1)
     grad = lax.all_to_all(grad, "z", 0, 0, tiled=True)
+    right = right_part(core, head, rest, mine, other)
+    right_got = swap(right, "x", 1)
+    right, mine = tie((right, mine))
     gram = jnp.dot(mine.T, mine, precision=HIGHEST)
     gram = gram + swap(gram, "c", 1)
-    gram, other = tie((gram, other))
-    right = right_part(core, head, rest, mine, other)
+    gram, right = tie((gram, right + right_got))
+    right_got = swap(right, "x", 3)
     inverse = inverse_part(gram)
-    right = right + swap(right, "x", 1)
-    inverse, right = tie((inverse, right))
-    right_got = swap(right, "x", 2)
+    new_error, new_basis = last_part(core, merged, mine, other, right, right_got, inverse)
+    grad, new_basis = tie((grad, new_basis))
     grad = grad.reshape(n_z, -1, width).astype(F32).sum(0).astype(BF16)
-    grad, right_got = tie((grad, right_got))
-    new_error, new_basis = last_part(core, merged, mine, other, right, right_got, inverse)
     return grad, new_error, new_basis
 
 

time: 158 us -> 153 us (0.968)
  starting transfers between devices: 53.4 us -> 42.9 us
  waiting for transfers between devices: 32.1 us -> 38.9 us
  Pallas kernels: 34 us -> 30.8 us
    ppermute x13, starting transfers between devices: 20.6 us -> 10.7 us  [swap(): return lax.ppermute(value, axis, [(i, i ^ bit) for i in range(n)])]
    all_to_all x1, waiting for transfers between devices: 0.01 us -> 3.92 us  [per_device(): lax.all_to_all(jnp.broadcast_to(part[None], (n_inter * n_y,) + part.shape...]
    pallas_call x1, Pallas kernels: 9.66 us -> 6.45 us  [merge_part(): pl.pallas_call(merge_kernel, out_shape=(jax.ShapeDtypeStruct((width, cols...]
    ppermute x13, waiting for transfers between devices: 16.7 us -> 19.4 us  [swap(): return lax.ppermute(value, axis, [(i, i ^ bit) for i in range(n)])]
    unnamed x20 -> x22, local copies, waits for them, and re-layouts: 3.2 us -> 3.21 us
  transfers between devices with their start and end apart: 22 -> 22, of which waited for: 7 -> 8; matrix products, arithmetic and copies ran while one was open for 12% -> 11% of each run, Pallas kernels for 18% -> 20%
where the time goes in v5:
time: 153 us; the launch traced here: 151 us
  starting transfers between devices  42.9 us (28%)
  waiting for transfers between devices  38.9 us (25%)
  Pallas kernels  30.8 us (20%)
  between operations  16.3 us (11%)
  matrix products  8.81 us (6%)
  other arithmetic  7.22 us (5%)
  local copies, waits for them, and re-layouts  6.18 us (4%)
    ppermute x13, waiting for transfers between devices, swap(): return lax.ppermute(value, axis, [(i, i ^ bit) for i in range(n)])  19.4 us
    all_to_all x1, waiting for transfers between devices, per_device(): part = lax.all_to_all(part, ('x', 'y'), 0, 0, tiled=True)  13 us
    all_to_all x1, starting transfers between devices, per_device(): lax.all_to_all(share, ('z', 'y'), 0, 0, tiled=True)  11.7 us
    ppermute x13, starting transfers between devices, swap(): return lax.ppermute(value, axis, [(i, i ^ bit) for i in range(n)])  10.7 us
    pallas_call x1, Pallas kernels, merge_part(): pl.pallas_call(merge_kernel, out_shape=(jax.ShapeDtypeStruct((width, cols...  6.45 us
    all_to_all x1, starting transfers between devices, per_device(): part = lax.all_to_all(part, ('x', 'y'), 0, 0, tiled=True)  6.04 us
    pallas_call x1, Pallas kernels, last_part(): pl.pallas_call(last_kernel, out_shape=(jax.ShapeDtypeStruct((width, cols)...  5.78 us
    all_to_all x1, starting transfers between devices, per_device(): grad = lax.all_to_all(grad, 'z', 0, 0, tiled=True)  5.49 us
  transfers between devices with their start and end apart: 22, of which 8 were waited for; matrix products, arithmetic and copies ran while one was open for 11% of the time, Pallas kernels for 20%

profile of v5, /device:TPU:8, one launch (start us, length us, event | category | flops | bytes accessed | tf_op | source)
XLA Modules:
  0.0 151.1 jit_solution(1102101892726801138)
XLA Ops:
  7.2 0.0 copy-start
  7.2 0.0 all-gather.2.cloned.1.call-start
  7.2 0.7 all-gather.2.cloned.1.call-update
  8.6 2.9 %collective-permute-start = (f32[1]{0:T(128)}, f32[1]{0:T(128)}, u32[]{:S(2)}, u32[]{:S(2)}) collective-permute-start(f32[1]{0:T(128)} %convert_element_type.29), channel_id=1, source_target_pairs={{0,64},{64,0},{128,192},{192,128},{1,65},{65,1},{129,193},{193,129... | collective-permute-start | bytes 20 | tf_op jit(solution)/shard_map/ppermute | solution.py:320
  11.4 2.9 %shard_map.112 = (bf16[512,256]{1,0:T(8,128)(2,1)}, bf16[512,256]{1,0:T(8,128)(2,1)}, f32[512,128]{1,0:T(8,128)}) custom-call(s32[1]{0:T(128)S(6)} %copy.12.count_ref, s32[2,512]{1,0:T(2,128)} %bitcast.57, f32[1,512]{1,0:T(1,128)} %bitcast.58, bf16[512,256]{1,0:T(8,128)(2,1)} %up_ref.1, bf16[512,256]{1,0:T(8,128)(2,1)} %pre_ref.1, f32[256,128]{1,0:T(8,128)} %basis_ref.3), custom_call_target="tpu_custom_call" | custom-call | flops 100000 | bytes 10000 | tf_op jit(solution)/shard_map/pallas_call | solution.py:76
  15.0 0.0 copy-start.7
  15.0 3.0 %convolution_convert_fusion = bf16[256,4096]{1,0:T(8,128)(2,1)} fusion(bf16[4096,256]{1,0:T(8,128)(2,1)S(1)} %copy-done, bf16[2,256,256]{2,1,0:T(8,128)(2,1)} %bitcast.55, s32[]{:T(128)S(6)} %select_n.54), kind=kOutput, calls=%fused_computation | convolution fusion | flops 537919488 | bytes 4325380 | tf_op jit(solution)/shard_map/dot_general | solution.py:26
  18.0 0.0 collective-permute-start.4
  18.0 0.6 collective-permute-start.3
  18.6 3.4 %collective-permute-start.1 = (f32[1]{0:T(128)}, f32[1]{0:T(128)}, u32[]{:S(2)}, u32[]{:S(2)}) collective-permute-start(f32[1]{0:T(128)} %add.82), channel_id=1, source_target_pairs={{0,192},{64,128},{128,64},{192,0},{1,193},{65,129},{129,65},{193,1... | collective-permute-start | bytes 20 | tf_op jit(solution)/shard_map/ppermute | solution.py:320
  22.0 11.7 %all-to-all-start = ((f32[32,16,128]{2,1,0:T(8,128)}), f32[32,16,128]{2,1,0:T(8,128)S(1)}, u32[]{:S(2)}, u32[]{:S(2)}) async-start(f32[32,16,128]{2,1,0:T(8,128)} %bitcast.2), calls=%async_computation | async-start | bytes 524288 | tf_op jit(solution)/shard_map/all_to_all | solution.py:357
  33.7 3.6 %shard_map.113 = (f32[2048,128]{1,0:T(8,128)}, f32[2048,128]{1,0:T(8,128)}) custom-call(s32[1]{0:T(128)} %bitcast.3.core_ref, bf16[4096,256]{1,0:T(8,128)(2,1)} %error_ref.2, f32[256,128]{1,0:T(8,128)} %basis_ref.3), custom_call_target="tpu_custom_call" | custom-call | flops 100000 | bytes 10000 | tf_op jit(solution)/shard_map/pallas_call | solution.py:106
  37.3 0.0 collective-permute-start.2
  38.1 0.0 collective-permute-done.3
  38.1 0.6 maximum_select_fusion.feat_ref
  38.7 2.4 %add_convert_fusion = bf16[256,4096]{1,0:T(8,128)(2,1)S(1)} fusion(bf16[256,4096]{1,0:T(8,128)(2,1)} %collective-permute-done.4, bf16[4096,256]{1,0:T(8,128)(2,1)S(1)} %copy-done, bf16[2,256,256]{2,1,0:T(8,128)(2,1)} %bitcast.56, s32[]{:T(128)S(6)} %select_n.53), kind=kOutput, calls=%fused_computation.1 | convolution fusion | flops 540016640 | bytes 6422532 | tf_op jit(solution)/shard_map/dot_general | solution.py:26
  41.2 0.0 copy-start.3
  41.2 1.3 copy-done.3
  42.5 0.8 dynamic-slice_bitcast_fusion.4
  43.3 1.9 %all-to-all-done = f32[32,16,128]{2,1,0:T(8,128)S(1)} async-done(((f32[32,16,128]{2,1,0:T(8,128)}), f32[32,16,128]{2,1,0:T(8,128)S(1)}, u32[]{:S(2)}, u32[]{:S(2)}) %all-to-all-start) | async-done | bytes 262176 | tf_op jit(solution)/shard_map/all_to_all | solution.py:357
  45.2 0.0 collective-permute-done.2.got_ref
  45.3 0.0 copy-start.9
  45.3 0.1 collective-permute-start.5
  45.4 1.7 %collective-permute-start.7 = (bf16[32,4096]{1,0:T(8,128)(2,1)}, bf16[32,4096]{1,0:T(8,128)(2,1)S(1)}, u32[]{:S(2)}, u32[]{:S(2)}) collective-permute-start(bf16[32,4096]{1,0:T(8,128)(2,1)} %get-tuple-element.56), channel_id=1, source_target_pairs={{0,6},{2,0},{4,2},{6,4},{1,7},{3,1},{5,3},{7,5},{8,14},{10,8},{12,... | collective-permute-start | bytes 786440 | tf_op jit(solution)/shard_map/ppermute | solution.py:325
  47.2 0.4 collective-permute-start.6
  47.6 0.6 copy-done.10
  48.2 2.7 %shard_map.114 = f32[2048,128]{1,0:T(8,128)} custom-call(f32[1]{0:T(128)S(6)} %div.3.inv_ref, f32[16,128]{1,0:T(8,128)} %copy-done.9, f32[16,128]{1,0:T(8,128)} %copy-done.10, bf16[16,2048]{1,0:T(8,128)(2,1)} %maximum_select_fusion.feat_ref, f32[2048,128]{1,0:T(8,128)} %get-tuple-element.52.keep_ref, f32[2048,128]{1,0:T(8,128)} %copy-done.4), custom_call_target="tpu_custom_call" | custom-call | flops 100000000 | bytes 4000000 | tf_op jit(solution)/shard_map/pallas_call | solution.py:137
  50.9 6.0 %all-to-all-start.1 = ((f32[16,128,128]{2,1,0:T(8,128)}), f32[16,128,128]{2,1,0:T(8,128)S(1)}, u32[]{:S(2)}, u32[]{:S(2)}) async-start(f32[16,128,128]{2,1,0:T(8,128)} %bitcast.53), calls=%async_computation.1 | async-start | bytes 2097152 | tf_op jit(solution)/shard_map/all_to_all | solution.py:374
  57.0 1.1 dynamic-slice_bitcast_fusion.1
  58.0 0.0 collective-permute-done.7
  58.0 1.2 fusion.2
  59.3 1.1 pad_maximum_fusion
  60.4 13.0 %all-to-all-done.1 = f32[16,128,128]{2,1,0:T(8,128)S(1)} async-done(((f32[16,128,128]{2,1,0:T(8,128)}), f32[16,128,128]{2,1,0:T(8,128)S(1)}, u32[]{:S(2)}, u32[]{:S(2)}) %all-to-all-start.1) | async-done | bytes 1048608 | tf_op jit(solution)/shard_map/all_to_all | solution.py:374
  73.3 0.1 collective-permute-start.8
  73.4 2.0 %collective-permute-start.9 = (bf16[64,4096]{1,0:T(8,128)(2,1)}, bf16[64,4096]{1,0:T(8,128)(2,1)}, u32[]{:S(2)}, u32[]{:S(2)}) collective-permute-start(bf16[64,4096]{1,0:T(8,128)(2,1)} %get-tuple-element.59), channel_id=1, source_target_pairs={{0,6},{2,0},{4,2},{6,4},{1,7},{3,1},{5,3},{7,5},{8,14},{10,8},{12,... | collective-permute-start | bytes 1572872 | tf_op jit(solution)/shard_map/ppermute | solution.py:325
  75.4 0.1 reduce_sum.31
  75.4 1.1 collective-permute-start.10
  76.5 4.5 %collective-permute-done.10 = f32[128,128]{1,0:T(8,128)S(1)} collective-permute-done((f32[128,128]{1,0:T(8,128)S(1)}, f32[128,128]{1,0:T(8,128)S(1)}, u32[]{:S(2)}, u32[]{:S(2)}) %collective-permute-start.10) | collective-permute-done | bytes 65568 | tf_op jit(solution)/shard_map/ppermute | solution.py:320
  81.1 0.2 collective-permute-start.11
  81.3 6.7 %collective-permute-done.11 = f32[128,128]{1,0:T(8,128)S(1)} collective-permute-done((f32[128,128]{1,0:T(8,128)S(1)}, f32[128,128]{1,0:T(8,128)S(1)}, u32[]{:S(2)}, u32[]{:S(2)}) %collective-permute-start.11) | collective-permute-done | bytes 65568 | tf_op jit(solution)/shard_map/ppermute | solution.py:320
  88.0 0.7 collective-permute-start.12
  88.7 6.0 %collective-permute-done.12 = f32[128,128]{1,0:T(8,128)S(1)} collective-permute-done((f32[128,128]{1,0:T(8,128)S(1)}, f32[128,128]{1,0:T(8,128)S(1)}, u32[]{:S(2)}, u32[]{:S(2)}) %collective-permute-start.12) | collective-permute-done | bytes 65568 | tf_op jit(solution)/shard_map/ppermute | solution.py:320
  94.7 0.0 collective-permute-done.8
  94.7 0.0 collective-permute-done.9
  94.7 1.1 broadcast_in_dim.14
  95.8 4.7 %all-to-all-start.2 = ((f32[16,128,128]{2,1,0:T(8,128)}), f32[16,128,128]{2,1,0:T(8,128)S(1)}, u32[]{:S(2)}, u32[]{:S(2)}) async-start(f32[16,128,128]{2,1,0:T(8,128)} %broadcast_in_dim.14), calls=%async_computation.2 | async-start | bytes 2097152 | tf_op jit(solution)/shard_map/all_to_all | solution.py:383
  100.5 2.4 %fusion.1 = bf16[64,4096]{1,0:T(8,128)(2,1)} fusion(bf16[64,4096]{1,0:T(8,128)(2,1)} %collective-permute-done.9, bf16[64,4096]{1,0:T(8,128)(2,1)} %collective-permute-done.8, bf16[4,64,4096]{2,1,0:T(8,128)(2,1)} %bitcast.52, s32[]{:T(128)S(6)} %select_n.57), kind=kLoop, calls=%fused_computation.4 | loop fusion | flops 1572864 | bytes 2097156 | tf_op jit(solution)/shard_map/convert_element_type | solution.py:388
  102.9 6.5 %shard_map.115 = (f32[4096,256]{1,0:T(8,128)}, bf16[256,4096]{1,0:T(8,128)(2,1)}, bf16[256,4096]{1,0:T(8,128)(2,1)}) custom-call(f32[1]{0:T(128)S(6)} %div.3.inv_ref, bf16[512,4096]{1,0:T(8,128)(2,1)} %all-gather.2.cloned.1.call-done.feat_ref, bf16[512,256]{1,0:T(8,128)(2,1)} %get-tuple-element.63.dpre_ref, bf16[4096,256]{1,0:T(8,128)(2,1)} %error_ref.2), custom_call_target="tpu_custom_call" | custom-call | flops 2000000000 | bytes 16000000 | tf_op jit(solution)/shard_map/pallas_call | solution.py:168
  109.3 3.9 %all-to-all-done.2 = f32[16,128,128]{2,1,0:T(8,128)S(1)} async-done(((f32[16,128,128]{2,1,0:T(8,128)}), f32[16,128,128]{2,1,0:T(8,128)S(1)}, u32[]{:S(2)}, u32[]{:S(2)}) %all-to-all-start.2) | async-done | bytes 1048608 | tf_op jit(solution)/shard_map/all_to_all | solution.py:383
  113.3 0.0 collective-permute-start.13
  113.3 5.5 %all-to-all-start.3 = ((bf16[8,8,4096]{2,1,0:T(8,128)(2,1)}), bf16[8,8,4096]{2,1,0:T(8,128)(2,1)}, u32[]{:S(2)}, u32[]{:S(2)}) async-start(bf16[8,8,4096]{2,1,0:T(8,128)(2,1)} %bitcast.54), calls=%async_computation.3 | async-start | bytes 1048576 | tf_op jit(solution)/shard_map/all_to_all | solution.py:392
  118.8 4.3 %shard_map.116 = f32[256,128]{1,0:T(8,128)} custom-call(s32[1]{0:T(128)} %bitcast.3.core_ref, bf16[256,4096]{1,0:T(8,128)(2,1)} %get-tuple-element.68.head_ref, bf16[256,4096]{1,0:T(8,128)(2,1)} %get-tuple-element.69.rest_ref, f32[2048,128]{1,0:T(8,128)} %bitcast.46, f32[2048,128]{1,0:T(8,128)} %collective-permute-done.13.other_ref), custom_call_target="tpu_custom_call" | custom-call | flops 1000000000 | bytes 6000000 | tf_op jit(solution)/shard_map/pallas_call | solution.py:213
  123.1 0.0 collective-permute-start.15
  123.1 3.4 %fusion.13 = f32[128,128]{1,0:T(8,128)S(1)} fusion(f32[2048,128]{1,0:T(8,128)} %bitcast.47), kind=kOutput, calls=%fused_computation.26 | convolution fusion | flops 402653184 | bytes 1114112 | tf_op jit(solution)/shard_map/dot_general | solution.py:396
  126.5 0.3 collective-permute-start.14
  126.8 1.0 collective-permute-done.14
  127.9 1.1 collective-permute-done.15
  129.0 1.5 collective-permute-start.16
  130.4 5.0 %shard_map.117.inverse_ref = f32[128,128]{1,0:T(8,128)S(1)} custom-call(f32[128,128]{1,0:T(8,128)S(1)} %add.106.gram_ref), custom_call_target="tpu_custom_call" | custom-call | flops 10000000 | bytes 100000 | tf_op jit(solution)/shard_map/pallas_call | solution.py:256
  135.4 0.0 copy-start.1
  135.5 0.6 copy-done.1
  136.1 0.6 copy-done.8
  136.7 5.8 %shard_map.118 = (bf16[4096,256]{1,0:T(8,128)(2,1)}, f32[256,128]{1,0:T(8,128)}) custom-call(s32[1]{0:T(128)} %bitcast.3.core_ref, f32[4096,256]{1,0:T(8,128)} %get-tuple-element.67.merged_ref, f32[2048,128]{1,0:T(8,128)} %bitcast.48, f32[2048,128]{1,0:T(8,128)} %collective-permute-done.13.other_ref, f32[256,128]{1,0:T(8,128)} %copy-done.6, ...), custom_call_target="tpu_custom_call" | custom-call | flops 1000000000 | bytes 8000000 | tf_op jit(solution)/shard_map/pallas_call | solution.py:289
  142.5 1.8 %bitcast_reduce_fusion = bf16[8,4096]{1,0:T(8,128)(2,1)} fusion(bf16[64,4096]{1,0:T(8,128)(2,1)} %bitcast.20), kind=kLoop, calls=%fused_computation.7 | loop fusion | flops 229376 | bytes 589824 | tf_op jit(solution)/shard_map/reduce_sum | solution.py:403
  (29 shorter events, 0.1 us)
Async XLA Ops:
  7.2 7.8 %copy-start = (bf16[4096,256]{1,0:T(8,128)(2,1)S(1)}, bf16[4096,256]{1,0:T(8,128)(2,1)}, u32[]{:S(2)}) copy-start(bf16[4096,256]{1,0:T(8,128)(2,1)} %param.12) | copy-start | bytes 6291460
  7.2 95.7 %all-gather.2.cloned.1.call-start = ((), (), s32[]{:S(2)}) async-start(), calls=%async_computation.4 | async-start | bytes 4259840 | tf_op jit(solution)/shard_map/all_gather | solution.py:341
  8.6 5.8 %collective-permute-start = (f32[1]{0:T(128)}, f32[1]{0:T(128)}, u32[]{:S(2)}, u32[]{:S(2)}) collective-permute-start(f32[1]{0:T(128)} %convert_element_type.29), channel_id=1, source_target_pairs={{0,64},{64,0},{128,192},{192,128},{1,65},{65,1},{129,193},{193,129... | collective-permute-start | bytes 20 | tf_op jit(solution)/shard_map/ppermute | solution.py:320
  15.0 3.0 %copy-start.7 = (bf16[8,4096]{1,0:T(8,128)(2,1)S(1)}, bf16[8,4096]{1,0:T(8,128)(2,1)}, u32[]{:S(2)}) copy-start(bf16[8,4096]{1,0:T(8,128)(2,1)} %param.9) | copy-start | bytes 196612
  18.0 20.7 %collective-permute-start.4 = (bf16[256,4096]{1,0:T(8,128)(2,1)}, bf16[256,4096]{1,0:T(8,128)(2,1)}, u32[]{:S(2)}, u32[]{:S(2)}) collective-permute-start(bf16[256,4096]{1,0:T(8,128)(2,1)} %convolution_convert_fusion), channel_id=1, source_target_pairs={{0,1},{1,0},{2,3},{3,2},{4,5},{5,4},{6,7},{7,6},{8,9},{9,8},{10,11... | collective-permute-start | bytes 6291464 | tf_op jit(solution)/shard_map/ppermute | solution.py:320
  18.0 20.0 %collective-permute-start.3 = (bf16[8,2048]{1,0:T(8,128)(2,1)S(1)}, bf16[8,2048]{1,0:T(8,128)(2,1)S(1)}, u32[]{:S(2)}, u32[]{:S(2)}) collective-permute-start(bf16[8,2048]{1,0:T(8,128)(2,1)S(1)} %get-tuple-element.86), channel_id=1, source_target_pairs={{0,1},{1,0},{2,3},{3,2},{4,5},{5,4},{6,7},{7,6},{8,9},{9,8},{10,11... | collective-permute-start | bytes 98312 | tf_op jit(solution)/shard_map/ppermute | solution.py:320
  18.6 18.7 %collective-permute-start.1 = (f32[1]{0:T(128)}, f32[1]{0:T(128)}, u32[]{:S(2)}, u32[]{:S(2)}) collective-permute-start(f32[1]{0:T(128)} %add.82), channel_id=1, source_target_pairs={{0,192},{64,128},{128,64},{192,0},{1,193},{65,129},{129,65},{193,1... | collective-permute-start | bytes 20 | tf_op jit(solution)/shard_map/ppermute | solution.py:320
  22.0 23.2 %all-to-all-start = ((f32[32,16,128]{2,1,0:T(8,128)}), f32[32,16,128]{2,1,0:T(8,128)S(1)}, u32[]{:S(2)}, u32[]{:S(2)}) async-start(f32[32,16,128]{2,1,0:T(8,128)} %bitcast.2), calls=%async_computation | async-start | bytes 524288 | tf_op jit(solution)/shard_map/all_to_all | solution.py:357
  37.3 7.9 %collective-permute-start.2 = (f32[2048,128]{1,0:T(8,128)}, f32[2048,128]{1,0:T(8,128)S(1)}, u32[]{:S(2)}, u32[]{:S(2)}) collective-permute-start(f32[2048,128]{1,0:T(8,128)} %get-tuple-element.46), channel_id=1, source_target_pairs={{0,1},{1,0},{2,3},{3,2},{4,5},{5,4},{6,7},{7,6},{8,9},{9,8},{10,11... | collective-permute-start | bytes 3145736 | tf_op jit(solution)/shard_map/ppermute | solution.py:320
  41.2 1.3 copy-start.3
  45.2 2.3 %copy-start.4 = (f32[2048,128]{1,0:T(8,128)}, f32[2048,128]{1,0:T(8,128)S(1)}, u32[]{:S(2)}) copy-start(f32[2048,128]{1,0:T(8,128)S(1)} %collective-permute-done.2.got_ref) | copy-start | bytes 3145732
  45.3 2.3 %copy-start.9 = (f32[16,128]{1,0:T(8,128)}, f32[16,128]{1,0:T(8,128)S(1)}, u32[]{:S(2)}) copy-start(f32[16,128]{1,0:T(8,128)S(1)} %reduce_sum.30.share_ref) | copy-start | bytes 24580
  45.3 2.3 %collective-permute-start.5 = (f32[16,128]{1,0:T(8,128)S(1)}, f32[16,128]{1,0:T(8,128)S(1)}, u32[]{:S(2)}, u32[]{:S(2)}) collective-permute-start(f32[16,128]{1,0:T(8,128)S(1)} %reduce_sum.30.share_ref), channel_id=1, source_target_pairs={{0,1},{1,0},{2,3},{3,2},{4,5},{5,4},{6,7},{7,6},{8,9},{9,8},{10,11... | collective-permute-start | bytes 24584 | tf_op jit(solution)/shard_map/ppermute | solution.py:320
  45.4 12.6 %collective-permute-start.7 = (bf16[32,4096]{1,0:T(8,128)(2,1)}, bf16[32,4096]{1,0:T(8,128)(2,1)S(1)}, u32[]{:S(2)}, u32[]{:S(2)}) collective-permute-start(bf16[32,4096]{1,0:T(8,128)(2,1)} %get-tuple-element.56), channel_id=1, source_target_pairs={{0,6},{2,0},{4,2},{6,4},{1,7},{3,1},{5,3},{7,5},{8,14},{10,8},{12,... | collective-permute-start | bytes 786440 | tf_op jit(solution)/shard_map/ppermute | solution.py:325
  47.2 10.8 %collective-permute-start.6 = (bf16[32,4096]{1,0:T(8,128)(2,1)}, bf16[32,4096]{1,0:T(8,128)(2,1)}, u32[]{:S(2)}, u32[]{:S(2)}) collective-permute-start(bf16[32,4096]{1,0:T(8,128)(2,1)} %get-tuple-element.55), channel_id=1, source_target_pairs={{0,2},{2,4},{4,6},{6,0},{1,3},{3,5},{5,7},{7,1},{8,10},{10,12},{12... | collective-permute-start | bytes 786440 | tf_op jit(solution)/shard_map/ppermute | solution.py:325
  47.6 0.6 copy-start.10
  50.9 22.4 %all-to-all-start.1 = ((f32[16,128,128]{2,1,0:T(8,128)}), f32[16,128,128]{2,1,0:T(8,128)S(1)}, u32[]{:S(2)}, u32[]{:S(2)}) async-start(f32[16,128,128]{2,1,0:T(8,128)} %bitcast.53), calls=%async_computation.1 | async-start | bytes 2097152 | tf_op jit(solution)/shard_map/all_to_all | solution.py:374
  73.3 21.4 %collective-permute-start.8 = (bf16[64,4096]{1,0:T(8,128)(2,1)}, bf16[64,4096]{1,0:T(8,128)(2,1)}, u32[]{:S(2)}, u32[]{:S(2)}) collective-permute-start(bf16[64,4096]{1,0:T(8,128)(2,1)} %get-tuple-element.58), channel_id=1, source_target_pairs={{0,2},{2,4},{4,6},{6,0},{1,3},{3,5},{5,7},{7,1},{8,10},{10,12},{12... | collective-permute-start | bytes 1572872 | tf_op jit(solution)/shard_map/ppermute | solution.py:325
  73.4 21.3 %collective-permute-start.9 = (bf16[64,4096]{1,0:T(8,128)(2,1)}, bf16[64,4096]{1,0:T(8,128)(2,1)}, u32[]{:S(2)}, u32[]{:S(2)}) collective-permute-start(bf16[64,4096]{1,0:T(8,128)(2,1)} %get-tuple-element.59), channel_id=1, source_target_pairs={{0,6},{2,0},{4,2},{6,4},{1,7},{3,1},{5,3},{7,5},{8,14},{10,8},{12,... | collective-permute-start | bytes 1572872 | tf_op jit(solution)/shard_map/ppermute | solution.py:325
  75.4 5.6 %collective-permute-start.10 = (f32[128,128]{1,0:T(8,128)S(1)}, f32[128,128]{1,0:T(8,128)S(1)}, u32[]{:S(2)}, u32[]{:S(2)}) collective-permute-start(f32[128,128]{1,0:T(8,128)S(1)} %reduce_sum.31), channel_id=1, source_target_pairs={{0,8},{8,0},{16,24},{24,16},{32,40},{40,32},{48,56},{56,48},{1,9},... | collective-permute-start | bytes 196616 | tf_op jit(solution)/shard_map/ppermute | solution.py:320
  81.1 6.9 %collective-permute-start.11 = (f32[128,128]{1,0:T(8,128)S(1)}, f32[128,128]{1,0:T(8,128)S(1)}, u32[]{:S(2)}, u32[]{:S(2)}) collective-permute-start(f32[128,128]{1,0:T(8,128)S(1)} %add.101), channel_id=1, source_target_pairs={{0,16},{8,24},{16,0},{24,8},{32,48},{40,56},{48,32},{56,40},{1,17}... | collective-permute-start | bytes 196616 | tf_op jit(solution)/shard_map/ppermute | solution.py:320
  88.0 6.7 %collective-permute-start.12 = (f32[128,128]{1,0:T(8,128)S(1)}, f32[128,128]{1,0:T(8,128)S(1)}, u32[]{:S(2)}, u32[]{:S(2)}) collective-permute-start(f32[128,128]{1,0:T(8,128)S(1)} %add.102), channel_id=1, source_target_pairs={{0,56},{8,48},{16,40},{24,32},{32,24},{40,16},{48,8},{56,0},{1,57}... | collective-permute-start | bytes 196616 | tf_op jit(solution)/shard_map/ppermute | solution.py:320
  95.8 17.5 %all-to-all-start.2 = ((f32[16,128,128]{2,1,0:T(8,128)}), f32[16,128,128]{2,1,0:T(8,128)S(1)}, u32[]{:S(2)}, u32[]{:S(2)}) async-start(f32[16,128,128]{2,1,0:T(8,128)} %broadcast_in_dim.14), calls=%async_computation.2 | async-start | bytes 2097152 | tf_op jit(solution)/shard_map/all_to_all | solution.py:383
  113.3 5.5 %copy-start.2 = (f32[16,128,128]{2,1,0:T(8,128)}, f32[16,128,128]{2,1,0:T(8,128)S(1)}, u32[]{:S(2)}) copy-start(f32[16,128,128]{2,1,0:T(8,128)S(1)} %all-to-all-done.2) | copy-start | bytes 3145732
  113.3 5.5 %collective-permute-start.13 = (f32[2048,128]{1,0:T(8,128)S(1)}, f32[2048,128]{1,0:T(8,128)}, u32[]{:S(2)}, u32[]{:S(2)}) collective-permute-start(f32[2048,128]{1,0:T(8,128)S(1)} %bitcast.45), channel_id=1, source_target_pairs={{0,1},{1,0},{2,3},{3,2},{4,5},{5,4},{6,7},{7,6},{8,9},{9,8},{10,11... | collective-permute-start | bytes 3145736 | tf_op jit(solution)/shard_map/ppermute | solution.py:320
  113.3 29.2 %all-to-all-start.3 = ((bf16[8,8,4096]{2,1,0:T(8,128)(2,1)}), bf16[8,8,4096]{2,1,0:T(8,128)(2,1)}, u32[]{:S(2)}, u32[]{:S(2)}) async-start(bf16[8,8,4096]{2,1,0:T(8,128)(2,1)} %bitcast.54), calls=%async_computation.3 | async-start | bytes 1048576 | tf_op jit(solution)/shard_map/all_to_all | solution.py:392
  123.1 5.8 %copy-start.5 = (f32[256,128]{1,0:T(8,128)S(1)}, f32[256,128]{1,0:T(8,128)}, u32[]{:S(2)}) copy-start(f32[256,128]{1,0:T(8,128)} %shard_map.116) | copy-start | bytes 393220
  123.1 5.8 %collective-permute-start.15 = (f32[256,128]{1,0:T(8,128)}, f32[256,128]{1,0:T(8,128)S(1)}, u32[]{:S(2)}, u32[]{:S(2)}) collective-permute-start(f32[256,128]{1,0:T(8,128)} %shard_map.116), channel_id=1, source_target_pairs={{0,64},{64,0},{128,192},{192,128},{1,65},{65,1},{129,193},{193,129... | collective-permute-start | bytes 393224 | tf_op jit(solution)/shard_map/ppermute | solution.py:320
  126.5 1.3 collective-permute-start.14
  129.0 7.1 %copy-start.6 = (f32[256,128]{1,0:T(8,128)}, f32[256,128]{1,0:T(8,128)S(1)}, u32[]{:S(2)}) copy-start(f32[256,128]{1,0:T(8,128)S(1)} %add.107.right_ref) | copy-start | bytes 393220
  129.0 7.1 %collective-permute-start.16 = (f32[256,128]{1,0:T(8,128)S(1)}, f32[256,128]{1,0:T(8,128)S(1)}, u32[]{:S(2)}, u32[]{:S(2)}) collective-permute-start(f32[256,128]{1,0:T(8,128)S(1)} %add.107.right_ref), channel_id=1, source_target_pairs={{0,192},{64,128},{128,64},{192,0},{1,193},{65,129},{129,65},{193,1... | collective-permute-start | bytes 393224 | tf_op jit(solution)/shard_map/ppermute | solution.py:320
  135.4 0.6 copy-start.1
  136.1 0.6 copy-start.8
Sparse Core Ops, SparseCore 0:
  10.8 85.2 all-gather.1

commit v6 on v5

--- a/solution.py
+++ b/solution.py
@@ -132,7 +132,7 @@
 def left_part(inv_mean, share, share_got, feats, keep, got):
     tokens, rank = share.shape
     half = got.shape[0]
-    step = half // 2
+    step = half
     rows = pl.BlockSpec((step, rank), lambda i: (i, 0))
     return pl.pallas_call(
         left_kernel,
@@ -147,7 +147,7 @@
             rows,
         ],
         out_specs=rows,
-        compiler_params=params(),
+        compiler_params=params(VMEM // 4),
         cost_estimate=pl.CostEstimate(flops=10**8, bytes_accessed=4 * 10**6, transcendentals=0),
     )(inv_mean, share, share_got, feats, keep, got)
 
@@ -263,7 +263,7 @@
     )(gram)
 
 
-def last_kernel(core_ref, merged_ref, own_ref, other_ref, right_ref, got_ref, inverse_ref, error_ref, basis_ref, back_ref):
+def last_kernel(core_ref, merged_ref, own_ref, other_ref, right_ref, got_ref, inverse_ref, grad_ref, error_ref, basis_ref, sum_ref, back_ref):
     def fill(left):
         out = mm_split(split(left), (back_ref[0], back_ref[1]), ((1,), (1,)))
         error_ref[...] = (merged_ref[...] - out).astype(BF16)
@@ -277,11 +277,18 @@
         back_ref[0] = head
         back_ref[1] = rest
         fill(own_ref[...])
+        rows, step = sum_ref.shape[0], 512
+        for start in range(0, sum_ref.shape[1], step):
+            blocks = grad_ref[:, start : start + step].astype(F32)
+            total = blocks[:rows]
+            for first in range(rows, blocks.shape[0], rows):
+                total = total + blocks[first : first + rows]
+            sum_ref[:, start : start + step] = total.astype(BF16)
 
     pl.when(pl.program_id(0) == 1)(lambda: fill(other_ref[...]))
 
 
-def last_part(core, merged, own, other, right, got, inverse):
+def last_part(core, merged, own, other, right, got, inverse, grad):
     width, cols = merged.shape
     half, rank = own.shape
     whole = lambda h, core: (0, 0)
@@ -291,6 +298,7 @@
         out_shape=(
             jax.ShapeDtypeStruct((width, cols), BF16),
             jax.ShapeDtypeStruct((cols, rank), F32),
+            jax.ShapeDtypeStruct((8, grad.shape[1]), BF16),
         ),
         grid_spec=pltpu.PrefetchScalarGridSpec(
             num_scalar_prefetch=1,
@@ -302,13 +310,18 @@
                 pl.BlockSpec((cols, rank), whole),
                 pl.BlockSpec((cols, rank), whole),
                 pl.BlockSpec((rank, rank), whole),
+                pl.BlockSpec(grad.shape, whole),
             ],
-            out_specs=(row, pl.BlockSpec((cols, rank), whole)),
+            out_specs=(
+                row,
+                pl.BlockSpec((cols, rank), whole),
+                pl.BlockSpec((8, grad.shape[1]), whole),
+            ),
             scratch_shapes=[pltpu.VMEM((2, cols, rank), BF16)],
         ),
         compiler_params=params(),
         cost_estimate=pl.CostEstimate(flops=10**9, bytes_accessed=8 * 10**6, transcendentals=0),
-    )(core, merged, own, other, right, got, inverse)
+    )(core, merged, own, other, right, got, inverse, grad)
 
 
 PLANE = ("z", "y", "c")
@@ -398,9 +411,9 @@
     gram, right = tie((gram, right + right_got))
     right_got = swap(right, "x", 3)
     inverse = inverse_part(gram)
-    new_error, new_basis = last_part(core, merged, mine, other, right, right_got, inverse)
-    grad, new_basis = tie((grad, new_basis))
-    grad = grad.reshape(n_z, -1, width).astype(F32).sum(0).astype(BF16)
+    new_error, new_basis, grad = last_part(
+        core, merged, mine, other, right, right_got, inverse, grad
+    )
     return grad, new_error, new_basis
 
 

time: 153 us -> 152 us (level)
  other arithmetic: 7.22 us -> 4.81 us
    reduce_sum x1 -> x0, other arithmetic: 1.76 us -> none  [per_device(): grad = grad.reshape(n_z, -1, width).astype(F32).sum(0).astype(BF16)]
    all_to_all x1, starting transfers between devices: 4.75 us -> 6.45 us  [per_device(): lax.all_to_all(jnp.broadcast_to(part[None], (n_inter * n_y,) + part.shape...]
    ppermute x13, waiting for transfers between devices: 19.4 us -> 17.7 us  [swap(): return lax.ppermute(value, axis, [(i, i ^ bit) for i in range(n)])]
    unnamed x22 -> x20, local copies, waits for them, and re-layouts: 3.21 us -> 2.61 us
  transfers between devices with their start and end apart: 22 -> 22, of which waited for: 8 -> 9; matrix products, arithmetic and copies ran while one was open for 11% -> 11% of each run, Pallas kernels for 20% -> 17%
where the time goes in v6:
time: 152 us; the launch traced here: 149 us
  starting transfers between devices  44.2 us (29%)
  waiting for transfers between devices  38.7 us (25%)
  Pallas kernels  31 us (20%)
  between operations  16.1 us (11%)
  matrix products  8.75 us (6%)
  local copies, waits for them, and re-layouts  5.57 us (4%)
  other arithmetic  4.81 us (3%)
    ppermute x13, waiting for transfers between devices, swap(): return lax.ppermute(value, axis, [(i, i ^ bit) for i in range(n)])  17.7 us
    all_to_all x1, waiting for transfers between devices, per_device(): part = lax.all_to_all(part, ('x', 'y'), 0, 0, tiled=True)  13.1 us
    all_to_all x1, starting transfers between devices, per_device(): lax.all_to_all(share, ('z', 'y'), 0, 0, tiled=True)  11.7 us
    ppermute x13, starting transfers between devices, swap(): return lax.ppermute(value, axis, [(i, i ^ bit) for i in range(n)])  11.1 us
    all_to_all x1, starting transfers between devices, per_device(): lax.all_to_all(jnp.broadcast_to(part[None], (n_inter * n_y,) + part.shape...  6.45 us
    pallas_call x1, Pallas kernels, merge_part(): pl.pallas_call(merge_kernel, out_shape=(jax.ShapeDtypeStruct((width, cols...  6.38 us
    all_to_all x1, starting transfers between devices, per_device(): part = lax.all_to_all(part, ('x', 'y'), 0, 0, tiled=True)  6.13 us
    pallas_call x1, Pallas kernels, last_part(): pl.pallas_call(last_kernel, out_shape=(jax.ShapeDtypeStruct((width, cols)...  5.97 us
  transfers between devices with their start and end apart: 22, of which 9 were waited for; matrix products, arithmetic and copies ran while one was open for 11% of the time, Pallas kernels for 17%

profile of v6, /device:TPU:8, one launch (start us, length us, event | category | flops | bytes accessed | tf_op | source)
XLA Modules:
  0.0 149.1 jit_solution(1641304624622707978)
XLA Ops:
  7.2 0.0 copy-start
  7.2 0.0 all-gather.2.cloned.1.call-start
  7.2 0.7 all-gather.2.cloned.1.call-update
  8.6 2.9 %collective-permute-start = (f32[1]{0:T(128)}, f32[1]{0:T(128)}, u32[]{:S(2)}, u32[]{:S(2)}) collective-permute-start(f32[1]{0:T(128)} %convert_element_type.27), channel_id=1, source_target_pairs={{0,64},{64,0},{128,192},{192,128},{1,65},{65,1},{129,193},{193,129... | collective-permute-start | bytes 20 | tf_op jit(solution)/shard_map/ppermute | solution.py:333
  11.4 2.8 %shard_map.112 = (bf16[512,256]{1,0:T(8,128)(2,1)}, bf16[512,256]{1,0:T(8,128)(2,1)}, f32[512,128]{1,0:T(8,128)}) custom-call(s32[1]{0:T(128)S(6)} %copy.12.count_ref, s32[2,512]{1,0:T(2,128)} %bitcast.54, f32[1,512]{1,0:T(1,128)} %bitcast.55, bf16[512,256]{1,0:T(8,128)(2,1)} %up_ref.1, bf16[512,256]{1,0:T(8,128)(2,1)} %pre_ref.1, f32[256,128]{1,0:T(8,128)} %basis_ref.3), custom_call_target="tpu_custom_call" | custom-call | flops 100000 | bytes 10000 | tf_op jit(solution)/shard_map/pallas_call | solution.py:76
  14.9 0.0 copy-start.8
  14.9 3.0 %convolution_convert_fusion = bf16[256,4096]{1,0:T(8,128)(2,1)} fusion(bf16[4096,256]{1,0:T(8,128)(2,1)S(1)} %copy-done, bf16[2,256,256]{2,1,0:T(8,128)(2,1)} %bitcast.52, s32[]{:T(128)S(6)} %select_n.54), kind=kOutput, calls=%fused_computation | convolution fusion | flops 537919488 | bytes 4325380 | tf_op jit(solution)/shard_map/dot_general | solution.py:26
  17.9 0.0 collective-permute-start.4
  17.9 0.6 collective-permute-start.3
  18.5 3.4 %collective-permute-start.1 = (f32[1]{0:T(128)}, f32[1]{0:T(128)}, u32[]{:S(2)}, u32[]{:S(2)}) collective-permute-start(f32[1]{0:T(128)} %add.82), channel_id=1, source_target_pairs={{0,192},{64,128},{128,64},{192,0},{1,193},{65,129},{129,65},{193,1... | collective-permute-start | bytes 20 | tf_op jit(solution)/shard_map/ppermute | solution.py:333
  21.9 11.7 %all-to-all-start = ((f32[32,16,128]{2,1,0:T(8,128)}), f32[32,16,128]{2,1,0:T(8,128)S(1)}, u32[]{:S(2)}, u32[]{:S(2)}) async-start(f32[32,16,128]{2,1,0:T(8,128)} %bitcast.3), calls=%async_computation | async-start | bytes 524288 | tf_op jit(solution)/shard_map/all_to_all | solution.py:370
  33.6 3.7 %shard_map.113 = (f32[2048,128]{1,0:T(8,128)}, f32[2048,128]{1,0:T(8,128)}) custom-call(s32[1]{0:T(128)} %bitcast.core_ref, bf16[4096,256]{1,0:T(8,128)(2,1)} %error_ref.2, f32[256,128]{1,0:T(8,128)} %basis_ref.3), custom_call_target="tpu_custom_call" | custom-call | flops 100000 | bytes 10000 | tf_op jit(solution)/shard_map/pallas_call | solution.py:106
  37.3 0.0 collective-permute-start.2
  37.9 0.0 collective-permute-done.3
  38.0 0.0 collective-permute-done.4
  38.0 2.3 %add_convert_fusion = bf16[256,4096]{1,0:T(8,128)(2,1)S(1)} fusion(bf16[256,4096]{1,0:T(8,128)(2,1)} %collective-permute-done.4, bf16[4096,256]{1,0:T(8,128)(2,1)S(1)} %copy-done, bf16[2,256,256]{2,1,0:T(8,128)(2,1)S(1)} %bitcast.53, s32[]{:T(128)S(6)} %select_n.53), kind=kOutput, calls=%fused_computation.1 | convolution fusion | flops 540016640 | bytes 6422532 | tf_op jit(solution)/shard_map/dot_general | solution.py:26
  40.3 0.0 copy-start.4
  40.4 1.3 copy-done.4
  41.7 0.8 dynamic-slice_bitcast_fusion.4
  42.5 2.6 %all-to-all-done = f32[32,16,128]{2,1,0:T(8,128)S(1)} async-done(((f32[32,16,128]{2,1,0:T(8,128)}), f32[32,16,128]{2,1,0:T(8,128)S(1)}, u32[]{:S(2)}, u32[]{:S(2)}) %all-to-all-start) | async-done | bytes 262176 | tf_op jit(solution)/shard_map/all_to_all | solution.py:370
  45.1 0.0 collective-permute-done.2.got_ref
  45.1 0.1 collective-permute-start.5
  45.2 2.1 %collective-permute-start.7 = (bf16[32,4096]{1,0:T(8,128)(2,1)}, bf16[32,4096]{1,0:T(8,128)(2,1)S(1)}, u32[]{:S(2)}, u32[]{:S(2)}) collective-permute-start(bf16[32,4096]{1,0:T(8,128)(2,1)} %get-tuple-element.55), channel_id=1, source_target_pairs={{0,6},{2,0},{4,2},{6,4},{1,7},{3,1},{5,3},{7,5},{8,14},{10,8},{12,... | collective-permute-start | bytes 786440 | tf_op jit(solution)/shard_map/ppermute | solution.py:338
  47.3 0.0 collective-permute-start.6
  47.4 0.0 collective-permute-done.5.other_ref
  47.4 2.7 %shard_map.114 = f32[2048,128]{1,0:T(8,128)} custom-call(f32[1]{0:T(128)S(6)} %div.3.inv_ref, f32[16,128]{1,0:T(8,128)S(1)} %reduce_sum.18.share_ref, f32[16,128]{1,0:T(8,128)S(1)} %collective-permute-done.5.other_ref, bf16[16,2048]{1,0:T(8,128)(2,1)S(1)} %maximum_select_fusion.feat_ref, f32[2048,128]{1,0:T(8,128)S(1)} %copy-done.1, ...), custom_call_target="tpu_custom_call" | custom-call | flops 100000000 | bytes 4000000 | tf_op jit(solution)/shard_map/pallas_call | solution.py:137
  50.1 6.1 %all-to-all-start.1 = ((f32[16,128,128]{2,1,0:T(8,128)}), f32[16,128,128]{2,1,0:T(8,128)S(1)}, u32[]{:S(2)}, u32[]{:S(2)}) async-start(f32[16,128,128]{2,1,0:T(8,128)} %bitcast.15), calls=%async_computation.1 | async-start | bytes 2097152 | tf_op jit(solution)/shard_map/all_to_all | solution.py:387
  56.2 1.1 dynamic-slice_bitcast_fusion.1
  57.3 0.0 collective-permute-done.7
  57.3 0.0 collective-permute-done.6
  57.3 1.2 fusion.2
  58.6 1.1 pad_maximum_fusion
  59.6 13.1 %all-to-all-done.1 = f32[16,128,128]{2,1,0:T(8,128)S(1)} async-done(((f32[16,128,128]{2,1,0:T(8,128)}), f32[16,128,128]{2,1,0:T(8,128)S(1)}, u32[]{:S(2)}, u32[]{:S(2)}) %all-to-all-start.1) | async-done | bytes 1048608 | tf_op jit(solution)/shard_map/all_to_all | solution.py:387
  72.7 0.1 collective-permute-start.8
  72.8 2.0 %collective-permute-start.9 = (bf16[64,4096]{1,0:T(8,128)(2,1)}, bf16[64,4096]{1,0:T(8,128)(2,1)}, u32[]{:S(2)}, u32[]{:S(2)}) collective-permute-start(bf16[64,4096]{1,0:T(8,128)(2,1)} %get-tuple-element.58), channel_id=1, source_target_pairs={{0,6},{2,0},{4,2},{6,4},{1,7},{3,1},{5,3},{7,5},{8,14},{10,8},{12,... | collective-permute-start | bytes 1572872 | tf_op jit(solution)/shard_map/ppermute | solution.py:338
  74.8 0.1 reduce_sum.19
  74.8 0.9 collective-permute-start.10
  75.7 4.7 %collective-permute-done.10 = f32[128,128]{1,0:T(8,128)S(1)} collective-permute-done((f32[128,128]{1,0:T(8,128)S(1)}, f32[128,128]{1,0:T(8,128)S(1)}, u32[]{:S(2)}, u32[]{:S(2)}) %collective-permute-start.10) | collective-permute-done | bytes 65568 | tf_op jit(solution)/shard_map/ppermute | solution.py:333
  80.5 1.2 collective-permute-start.11
  81.7 5.4 %collective-permute-done.11 = f32[128,128]{1,0:T(8,128)S(1)} collective-permute-done((f32[128,128]{1,0:T(8,128)S(1)}, f32[128,128]{1,0:T(8,128)S(1)}, u32[]{:S(2)}, u32[]{:S(2)}) %collective-permute-start.11) | collective-permute-done | bytes 65568 | tf_op jit(solution)/shard_map/ppermute | solution.py:333
  87.0 0.3 collective-permute-start.12
  87.3 5.5 %collective-permute-done.12 = f32[128,128]{1,0:T(8,128)S(1)} collective-permute-done((f32[128,128]{1,0:T(8,128)S(1)}, f32[128,128]{1,0:T(8,128)S(1)}, u32[]{:S(2)}, u32[]{:S(2)}) %collective-permute-start.12) | collective-permute-done | bytes 65568 | tf_op jit(solution)/shard_map/ppermute | solution.py:333
  92.8 0.0 collective-permute-done.8
  92.8 0.0 collective-permute-done.9
  92.8 1.1 broadcast_in_dim.14
  93.9 6.4 %all-to-all-start.2 = ((f32[16,128,128]{2,1,0:T(8,128)}), f32[16,128,128]{2,1,0:T(8,128)S(1)}, u32[]{:S(2)}, u32[]{:S(2)}) async-start(f32[16,128,128]{2,1,0:T(8,128)} %broadcast_in_dim.14), calls=%async_computation.2 | async-start | bytes 2097152 | tf_op jit(solution)/shard_map/all_to_all | solution.py:396
  100.3 2.3 %fusion.1 = bf16[64,4096]{1,0:T(8,128)(2,1)} fusion(bf16[64,4096]{1,0:T(8,128)(2,1)} %collective-permute-done.9, bf16[64,4096]{1,0:T(8,128)(2,1)} %collective-permute-done.8, bf16[4,64,4096]{2,1,0:T(8,128)(2,1)} %bitcast.50, s32[]{:T(128)S(6)} %select_n.57), kind=kLoop, calls=%fused_computation.4 | loop fusion | flops 1572864 | bytes 2097156 | tf_op jit(solution)/shard_map/convert_element_type | solution.py:401
  102.7 6.4 %shard_map.115 = (f32[4096,256]{1,0:T(8,128)}, bf16[256,4096]{1,0:T(8,128)(2,1)}, bf16[256,4096]{1,0:T(8,128)(2,1)}) custom-call(f32[1]{0:T(128)S(6)} %div.3.inv_ref, bf16[512,4096]{1,0:T(8,128)(2,1)} %all-gather.2.cloned.1.call-done.feat_ref, bf16[512,256]{1,0:T(8,128)(2,1)} %get-tuple-element.62.dpre_ref, bf16[4096,256]{1,0:T(8,128)(2,1)} %error_ref.2), custom_call_target="tpu_custom_call" | custom-call | flops 2000000000 | bytes 16000000 | tf_op jit(solution)/shard_map/pallas_call | solution.py:168
  109.1 3.6 %all-to-all-done.2 = f32[16,128,128]{2,1,0:T(8,128)S(1)} async-done(((f32[16,128,128]{2,1,0:T(8,128)}), f32[16,128,128]{2,1,0:T(8,128)S(1)}, u32[]{:S(2)}, u32[]{:S(2)}) %all-to-all-start.2) | async-done | bytes 1048608 | tf_op jit(solution)/shard_map/all_to_all | solution.py:396
  112.7 0.0 collective-permute-start.13
  112.7 4.6 %all-to-all-start.3 = ((bf16[8,8,4096]{2,1,0:T(8,128)(2,1)}), bf16[8,8,4096]{2,1,0:T(8,128)(2,1)}, u32[]{:S(2)}, u32[]{:S(2)}) async-start(bf16[8,8,4096]{2,1,0:T(8,128)(2,1)} %bitcast.51), calls=%async_computation.3 | async-start | bytes 1048576 | tf_op jit(solution)/shard_map/all_to_all | solution.py:405
  117.3 0.0 collective-permute-done.13.other_ref
  117.3 4.3 %shard_map.116 = f32[256,128]{1,0:T(8,128)} custom-call(s32[1]{0:T(128)} %bitcast.core_ref, bf16[256,4096]{1,0:T(8,128)(2,1)} %get-tuple-element.66.head_ref, bf16[256,4096]{1,0:T(8,128)(2,1)} %get-tuple-element.67.rest_ref, f32[2048,128]{1,0:T(8,128)} %bitcast.44, f32[2048,128]{1,0:T(8,128)} %collective-permute-done.13.other_ref), custom_call_target="tpu_custom_call" | custom-call | flops 1000000000 | bytes 6000000 | tf_op jit(solution)/shard_map/pallas_call | solution.py:213
  121.6 0.0 collective-permute-start.15
  121.6 3.4 %fusion.13 = f32[128,128]{1,0:T(8,128)S(1)} fusion(f32[2048,128]{1,0:T(8,128)} %bitcast.45), kind=kOutput, calls=%fused_computation.25 | convolution fusion | flops 402653184 | bytes 1114112 | tf_op jit(solution)/shard_map/dot_general | solution.py:409
  125.0 0.3 collective-permute-start.14
  125.3 1.0 collective-permute-done.14
  126.4 1.1 collective-permute-done.15
  127.5 1.5 collective-permute-start.16
  128.9 5.0 %shard_map.117.inverse_ref = f32[128,128]{1,0:T(8,128)S(1)} custom-call(f32[128,128]{1,0:T(8,128)S(1)} %add.106.gram_ref), custom_call_target="tpu_custom_call" | custom-call | flops 10000000 | bytes 100000 | tf_op jit(solution)/shard_map/pallas_call | solution.py:256
  134.0 0.6 copy-done.2
  134.6 1.0 all-to-all-done.3
  135.6 0.7 copy-done.9
  136.3 6.0 %shard_map.118 = (bf16[4096,256]{1,0:T(8,128)(2,1)}, f32[256,128]{1,0:T(8,128)}, bf16[8,4096]{1,0:T(8,128)(2,1)}) custom-call(s32[1]{0:T(128)} %bitcast.core_ref, f32[4096,256]{1,0:T(8,128)} %get-tuple-element.65.merged_ref, f32[2048,128]{1,0:T(8,128)} %bitcast.46, f32[2048,128]{1,0:T(8,128)} %collective-permute-done.13.other_ref, f32[256,128]{1,0:T(8,128)} %copy-done.5, ...), custom_call_target="tpu_custom_call" | custom-call | flops 1000000000 | bytes 8000000 | tf_op jit(solution)/shard_map/pallas_call | solution.py:296
  (26 shorter events, 0.2 us)
Async XLA Ops:
  7.2 7.7 %copy-start = (bf16[4096,256]{1,0:T(8,128)(2,1)S(1)}, bf16[4096,256]{1,0:T(8,128)(2,1)}, u32[]{:S(2)}) copy-start(bf16[4096,256]{1,0:T(8,128)(2,1)} %param.12) | copy-start | bytes 6291460
  7.2 95.5 %all-gather.2.cloned.1.call-start = ((), (), s32[]{:S(2)}) async-start(), calls=%async_computation.4 | async-start | bytes 4259840 | tf_op jit(solution)/shard_map/all_gather | solution.py:354
  8.6 5.7 %collective-permute-start = (f32[1]{0:T(128)}, f32[1]{0:T(128)}, u32[]{:S(2)}, u32[]{:S(2)}) collective-permute-start(f32[1]{0:T(128)} %convert_element_type.27), channel_id=1, source_target_pairs={{0,64},{64,0},{128,192},{192,128},{1,65},{65,1},{129,193},{193,129... | collective-permute-start | bytes 20 | tf_op jit(solution)/shard_map/ppermute | solution.py:333
  14.9 3.0 %copy-start.8 = (bf16[8,4096]{1,0:T(8,128)(2,1)S(1)}, bf16[8,4096]{1,0:T(8,128)(2,1)}, u32[]{:S(2)}) copy-start(bf16[8,4096]{1,0:T(8,128)(2,1)} %param.9) | copy-start | bytes 196612
  17.9 20.1 %copy-start.7 = (bf16[512,256]{1,0:T(8,128)(2,1)S(1)}, bf16[512,256]{1,0:T(8,128)(2,1)}, u32[]{:S(2)}) copy-start(bf16[512,256]{1,0:T(8,128)(2,1)} %get-tuple-element.46) | copy-start | bytes 786436
  17.9 20.1 %collective-permute-start.4 = (bf16[256,4096]{1,0:T(8,128)(2,1)}, bf16[256,4096]{1,0:T(8,128)(2,1)}, u32[]{:S(2)}, u32[]{:S(2)}) collective-permute-start(bf16[256,4096]{1,0:T(8,128)(2,1)} %convolution_convert_fusion), channel_id=1, source_target_pairs={{0,1},{1,0},{2,3},{3,2},{4,5},{5,4},{6,7},{7,6},{8,9},{9,8},{10,11... | collective-permute-start | bytes 6291464 | tf_op jit(solution)/shard_map/ppermute | solution.py:333
  17.9 20.0 %collective-permute-start.3 = (bf16[8,2048]{1,0:T(8,128)(2,1)S(1)}, bf16[8,2048]{1,0:T(8,128)(2,1)S(1)}, u32[]{:S(2)}, u32[]{:S(2)}) collective-permute-start(bf16[8,2048]{1,0:T(8,128)(2,1)S(1)} %get-tuple-element.84), channel_id=1, source_target_pairs={{0,1},{1,0},{2,3},{3,2},{4,5},{5,4},{6,7},{7,6},{8,9},{9,8},{10,11... | collective-permute-start | bytes 98312 | tf_op jit(solution)/shard_map/ppermute | solution.py:333
  18.5 18.8 %collective-permute-start.1 = (f32[1]{0:T(128)}, f32[1]{0:T(128)}, u32[]{:S(2)}, u32[]{:S(2)}) collective-permute-start(f32[1]{0:T(128)} %add.82), channel_id=1, source_target_pairs={{0,192},{64,128},{128,64},{192,0},{1,193},{65,129},{129,65},{193,1... | collective-permute-start | bytes 20 | tf_op jit(solution)/shard_map/ppermute | solution.py:333
  21.9 23.2 %all-to-all-start = ((f32[32,16,128]{2,1,0:T(8,128)}), f32[32,16,128]{2,1,0:T(8,128)S(1)}, u32[]{:S(2)}, u32[]{:S(2)}) async-start(f32[32,16,128]{2,1,0:T(8,128)} %bitcast.3), calls=%async_computation | async-start | bytes 524288 | tf_op jit(solution)/shard_map/all_to_all | solution.py:370
  37.3 7.8 %collective-permute-start.2 = (f32[2048,128]{1,0:T(8,128)}, f32[2048,128]{1,0:T(8,128)}, u32[]{:S(2)}, u32[]{:S(2)}) collective-permute-start(f32[2048,128]{1,0:T(8,128)} %get-tuple-element.45), channel_id=1, source_target_pairs={{0,1},{1,0},{2,3},{3,2},{4,5},{5,4},{6,7},{7,6},{8,9},{9,8},{10,11... | collective-permute-start | bytes 3145736 | tf_op jit(solution)/shard_map/ppermute | solution.py:333
  40.3 1.3 copy-start.4
  40.3 7.0 %copy-start.1 = (f32[2048,128]{1,0:T(8,128)S(1)}, f32[2048,128]{1,0:T(8,128)}, u32[]{:S(2)}) copy-start(f32[2048,128]{1,0:T(8,128)} %get-tuple-element.51.keep_ref) | copy-start | bytes 3145732
  45.1 2.3 %collective-permute-start.5 = (f32[16,128]{1,0:T(8,128)S(1)}, f32[16,128]{1,0:T(8,128)S(1)}, u32[]{:S(2)}, u32[]{:S(2)}) collective-permute-start(f32[16,128]{1,0:T(8,128)S(1)} %reduce_sum.18.share_ref), channel_id=1, source_target_pairs={{0,1},{1,0},{2,3},{3,2},{4,5},{5,4},{6,7},{7,6},{8,9},{9,8},{10,11... | collective-permute-start | bytes 24584 | tf_op jit(solution)/shard_map/ppermute | solution.py:333
  45.2 12.1 %collective-permute-start.7 = (bf16[32,4096]{1,0:T(8,128)(2,1)}, bf16[32,4096]{1,0:T(8,128)(2,1)S(1)}, u32[]{:S(2)}, u32[]{:S(2)}) collective-permute-start(bf16[32,4096]{1,0:T(8,128)(2,1)} %get-tuple-element.55), channel_id=1, source_target_pairs={{0,6},{2,0},{4,2},{6,4},{1,7},{3,1},{5,3},{7,5},{8,14},{10,8},{12,... | collective-permute-start | bytes 786440 | tf_op jit(solution)/shard_map/ppermute | solution.py:338
  47.3 10.0 %collective-permute-start.6 = (bf16[32,4096]{1,0:T(8,128)(2,1)}, bf16[32,4096]{1,0:T(8,128)(2,1)}, u32[]{:S(2)}, u32[]{:S(2)}) collective-permute-start(bf16[32,4096]{1,0:T(8,128)(2,1)} %get-tuple-element.54), channel_id=1, source_target_pairs={{0,2},{2,4},{4,6},{6,0},{1,3},{3,5},{5,7},{7,1},{8,10},{10,12},{12... | collective-permute-start | bytes 786440 | tf_op jit(solution)/shard_map/ppermute | solution.py:338
  50.1 22.6 %all-to-all-start.1 = ((f32[16,128,128]{2,1,0:T(8,128)}), f32[16,128,128]{2,1,0:T(8,128)S(1)}, u32[]{:S(2)}, u32[]{:S(2)}) async-start(f32[16,128,128]{2,1,0:T(8,128)} %bitcast.15), calls=%async_computation.1 | async-start | bytes 2097152 | tf_op jit(solution)/shard_map/all_to_all | solution.py:387
  72.7 20.1 %collective-permute-start.8 = (bf16[64,4096]{1,0:T(8,128)(2,1)}, bf16[64,4096]{1,0:T(8,128)(2,1)}, u32[]{:S(2)}, u32[]{:S(2)}) collective-permute-start(bf16[64,4096]{1,0:T(8,128)(2,1)} %get-tuple-element.57), channel_id=1, source_target_pairs={{0,2},{2,4},{4,6},{6,0},{1,3},{3,5},{5,7},{7,1},{8,10},{10,12},{12... | collective-permute-start | bytes 1572872 | tf_op jit(solution)/shard_map/ppermute | solution.py:338
  72.8 20.0 %collective-permute-start.9 = (bf16[64,4096]{1,0:T(8,128)(2,1)}, bf16[64,4096]{1,0:T(8,128)(2,1)}, u32[]{:S(2)}, u32[]{:S(2)}) collective-permute-start(bf16[64,4096]{1,0:T(8,128)(2,1)} %get-tuple-element.58), channel_id=1, source_target_pairs={{0,6},{2,0},{4,2},{6,4},{1,7},{3,1},{5,3},{7,5},{8,14},{10,8},{12,... | collective-permute-start | bytes 1572872 | tf_op jit(solution)/shard_map/ppermute | solution.py:338
  74.8 5.6 %collective-permute-start.10 = (f32[128,128]{1,0:T(8,128)S(1)}, f32[128,128]{1,0:T(8,128)S(1)}, u32[]{:S(2)}, u32[]{:S(2)}) collective-permute-start(f32[128,128]{1,0:T(8,128)S(1)} %reduce_sum.19), channel_id=1, source_target_pairs={{0,8},{8,0},{16,24},{24,16},{32,40},{40,32},{48,56},{56,48},{1,9},... | collective-permute-start | bytes 196616 | tf_op jit(solution)/shard_map/ppermute | solution.py:333
  80.5 6.6 %collective-permute-start.11 = (f32[128,128]{1,0:T(8,128)S(1)}, f32[128,128]{1,0:T(8,128)S(1)}, u32[]{:S(2)}, u32[]{:S(2)}) collective-permute-start(f32[128,128]{1,0:T(8,128)S(1)} %add.101), channel_id=1, source_target_pairs={{0,16},{8,24},{16,0},{24,8},{32,48},{40,56},{48,32},{56,40},{1,17}... | collective-permute-start | bytes 196616 | tf_op jit(solution)/shard_map/ppermute | solution.py:333
  87.0 5.7 %collective-permute-start.12 = (f32[128,128]{1,0:T(8,128)S(1)}, f32[128,128]{1,0:T(8,128)S(1)}, u32[]{:S(2)}, u32[]{:S(2)}) collective-permute-start(f32[128,128]{1,0:T(8,128)S(1)} %add.102), channel_id=1, source_target_pairs={{0,56},{8,48},{16,40},{24,32},{32,24},{40,16},{48,8},{56,0},{1,57}... | collective-permute-start | bytes 196616 | tf_op jit(solution)/shard_map/ppermute | solution.py:333
  93.9 18.8 %all-to-all-start.2 = ((f32[16,128,128]{2,1,0:T(8,128)}), f32[16,128,128]{2,1,0:T(8,128)S(1)}, u32[]{:S(2)}, u32[]{:S(2)}) async-start(f32[16,128,128]{2,1,0:T(8,128)} %broadcast_in_dim.14), calls=%async_computation.2 | async-start | bytes 2097152 | tf_op jit(solution)/shard_map/all_to_all | solution.py:396
  112.7 4.6 %copy-start.3 = (f32[16,128,128]{2,1,0:T(8,128)}, f32[16,128,128]{2,1,0:T(8,128)S(1)}, u32[]{:S(2)}) copy-start(f32[16,128,128]{2,1,0:T(8,128)S(1)} %all-to-all-done.2) | copy-start | bytes 3145732
  112.7 4.6 %collective-permute-start.13 = (f32[2048,128]{1,0:T(8,128)S(1)}, f32[2048,128]{1,0:T(8,128)}, u32[]{:S(2)}, u32[]{:S(2)}) collective-permute-start(f32[2048,128]{1,0:T(8,128)S(1)} %bitcast.43), channel_id=1, source_target_pairs={{0,1},{1,0},{2,3},{3,2},{4,5},{5,4},{6,7},{7,6},{8,9},{9,8},{10,11... | collective-permute-start | bytes 3145736 | tf_op jit(solution)/shard_map/ppermute | solution.py:333
  112.7 22.9 %all-to-all-start.3 = ((bf16[8,8,4096]{2,1,0:T(8,128)(2,1)}), bf16[8,8,4096]{2,1,0:T(8,128)(2,1)}, u32[]{:S(2)}, u32[]{:S(2)}) async-start(bf16[8,8,4096]{2,1,0:T(8,128)(2,1)} %bitcast.51), calls=%async_computation.3 | async-start | bytes 1048576 | tf_op jit(solution)/shard_map/all_to_all | solution.py:405
  121.6 5.8 %copy-start.6 = (f32[256,128]{1,0:T(8,128)S(1)}, f32[256,128]{1,0:T(8,128)}, u32[]{:S(2)}) copy-start(f32[256,128]{1,0:T(8,128)} %shard_map.116) | copy-start | bytes 393220
  121.6 5.8 %collective-permute-start.15 = (f32[256,128]{1,0:T(8,128)}, f32[256,128]{1,0:T(8,128)S(1)}, u32[]{:S(2)}, u32[]{:S(2)}) collective-permute-start(f32[256,128]{1,0:T(8,128)} %shard_map.116), channel_id=1, source_target_pairs={{0,64},{64,0},{128,192},{192,128},{1,65},{65,1},{129,193},{193,129... | collective-permute-start | bytes 393224 | tf_op jit(solution)/shard_map/ppermute | solution.py:333
  125.0 1.3 collective-permute-start.14
  127.5 8.1 %copy-start.5 = (f32[256,128]{1,0:T(8,128)}, f32[256,128]{1,0:T(8,128)S(1)}, u32[]{:S(2)}) copy-start(f32[256,128]{1,0:T(8,128)S(1)} %add.107.right_ref) | copy-start | bytes 393220
  127.5 8.1 %collective-permute-start.16 = (f32[256,128]{1,0:T(8,128)S(1)}, f32[256,128]{1,0:T(8,128)S(1)}, u32[]{:S(2)}, u32[]{:S(2)}) collective-permute-start(f32[256,128]{1,0:T(8,128)S(1)} %add.107.right_ref), channel_id=1, source_target_pairs={{0,192},{64,128},{128,64},{192,0},{1,193},{65,129},{129,65},{193,1... | collective-permute-start | bytes 393224 | tf_op jit(solution)/shard_map/ppermute | solution.py:333
  134.0 0.6 copy-start.2
  135.6 0.7 copy-start.9
Sparse Core Ops, SparseCore 0:
  10.8 84.7 all-gather.1

commit v7 on v6

--- a/solution.py
+++ b/solution.py
@@ -265,7 +265,9 @@
 
 def last_kernel(core_ref, merged_ref, own_ref, other_ref, right_ref, got_ref, inverse_ref, grad_ref, error_ref, basis_ref, sum_ref, back_ref):
     def fill(left):
-        out = mm_split(split(left), (back_ref[0], back_ref[1]), ((1,), (1,)))
+        lh, ll = split(left)
+        head = jnp.concatenate([back_ref[0], back_ref[0]], axis=1)
+        out = mm(jnp.concatenate([lh, ll], axis=1), head, ((1,), (1,))) + mm(lh, back_ref[1], ((1,), (1,)))
         error_ref[...] = (merged_ref[...] - out).astype(BF16)
 
     @pl.when(pl.program_id(0) == 0)

time: 152 us -> 151 us (level)
  no operation moved by 1% of the time
where the time goes in v7:
time: 151 us; the launch traced here: 149 us
  starting transfers between devices  44.2 us (29%)
  waiting for transfers between devices  38.7 us (26%)
  Pallas kernels  30.4 us (20%)
  between operations  16.1 us (11%)
  matrix products  8.75 us (6%)
  local copies, waits for them, and re-layouts  5.57 us (4%)
  other arithmetic  4.81 us (3%)
    ppermute x13, waiting for transfers between devices, swap(): return lax.ppermute(value, axis, [(i, i ^ bit) for i in range(n)])  17.7 us
    all_to_all x1, waiting for transfers between devices, per_device(): part = lax.all_to_all(part, ('x', 'y'), 0, 0, tiled=True)  13.1 us
    all_to_all x1, starting transfers between devices, per_device(): lax.all_to_all(share, ('z', 'y'), 0, 0, tiled=True)  11.7 us
    ppermute x13, starting transfers between devices, swap(): return lax.ppermute(value, axis, [(i, i ^ bit) for i in range(n)])  11.1 us
    all_to_all x1, starting transfers between devices, per_device(): lax.all_to_all(jnp.broadcast_to(part[None], (n_inter * n_y,) + part.shape...  6.45 us
    pallas_call x1, Pallas kernels, merge_part(): pl.pallas_call(merge_kernel, out_shape=(jax.ShapeDtypeStruct((width, cols...  6.38 us
    all_to_all x1, starting transfers between devices, per_device(): part = lax.all_to_all(part, ('x', 'y'), 0, 0, tiled=True)  6.13 us
    pallas_call x1, Pallas kernels, last_part(): pl.pallas_call(last_kernel, out_shape=(jax.ShapeDtypeStruct((width, cols)...  5.41 us
  transfers between devices with their start and end apart: 22, of which 9 were waited for; matrix products, arithmetic and copies ran while one was open for 11% of the time, Pallas kernels for 17%

profile of v7, /device:TPU:8, one launch (start us, length us, event | category | flops | bytes accessed | tf_op | source)
XLA Modules:
  0.0 148.5 jit_solution(16896850153140533517)
XLA Ops:
  7.2 0.0 copy-start
  7.2 0.0 all-gather.2.cloned.1.call-start
  7.2 0.7 all-gather.2.cloned.1.call-update
  8.6 2.9 %collective-permute-start = (f32[1]{0:T(128)}, f32[1]{0:T(128)}, u32[]{:S(2)}, u32[]{:S(2)}) collective-permute-start(f32[1]{0:T(128)} %convert_element_type.27), channel_id=1, source_target_pairs={{0,64},{64,0},{128,192},{192,128},{1,65},{65,1},{129,193},{193,129... | collective-permute-start | bytes 20 | tf_op jit(solution)/shard_map/ppermute | solution.py:335
  11.4 2.8 %shard_map.112 = (bf16[512,256]{1,0:T(8,128)(2,1)}, bf16[512,256]{1,0:T(8,128)(2,1)}, f32[512,128]{1,0:T(8,128)}) custom-call(s32[1]{0:T(128)S(6)} %copy.12.count_ref, s32[2,512]{1,0:T(2,128)} %bitcast.54, f32[1,512]{1,0:T(1,128)} %bitcast.55, bf16[512,256]{1,0:T(8,128)(2,1)} %up_ref.1, bf16[512,256]{1,0:T(8,128)(2,1)} %pre_ref.1, f32[256,128]{1,0:T(8,128)} %basis_ref.3), custom_call_target="tpu_custom_call" | custom-call | flops 100000 | bytes 10000 | tf_op jit(solution)/shard_map/pallas_call | solution.py:76
  14.9 0.0 copy-start.8
  14.9 3.0 %convolution_convert_fusion = bf16[256,4096]{1,0:T(8,128)(2,1)} fusion(bf16[4096,256]{1,0:T(8,128)(2,1)S(1)} %copy-done, bf16[2,256,256]{2,1,0:T(8,128)(2,1)} %bitcast.52, s32[]{:T(128)S(6)} %select_n.54), kind=kOutput, calls=%fused_computation | convolution fusion | flops 537919488 | bytes 4325380 | tf_op jit(solution)/shard_map/dot_general | solution.py:26
  17.9 0.0 collective-permute-start.4
  17.9 0.6 collective-permute-start.3
  18.5 3.4 %collective-permute-start.1 = (f32[1]{0:T(128)}, f32[1]{0:T(128)}, u32[]{:S(2)}, u32[]{:S(2)}) collective-permute-start(f32[1]{0:T(128)} %add.82), channel_id=1, source_target_pairs={{0,192},{64,128},{128,64},{192,0},{1,193},{65,129},{129,65},{193,1... | collective-permute-start | bytes 20 | tf_op jit(solution)/shard_map/ppermute | solution.py:335
  21.9 11.7 %all-to-all-start = ((f32[32,16,128]{2,1,0:T(8,128)}), f32[32,16,128]{2,1,0:T(8,128)S(1)}, u32[]{:S(2)}, u32[]{:S(2)}) async-start(f32[32,16,128]{2,1,0:T(8,128)} %bitcast.3), calls=%async_computation | async-start | bytes 524288 | tf_op jit(solution)/shard_map/all_to_all | solution.py:372
  33.6 3.7 %shard_map.113 = (f32[2048,128]{1,0:T(8,128)}, f32[2048,128]{1,0:T(8,128)}) custom-call(s32[1]{0:T(128)} %bitcast.core_ref, bf16[4096,256]{1,0:T(8,128)(2,1)} %error_ref.2, f32[256,128]{1,0:T(8,128)} %basis_ref.3), custom_call_target="tpu_custom_call" | custom-call | flops 100000 | bytes 10000 | tf_op jit(solution)/shard_map/pallas_call | solution.py:106
  37.3 0.0 collective-permute-start.2
  37.9 0.0 collective-permute-done.3
  38.0 0.0 collective-permute-done.4
  38.0 2.3 %add_convert_fusion = bf16[256,4096]{1,0:T(8,128)(2,1)S(1)} fusion(bf16[256,4096]{1,0:T(8,128)(2,1)} %collective-permute-done.4, bf16[4096,256]{1,0:T(8,128)(2,1)S(1)} %copy-done, bf16[2,256,256]{2,1,0:T(8,128)(2,1)S(1)} %bitcast.53, s32[]{:T(128)S(6)} %select_n.53), kind=kOutput, calls=%fused_computation.1 | convolution fusion | flops 540016640 | bytes 6422532 | tf_op jit(solution)/shard_map/dot_general | solution.py:26
  40.3 0.0 copy-start.4
  40.4 1.3 copy-done.4
  41.7 0.8 dynamic-slice_bitcast_fusion.4
  42.5 2.6 %all-to-all-done = f32[32,16,128]{2,1,0:T(8,128)S(1)} async-done(((f32[32,16,128]{2,1,0:T(8,128)}), f32[32,16,128]{2,1,0:T(8,128)S(1)}, u32[]{:S(2)}, u32[]{:S(2)}) %all-to-all-start) | async-done | bytes 262176 | tf_op jit(solution)/shard_map/all_to_all | solution.py:372
  45.1 0.0 collective-permute-done.2.got_ref
  45.1 0.1 collective-permute-start.5
  45.2 2.1 %collective-permute-start.7 = (bf16[32,4096]{1,0:T(8,128)(2,1)}, bf16[32,4096]{1,0:T(8,128)(2,1)S(1)}, u32[]{:S(2)}, u32[]{:S(2)}) collective-permute-start(bf16[32,4096]{1,0:T(8,128)(2,1)} %get-tuple-element.55), channel_id=1, source_target_pairs={{0,6},{2,0},{4,2},{6,4},{1,7},{3,1},{5,3},{7,5},{8,14},{10,8},{12,... | collective-permute-start | bytes 786440 | tf_op jit(solution)/shard_map/ppermute | solution.py:340
  47.3 0.0 collective-permute-start.6
  47.4 0.0 collective-permute-done.5.other_ref
  47.4 2.7 %shard_map.114 = f32[2048,128]{1,0:T(8,128)} custom-call(f32[1]{0:T(128)S(6)} %div.3.inv_ref, f32[16,128]{1,0:T(8,128)S(1)} %reduce_sum.18.share_ref, f32[16,128]{1,0:T(8,128)S(1)} %collective-permute-done.5.other_ref, bf16[16,2048]{1,0:T(8,128)(2,1)S(1)} %maximum_select_fusion.feat_ref, f32[2048,128]{1,0:T(8,128)S(1)} %copy-done.1, ...), custom_call_target="tpu_custom_call" | custom-call | flops 100000000 | bytes 4000000 | tf_op jit(solution)/shard_map/pallas_call | solution.py:137
  50.1 6.1 %all-to-all-start.1 = ((f32[16,128,128]{2,1,0:T(8,128)}), f32[16,128,128]{2,1,0:T(8,128)S(1)}, u32[]{:S(2)}, u32[]{:S(2)}) async-start(f32[16,128,128]{2,1,0:T(8,128)} %bitcast.15), calls=%async_computation.1 | async-start | bytes 2097152 | tf_op jit(solution)/shard_map/all_to_all | solution.py:389
  56.2 1.1 dynamic-slice_bitcast_fusion.1
  57.3 0.0 collective-permute-done.7
  57.3 0.0 collective-permute-done.6
  57.3 1.2 fusion.2
  58.6 1.1 pad_maximum_fusion
  59.6 13.1 %all-to-all-done.1 = f32[16,128,128]{2,1,0:T(8,128)S(1)} async-done(((f32[16,128,128]{2,1,0:T(8,128)}), f32[16,128,128]{2,1,0:T(8,128)S(1)}, u32[]{:S(2)}, u32[]{:S(2)}) %all-to-all-start.1) | async-done | bytes 1048608 | tf_op jit(solution)/shard_map/all_to_all | solution.py:389
  72.7 0.1 collective-permute-start.8
  72.8 2.0 %collective-permute-start.9 = (bf16[64,4096]{1,0:T(8,128)(2,1)}, bf16[64,4096]{1,0:T(8,128)(2,1)}, u32[]{:S(2)}, u32[]{:S(2)}) collective-permute-start(bf16[64,4096]{1,0:T(8,128)(2,1)} %get-tuple-element.58), channel_id=1, source_target_pairs={{0,6},{2,0},{4,2},{6,4},{1,7},{3,1},{5,3},{7,5},{8,14},{10,8},{12,... | collective-permute-start | bytes 1572872 | tf_op jit(solution)/shard_map/ppermute | solution.py:340
  74.8 0.1 reduce_sum.19
  74.8 0.9 collective-permute-start.10
  75.7 4.7 %collective-permute-done.10 = f32[128,128]{1,0:T(8,128)S(1)} collective-permute-done((f32[128,128]{1,0:T(8,128)S(1)}, f32[128,128]{1,0:T(8,128)S(1)}, u32[]{:S(2)}, u32[]{:S(2)}) %collective-permute-start.10) | collective-permute-done | bytes 65568 | tf_op jit(solution)/shard_map/ppermute | solution.py:335
  80.5 1.2 collective-permute-start.11
  81.7 5.4 %collective-permute-done.11 = f32[128,128]{1,0:T(8,128)S(1)} collective-permute-done((f32[128,128]{1,0:T(8,128)S(1)}, f32[128,128]{1,0:T(8,128)S(1)}, u32[]{:S(2)}, u32[]{:S(2)}) %collective-permute-start.11) | collective-permute-done | bytes 65568 | tf_op jit(solution)/shard_map/ppermute | solution.py:335
  87.0 0.3 collective-permute-start.12
  87.3 5.5 %collective-permute-done.12 = f32[128,128]{1,0:T(8,128)S(1)} collective-permute-done((f32[128,128]{1,0:T(8,128)S(1)}, f32[128,128]{1,0:T(8,128)S(1)}, u32[]{:S(2)}, u32[]{:S(2)}) %collective-permute-start.12) | collective-permute-done | bytes 65568 | tf_op jit(solution)/shard_map/ppermute | solution.py:335
  92.8 0.0 collective-permute-done.8
  92.8 0.0 collective-permute-done.9
  92.8 1.1 broadcast_in_dim.14
  93.9 6.4 %all-to-all-start.2 = ((f32[16,128,128]{2,1,0:T(8,128)}), f32[16,128,128]{2,1,0:T(8,128)S(1)}, u32[]{:S(2)}, u32[]{:S(2)}) async-start(f32[16,128,128]{2,1,0:T(8,128)} %broadcast_in_dim.14), calls=%async_computation.2 | async-start | bytes 2097152 | tf_op jit(solution)/shard_map/all_to_all | solution.py:398
  100.3 2.3 %fusion.1 = bf16[64,4096]{1,0:T(8,128)(2,1)} fusion(bf16[64,4096]{1,0:T(8,128)(2,1)} %collective-permute-done.9, bf16[64,4096]{1,0:T(8,128)(2,1)} %collective-permute-done.8, bf16[4,64,4096]{2,1,0:T(8,128)(2,1)} %bitcast.50, s32[]{:T(128)S(6)} %select_n.57), kind=kLoop, calls=%fused_computation.4 | loop fusion | flops 1572864 | bytes 2097156 | tf_op jit(solution)/shard_map/convert_element_type | solution.py:403
  102.7 6.4 %shard_map.115 = (f32[4096,256]{1,0:T(8,128)}, bf16[256,4096]{1,0:T(8,128)(2,1)}, bf16[256,4096]{1,0:T(8,128)(2,1)}) custom-call(f32[1]{0:T(128)S(6)} %div.3.inv_ref, bf16[512,4096]{1,0:T(8,128)(2,1)} %all-gather.2.cloned.1.call-done.feat_ref, bf16[512,256]{1,0:T(8,128)(2,1)} %get-tuple-element.62.dpre_ref, bf16[4096,256]{1,0:T(8,128)(2,1)} %error_ref.2), custom_call_target="tpu_custom_call" | custom-call | flops 2000000000 | bytes 16000000 | tf_op jit(solution)/shard_map/pallas_call | solution.py:168
  109.1 3.6 %all-to-all-done.2 = f32[16,128,128]{2,1,0:T(8,128)S(1)} async-done(((f32[16,128,128]{2,1,0:T(8,128)}), f32[16,128,128]{2,1,0:T(8,128)S(1)}, u32[]{:S(2)}, u32[]{:S(2)}) %all-to-all-start.2) | async-done | bytes 1048608 | tf_op jit(solution)/shard_map/all_to_all | solution.py:398
  112.7 0.0 collective-permute-start.13
  112.7 4.6 %all-to-all-start.3 = ((bf16[8,8,4096]{2,1,0:T(8,128)(2,1)}), bf16[8,8,4096]{2,1,0:T(8,128)(2,1)}, u32[]{:S(2)}, u32[]{:S(2)}) async-start(bf16[8,8,4096]{2,1,0:T(8,128)(2,1)} %bitcast.51), calls=%async_computation.3 | async-start | bytes 1048576 | tf_op jit(solution)/shard_map/all_to_all | solution.py:407
  117.3 0.0 collective-permute-done.13.other_ref
  117.3 4.3 %shard_map.116 = f32[256,128]{1,0:T(8,128)} custom-call(s32[1]{0:T(128)} %bitcast.core_ref, bf16[256,4096]{1,0:T(8,128)(2,1)} %get-tuple-element.66.head_ref, bf16[256,4096]{1,0:T(8,128)(2,1)} %get-tuple-element.67.rest_ref, f32[2048,128]{1,0:T(8,128)} %bitcast.44, f32[2048,128]{1,0:T(8,128)} %collective-permute-done.13.other_ref), custom_call_target="tpu_custom_call" | custom-call | flops 1000000000 | bytes 6000000 | tf_op jit(solution)/shard_map/pallas_call | solution.py:213
  121.6 0.0 collective-permute-start.15
  121.6 3.4 %fusion.13 = f32[128,128]{1,0:T(8,128)S(1)} fusion(f32[2048,128]{1,0:T(8,128)} %bitcast.45), kind=kOutput, calls=%fused_computation.25 | convolution fusion | flops 402653184 | bytes 1114112 | tf_op jit(solution)/shard_map/dot_general | solution.py:411
  125.0 0.3 collective-permute-start.14
  125.3 1.0 collective-permute-done.14
  126.4 1.1 collective-permute-done.15
  127.5 1.5 collective-permute-start.16
  128.9 5.0 %shard_map.117.inverse_ref = f32[128,128]{1,0:T(8,128)S(1)} custom-call(f32[128,128]{1,0:T(8,128)S(1)} %add.106.gram_ref), custom_call_target="tpu_custom_call" | custom-call | flops 10000000 | bytes 100000 | tf_op jit(solution)/shard_map/pallas_call | solution.py:256
  134.0 0.6 copy-done.2
  134.6 1.0 all-to-all-done.3
  135.6 0.7 copy-done.9
  136.3 5.4 %shard_map.118 = (bf16[4096,256]{1,0:T(8,128)(2,1)}, f32[256,128]{1,0:T(8,128)}, bf16[8,4096]{1,0:T(8,128)(2,1)}) custom-call(s32[1]{0:T(128)} %bitcast.core_ref, f32[4096,256]{1,0:T(8,128)} %get-tuple-element.65.merged_ref, f32[2048,128]{1,0:T(8,128)} %bitcast.46, f32[2048,128]{1,0:T(8,128)} %collective-permute-done.13.other_ref, f32[256,128]{1,0:T(8,128)} %copy-done.5, ...), custom_call_target="tpu_custom_call" | custom-call | flops 1000000000 | bytes 8000000 | tf_op jit(solution)/shard_map/pallas_call | solution.py:298
  (26 shorter events, 0.2 us)
Async XLA Ops:
  7.2 7.7 %copy-start = (bf16[4096,256]{1,0:T(8,128)(2,1)S(1)}, bf16[4096,256]{1,0:T(8,128)(2,1)}, u32[]{:S(2)}) copy-start(bf16[4096,256]{1,0:T(8,128)(2,1)} %param.12) | copy-start | bytes 6291460
  7.2 95.5 %all-gather.2.cloned.1.call-start = ((), (), s32[]{:S(2)}) async-start(), calls=%async_computation.4 | async-start | bytes 4259840 | tf_op jit(solution)/shard_map/all_gather | solution.py:356
  8.6 5.7 %collective-permute-start = (f32[1]{0:T(128)}, f32[1]{0:T(128)}, u32[]{:S(2)}, u32[]{:S(2)}) collective-permute-start(f32[1]{0:T(128)} %convert_element_type.27), channel_id=1, source_target_pairs={{0,64},{64,0},{128,192},{192,128},{1,65},{65,1},{129,193},{193,129... | collective-permute-start | bytes 20 | tf_op jit(solution)/shard_map/ppermute | solution.py:335
  14.9 3.0 %copy-start.8 = (bf16[8,4096]{1,0:T(8,128)(2,1)S(1)}, bf16[8,4096]{1,0:T(8,128)(2,1)}, u32[]{:S(2)}) copy-start(bf16[8,4096]{1,0:T(8,128)(2,1)} %param.9) | copy-start | bytes 196612
  17.9 20.1 %copy-start.7 = (bf16[512,256]{1,0:T(8,128)(2,1)S(1)}, bf16[512,256]{1,0:T(8,128)(2,1)}, u32[]{:S(2)}) copy-start(bf16[512,256]{1,0:T(8,128)(2,1)} %get-tuple-element.46) | copy-start | bytes 786436
  17.9 20.1 %collective-permute-start.4 = (bf16[256,4096]{1,0:T(8,128)(2,1)}, bf16[256,4096]{1,0:T(8,128)(2,1)}, u32[]{:S(2)}, u32[]{:S(2)}) collective-permute-start(bf16[256,4096]{1,0:T(8,128)(2,1)} %convolution_convert_fusion), channel_id=1, source_target_pairs={{0,1},{1,0},{2,3},{3,2},{4,5},{5,4},{6,7},{7,6},{8,9},{9,8},{10,11... | collective-permute-start | bytes 6291464 | tf_op jit(solution)/shard_map/ppermute | solution.py:335
  17.9 20.0 %collective-permute-start.3 = (bf16[8,2048]{1,0:T(8,128)(2,1)S(1)}, bf16[8,2048]{1,0:T(8,128)(2,1)S(1)}, u32[]{:S(2)}, u32[]{:S(2)}) collective-permute-start(bf16[8,2048]{1,0:T(8,128)(2,1)S(1)} %get-tuple-element.84), channel_id=1, source_target_pairs={{0,1},{1,0},{2,3},{3,2},{4,5},{5,4},{6,7},{7,6},{8,9},{9,8},{10,11... | collective-permute-start | bytes 98312 | tf_op jit(solution)/shard_map/ppermute | solution.py:335
  18.5 18.8 %collective-permute-start.1 = (f32[1]{0:T(128)}, f32[1]{0:T(128)}, u32[]{:S(2)}, u32[]{:S(2)}) collective-permute-start(f32[1]{0:T(128)} %add.82), channel_id=1, source_target_pairs={{0,192},{64,128},{128,64},{192,0},{1,193},{65,129},{129,65},{193,1... | collective-permute-start | bytes 20 | tf_op jit(solution)/shard_map/ppermute | solution.py:335
  21.9 23.2 %all-to-all-start = ((f32[32,16,128]{2,1,0:T(8,128)}), f32[32,16,128]{2,1,0:T(8,128)S(1)}, u32[]{:S(2)}, u32[]{:S(2)}) async-start(f32[32,16,128]{2,1,0:T(8,128)} %bitcast.3), calls=%async_computation | async-start | bytes 524288 | tf_op jit(solution)/shard_map/all_to_all | solution.py:372
  37.3 7.8 %collective-permute-start.2 = (f32[2048,128]{1,0:T(8,128)}, f32[2048,128]{1,0:T(8,128)}, u32[]{:S(2)}, u32[]{:S(2)}) collective-permute-start(f32[2048,128]{1,0:T(8,128)} %get-tuple-element.45), channel_id=1, source_target_pairs={{0,1},{1,0},{2,3},{3,2},{4,5},{5,4},{6,7},{7,6},{8,9},{9,8},{10,11... | collective-permute-start | bytes 3145736 | tf_op jit(solution)/shard_map/ppermute | solution.py:335
  40.3 1.3 copy-start.4
  40.3 7.0 %copy-start.1 = (f32[2048,128]{1,0:T(8,128)S(1)}, f32[2048,128]{1,0:T(8,128)}, u32[]{:S(2)}) copy-start(f32[2048,128]{1,0:T(8,128)} %get-tuple-element.51.keep_ref) | copy-start | bytes 3145732
  45.1 2.3 %collective-permute-start.5 = (f32[16,128]{1,0:T(8,128)S(1)}, f32[16,128]{1,0:T(8,128)S(1)}, u32[]{:S(2)}, u32[]{:S(2)}) collective-permute-start(f32[16,128]{1,0:T(8,128)S(1)} %reduce_sum.18.share_ref), channel_id=1, source_target_pairs={{0,1},{1,0},{2,3},{3,2},{4,5},{5,4},{6,7},{7,6},{8,9},{9,8},{10,11... | collective-permute-start | bytes 24584 | tf_op jit(solution)/shard_map/ppermute | solution.py:335
  45.2 12.1 %collective-permute-start.7 = (bf16[32,4096]{1,0:T(8,128)(2,1)}, bf16[32,4096]{1,0:T(8,128)(2,1)S(1)}, u32[]{:S(2)}, u32[]{:S(2)}) collective-permute-start(bf16[32,4096]{1,0:T(8,128)(2,1)} %get-tuple-element.55), channel_id=1, source_target_pairs={{0,6},{2,0},{4,2},{6,4},{1,7},{3,1},{5,3},{7,5},{8,14},{10,8},{12,... | collective-permute-start | bytes 786440 | tf_op jit(solution)/shard_map/ppermute | solution.py:340
  47.3 10.0 %collective-permute-start.6 = (bf16[32,4096]{1,0:T(8,128)(2,1)}, bf16[32,4096]{1,0:T(8,128)(2,1)}, u32[]{:S(2)}, u32[]{:S(2)}) collective-permute-start(bf16[32,4096]{1,0:T(8,128)(2,1)} %get-tuple-element.54), channel_id=1, source_target_pairs={{0,2},{2,4},{4,6},{6,0},{1,3},{3,5},{5,7},{7,1},{8,10},{10,12},{12... | collective-permute-start | bytes 786440 | tf_op jit(solution)/shard_map/ppermute | solution.py:340
  50.1 22.6 %all-to-all-start.1 = ((f32[16,128,128]{2,1,0:T(8,128)}), f32[16,128,128]{2,1,0:T(8,128)S(1)}, u32[]{:S(2)}, u32[]{:S(2)}) async-start(f32[16,128,128]{2,1,0:T(8,128)} %bitcast.15), calls=%async_computation.1 | async-start | bytes 2097152 | tf_op jit(solution)/shard_map/all_to_all | solution.py:389
  72.7 20.1 %collective-permute-start.8 = (bf16[64,4096]{1,0:T(8,128)(2,1)}, bf16[64,4096]{1,0:T(8,128)(2,1)}, u32[]{:S(2)}, u32[]{:S(2)}) collective-permute-start(bf16[64,4096]{1,0:T(8,128)(2,1)} %get-tuple-element.57), channel_id=1, source_target_pairs={{0,2},{2,4},{4,6},{6,0},{1,3},{3,5},{5,7},{7,1},{8,10},{10,12},{12... | collective-permute-start | bytes 1572872 | tf_op jit(solution)/shard_map/ppermute | solution.py:340
  72.8 20.0 %collective-permute-start.9 = (bf16[64,4096]{1,0:T(8,128)(2,1)}, bf16[64,4096]{1,0:T(8,128)(2,1)}, u32[]{:S(2)}, u32[]{:S(2)}) collective-permute-start(bf16[64,4096]{1,0:T(8,128)(2,1)} %get-tuple-element.58), channel_id=1, source_target_pairs={{0,6},{2,0},{4,2},{6,4},{1,7},{3,1},{5,3},{7,5},{8,14},{10,8},{12,... | collective-permute-start | bytes 1572872 | tf_op jit(solution)/shard_map/ppermute | solution.py:340
  74.8 5.6 %collective-permute-start.10 = (f32[128,128]{1,0:T(8,128)S(1)}, f32[128,128]{1,0:T(8,128)S(1)}, u32[]{:S(2)}, u32[]{:S(2)}) collective-permute-start(f32[128,128]{1,0:T(8,128)S(1)} %reduce_sum.19), channel_id=1, source_target_pairs={{0,8},{8,0},{16,24},{24,16},{32,40},{40,32},{48,56},{56,48},{1,9},... | collective-permute-start | bytes 196616 | tf_op jit(solution)/shard_map/ppermute | solution.py:335
  80.5 6.6 %collective-permute-start.11 = (f32[128,128]{1,0:T(8,128)S(1)}, f32[128,128]{1,0:T(8,128)S(1)}, u32[]{:S(2)}, u32[]{:S(2)}) collective-permute-start(f32[128,128]{1,0:T(8,128)S(1)} %add.101), channel_id=1, source_target_pairs={{0,16},{8,24},{16,0},{24,8},{32,48},{40,56},{48,32},{56,40},{1,17}... | collective-permute-start | bytes 196616 | tf_op jit(solution)/shard_map/ppermute | solution.py:335
  87.0 5.7 %collective-permute-start.12 = (f32[128,128]{1,0:T(8,128)S(1)}, f32[128,128]{1,0:T(8,128)S(1)}, u32[]{:S(2)}, u32[]{:S(2)}) collective-permute-start(f32[128,128]{1,0:T(8,128)S(1)} %add.102), channel_id=1, source_target_pairs={{0,56},{8,48},{16,40},{24,32},{32,24},{40,16},{48,8},{56,0},{1,57}... | collective-permute-start | bytes 196616 | tf_op jit(solution)/shard_map/ppermute | solution.py:335
  93.9 18.8 %all-to-all-start.2 = ((f32[16,128,128]{2,1,0:T(8,128)}), f32[16,128,128]{2,1,0:T(8,128)S(1)}, u32[]{:S(2)}, u32[]{:S(2)}) async-start(f32[16,128,128]{2,1,0:T(8,128)} %broadcast_in_dim.14), calls=%async_computation.2 | async-start | bytes 2097152 | tf_op jit(solution)/shard_map/all_to_all | solution.py:398
  112.7 4.6 %copy-start.3 = (f32[16,128,128]{2,1,0:T(8,128)}, f32[16,128,128]{2,1,0:T(8,128)S(1)}, u32[]{:S(2)}) copy-start(f32[16,128,128]{2,1,0:T(8,128)S(1)} %all-to-all-done.2) | copy-start | bytes 3145732
  112.7 4.6 %collective-permute-start.13 = (f32[2048,128]{1,0:T(8,128)S(1)}, f32[2048,128]{1,0:T(8,128)}, u32[]{:S(2)}, u32[]{:S(2)}) collective-permute-start(f32[2048,128]{1,0:T(8,128)S(1)} %bitcast.43), channel_id=1, source_target_pairs={{0,1},{1,0},{2,3},{3,2},{4,5},{5,4},{6,7},{7,6},{8,9},{9,8},{10,11... | collective-permute-start | bytes 3145736 | tf_op jit(solution)/shard_map/ppermute | solution.py:335
  112.7 22.9 %all-to-all-start.3 = ((bf16[8,8,4096]{2,1,0:T(8,128)(2,1)}), bf16[8,8,4096]{2,1,0:T(8,128)(2,1)}, u32[]{:S(2)}, u32[]{:S(2)}) async-start(bf16[8,8,4096]{2,1,0:T(8,128)(2,1)} %bitcast.51), calls=%async_computation.3 | async-start | bytes 1048576 | tf_op jit(solution)/shard_map/all_to_all | solution.py:407
  121.6 5.8 %copy-start.6 = (f32[256,128]{1,0:T(8,128)S(1)}, f32[256,128]{1,0:T(8,128)}, u32[]{:S(2)}) copy-start(f32[256,128]{1,0:T(8,128)} %shard_map.116) | copy-start | bytes 393220
  121.6 5.8 %collective-permute-start.15 = (f32[256,128]{1,0:T(8,128)}, f32[256,128]{1,0:T(8,128)S(1)}, u32[]{:S(2)}, u32[]{:S(2)}) collective-permute-start(f32[256,128]{1,0:T(8,128)} %shard_map.116), channel_id=1, source_target_pairs={{0,64},{64,0},{128,192},{192,128},{1,65},{65,1},{129,193},{193,129... | collective-permute-start | bytes 393224 | tf_op jit(solution)/shard_map/ppermute | solution.py:335
  125.0 1.3 collective-permute-start.14
  127.5 8.1 %copy-start.5 = (f32[256,128]{1,0:T(8,128)}, f32[256,128]{1,0:T(8,128)S(1)}, u32[]{:S(2)}) copy-start(f32[256,128]{1,0:T(8,128)S(1)} %add.107.right_ref) | copy-start | bytes 393220
  127.5 8.1 %collective-permute-start.16 = (f32[256,128]{1,0:T(8,128)S(1)}, f32[256,128]{1,0:T(8,128)S(1)}, u32[]{:S(2)}, u32[]{:S(2)}) collective-permute-start(f32[256,128]{1,0:T(8,128)S(1)} %add.107.right_ref), channel_id=1, source_target_pairs={{0,192},{64,128},{128,64},{192,0},{1,193},{65,129},{129,65},{193,1... | collective-permute-start | bytes 393224 | tf_op jit(solution)/shard_map/ppermute | solution.py:335
  134.0 0.6 copy-start.2
  135.6 0.7 copy-start.9
Sparse Core Ops, SparseCore 0:
  10.8 84.7 all-gather.1
